TPU v7x, 32 devices: a whole 2x2x4 slice. The times are simulated.
32 devices in a mesh: kz: 4 (over z), en: 8 (over y, x, core).
Axes of the slice: x: 2, y: 2, z: 4, core: 2. Of those that a mesh axis runs over, the one named last changes fastest.
Arguments:
- green_lesser: bfloat16 [4, 16, 2, 512, 512], P('kz', 'en'), may hold values from -6 to 6
- coupling: float32 [3, 4, 2, 128, 128], replicated, may hold values from -0.25 to 0.25
- block_list: int32 [3, 4, 2], replicated, may hold values from 0 to 3, as said below
- offsets: int32 [3], replicated, may hold values from -1 to 1, as said below
- shifts: int32 [3], replicated, may hold values from 1 to 2, as said below
- occupation: float32 [3], replicated, may hold values from 0.25 to 4
Outputs:
- sigma_lesser: float32 [4, 16, 2, 512, 512], P('kz', 'en')
Inputs may be any that keep to these rules, and one draw needn't show every extreme that they name: `block_list`: for each transfer, the 4 listed blocks hold every block row once and every block column once. -1 and +1 each occur among the offsets. 1 and 2 each occur among the shifts.
All inputs are finite; a program needn't handle non-finite values.
Results may differ from a plain program's by a relative error of at most 0.0057.
Values may be sent and summed in bfloat16 or wider, within the bound.
No kernel may reach another device: no remote copies, remote signals or barrier semaphores. Data moves between devices by JAX's collectives and lax.ppermute only.
A program may use at most 128 MiB of HBM per device.

v0:
```python
import jax
import jax.numpy as jnp
from jax import lax
from jax.sharding import PartitionSpec as P

NQ = 3
SMAX = 2


def padded(block, sides, width, periodic):
    for axis, dim in sides:
        count = lax.axis_size(axis)
        forward = [(i, i + 1) for i in range(count - 1)]
        if periodic:
            forward.append((count - 1, 0))
        backward = [(target, source) for source, target in forward]
        low = lax.ppermute(
            lax.slice_in_dim(block, block.shape[dim] - width, None, axis=dim), axis, forward
        )
        high = lax.ppermute(lax.slice_in_dim(block, 0, width, axis=dim), axis, backward)
        block = jnp.concatenate([low, block, high], axis=dim)
    return block


def sandwich(field, blocks, row_index, column_index):
    batch_count = field.shape[0]
    orbitals = field.shape[-1]
    block_size = blocks.shape[-1]
    block_count = orbitals // block_size
    real_part = blocks[:, 0]
    imag_part = blocks[:, 1]
    numbers = jnp.arange(block_count, dtype=jnp.int32)
    matches = (row_index[:, None] == numbers[None, :]).astype(jnp.int32)
    inverse = jnp.sum(numbers[:, None] * matches, axis=0)
    row_blocks = field.reshape(batch_count, 2, block_count, block_size, orbitals)
    picked = jnp.take(row_blocks, column_index, axis=2)

    def product_left(matrix, other):
        return jnp.einsum("nxy,lnyo->lnxo", matrix, other, preferred_element_type=jnp.float32)

    left_real = product_left(real_part, picked[:, 0]) - product_left(imag_part, picked[:, 1])
    left_imag = product_left(real_part, picked[:, 1]) + product_left(imag_part, picked[:, 0])
    products = jnp.stack([left_real.astype(jnp.bfloat16), left_imag.astype(jnp.bfloat16)], axis=1)
    left_half = jnp.take(products, inverse, axis=2)
    column_blocks = left_half.reshape(batch_count, 2, orbitals, block_count, block_size)
    chosen = jnp.take(column_blocks, column_index, axis=3)

    def product_right(other, matrix):
        return jnp.einsum("lony,nxy->lonx", other, matrix, preferred_element_type=jnp.float32)

    right_real = product_right(chosen[:, 0], real_part) + product_right(chosen[:, 1], imag_part)
    right_imag = product_right(chosen[:, 1], real_part) - product_right(chosen[:, 0], imag_part)
    stacked = jnp.stack([right_real, right_imag], axis=1)
    result = jnp.take(stacked, inverse, axis=3)
    return result.reshape(batch_count, 2, orbitals, orbitals)


def on_device(green_lesser, coupling, block_list, offsets, shifts, occupation):
    coupling_rounded = coupling.astype(jnp.bfloat16)
    momenta_here = green_lesser.shape[0]
    energies_here = green_lesser.shape[1]
    orbitals = green_lesser.shape[-1]
    widened = padded(green_lesser, (("kz", 0),), 1, True)
    widened = padded(widened, (("en", 1),), SMAX, False)
    sigma_sum = jnp.zeros(green_lesser.shape, jnp.float32)
    for transfer in range(NQ):
        start_momentum = 1 - offsets[transfer]
        source_rows = lax.dynamic_slice_in_dim(widened, start_momentum, momenta_here, 0)
        absorbed = lax.dynamic_slice_in_dim(source_rows, SMAX - shifts[transfer], energies_here, 1)
        emitted = lax.dynamic_slice_in_dim(source_rows, SMAX + shifts[transfer], energies_here, 1)
        weight = occupation[transfer]
        combined = (
            weight * absorbed.astype(jnp.float32) + (weight + 1.0) * emitted.astype(jnp.float32)
        ).astype(jnp.bfloat16)
        flattened = combined.reshape(momenta_here * energies_here, 2, orbitals, orbitals)
        term = sandwich(
            flattened,
            coupling_rounded[transfer],
            block_list[transfer, :, 0],
            block_list[transfer, :, 1],
        )
        sigma_sum = sigma_sum + term.reshape(green_lesser.shape)
    return sigma_sum


def solution(mesh):
    placed = (P("kz", "en", None, None, None), P(), P(), P(), P(), P())
    return jax.shard_map(
        on_device,
        mesh=mesh,
        in_specs=placed,
        out_specs=P("kz", "en", None, None, None),
        check_vma=False,
    )
```

profile of v0, /device:TPU:3, one launch (start us, length us, event | category | flops | bytes accessed | tf_op | source)
XLA Modules:
  0.0 405.8 jit_solution(933361782759799999)
XLA Ops:
  1.3 2.1 collective-permute-start.1
  3.4 45.5 %collective-permute-done = bf16[1,2,2,512,512]{4,3,2,1,0:T(8,128)(2,1)S(1)} collective-permute-done((bf16[1,2,2,512,512]{4,3,2,1,0:T(8,128)(2,1)}, bf16[1,2,2,512,512]{4,3,2,1,0:T(8,128)(2,1)S(1)}, u32[]{:S(2)}, u32[]{:S(2)}) %collective-permute-start) | collective-permute-done | bytes 2097184 | tf_op jit(solution)/shard_map/ppermute | solution.py:17
  51.8 41.5 %collective-permute-done.1 = bf16[1,2,2,512,512]{4,3,2,1,0:T(8,128)(2,1)S(1)} collective-permute-done((bf16[1,2,2,512,512]{4,3,2,1,0:T(8,128)(2,1)}, bf16[1,2,2,512,512]{4,3,2,1,0:T(8,128)(2,1)S(1)}, u32[]{:S(2)}, u32[]{:S(2)}) %collective-permute-start.1) | collective-permute-done | bytes 2097184 | tf_op jit(solution)/shard_map/ppermute | solution.py:20
  94.8 3.1 collective-permute-start.3
  97.9 3.4 collective-permute-start.2
  116.6 116.5 %collective-permute-done.3 = bf16[3,2,2,512,512]{4,3,2,1,0:T(8,128)(2,1)} collective-permute-done((bf16[3,2,2,512,512]{4,3,2,1,0:T(8,128)(2,1)}, bf16[3,2,2,512,512]{4,3,2,1,0:T(8,128)(2,1)}, u32[]{:S(2)}, u32[]{:S(2)}) %collective-permute-start.3) | collective-permute-done | bytes 6291488 | tf_op jit(solution)/shard_map/ppermute | solution.py:20
  233.7 9.6 %pad_maximum_fusion = bf16[3,6,2,512,512]{4,3,2,1,0:T(8,128)(2,1)S(1)} fusion(bf16[3,2,2,512,512]{4,3,2,1,0:T(8,128)(2,1)} %collective-permute-done.3, bf16[3,2,2,512,512]{4,3,2,1,0:T(8,128)(2,1)} %constant_dynamic-update-slice_fusion, bf16[3,2,2,512,512]{4,3,2,1,0:T(8,128)(2,1)} %collective-permute-done.2), kind=kLoop, calls=%fused_computation.12 | loop fusion | flops 18874368 | bytes 37748736 | tf_op jit(solution)/shard_map/concatenate | solution.py:21
  243.3 5.8 %add_convert_fusion.2 = (bf16[1,2,2,512,512]{4,3,2,1,0:T(8,128)(2,1)}, bf16[1,2,2,512,512]{4,3,2,1,0:T(8,128)(2,1)S(1)}, bf16[1,2,2,512,512]{4,3,2,1,0:T(8,128)(2,1)}) fusion(bf16[3,6,2,512,512]{4,3,2,1,0:T(8,128)(2,1)S(1)} %pad_maximum_fusion, s32[]{:T(128)S(6)} %select_n.65, s32[]{:T(128)S(6)} %select_n.69, f32[]{:T(128)S(6)} %add.195, s32[]{:T(128)S(6)} %select_n.67, ...), kind=kLoop, calls=%fused_computation.20 | loop fusion | flops 18874368 | bytes 18874428 | tf_op jit(solution)/shard_map/convert_element_type | solution.py:74
  249.1 2.0 gather_fusion.8
  251.1 3.0 copy.32
  256.3 2.2 gather_fusion.9
  260.3 2.4 copy.33
  262.7 4.0 reshape.99
  266.7 2.0 copy.34
  268.7 2.2 gather_fusion.10
  270.9 1.9 fusion
  276.2 3.6 gather_fusion.4
  279.9 4.1 %copy.28 = bf16[4,2,2,128,512]{3,4,1,0,2:T(8,128)(2,1)} copy(bf16[4,2,2,128,512]{4,3,2,1,0:T(8,128)(2,1)} %gather_fusion.4) | data formatting | bytes 4194304 | tf_op jit(solution)/shard_map/jit(_take)/gather | solution.py:36
  284.0 1.9 select_bitcast_fusion.3
  289.2 3.8 gather_fusion.5
  293.0 3.2 select_bitcast_fusion.2
  296.2 4.1 %copy.29 = bf16[2,2,4,128,512]{4,3,2,1,0:T(8,128)(2,1)} copy(bf16[2,2,4,128,512]{3,4,0,1,2:T(8,128)(2,1)} %select_bitcast_fusion.2) | data formatting | bytes 4194304 | tf_op jit(solution)/shard_map/jit(_take)/select_n | solution.py:44
  300.3 4.0 reshape.98
  304.3 3.4 copy.30
  307.7 3.8 gather_fusion.6
  313.3 2.0 fusion.16
  317.2 3.6 gather_fusion
  320.8 4.1 %copy.23 = bf16[4,2,2,128,512]{3,4,1,0,2:T(8,128)(2,1)} copy(bf16[4,2,2,128,512]{4,3,2,1,0:T(8,128)(2,1)} %gather_fusion) | data formatting | bytes 4194304 | tf_op jit(solution)/shard_map/jit(_take)/gather | solution.py:36
  324.9 1.9 select_bitcast_fusion.5
  330.0 3.7 gather_fusion.1
  333.7 3.2 select_bitcast_fusion.4
  336.9 4.1 %copy.25 = bf16[2,2,4,128,512]{4,3,2,1,0:T(8,128)(2,1)} copy(bf16[2,2,4,128,512]{3,4,0,1,2:T(8,128)(2,1)} %select_bitcast_fusion.4) | data formatting | bytes 4194304 | tf_op jit(solution)/shard_map/jit(_take)/select_n | solution.py:44
  341.0 4.0 reshape.97
  345.0 3.3 copy.26
  348.3 3.7 gather_fusion.2
  352.1 1.9 fusion.2
  353.9 2.0 fusion.12
  360.0 2.3 pad_maximum_fusion.3
  362.3 5.1 %gather_fusion.11 = f32[4,2,2,512,128]{4,3,1,2,0:T(8,128)} fusion(f32[2,2,512,4,128]{4,2,0,3,1:T(8,128)} %pad_maximum_fusion.3, s32[1024]{0:T(1024)S(1)} %pad_clamp_fusion), kind=kCustom, calls=%fused_computation.11.clone | custom fusion | bytes 8388624 | tf_op jit(solution)/shard_map/jit(_take)/gather | solution.py:54
  367.4 2.2 subtract_bitcast_fusion.1
  370.1 2.3 pad_maximum_fusion.2
  372.4 5.1 %gather_fusion.7 = f32[4,2,2,512,128]{4,3,1,2,0:T(8,128)} fusion(f32[2,2,512,4,128]{4,2,0,3,1:T(8,128)} %pad_maximum_fusion.2, s32[1024]{0:T(1024)S(1)} %pad_clamp_fusion.2), kind=kCustom, calls=%fused_computation.10.clone | custom fusion | bytes 8388624 | tf_op jit(solution)/shard_map/jit(_take)/gather | solution.py:54
  377.6 2.2 subtract_bitcast_fusion.2
  380.2 2.3 pad_maximum_fusion.1
  382.5 5.0 %gather_fusion.3 = f32[4,2,2,512,128]{4,3,1,2,0:T(8,128)} fusion(f32[2,2,512,4,128]{4,2,0,3,1:T(8,128)} %pad_maximum_fusion.1, s32[1024]{0:T(1024)S(1)} %pad_clamp_fusion.4), kind=kCustom, calls=%fused_computation.2.clone | custom fusion | bytes 8388624 | tf_op jit(solution)/shard_map/jit(_take)/gather | solution.py:54
  387.5 7.9 %bitcast_add_fusion = f32[2,2,512,4,128]{4,2,0,1,3:T(8,128)} fusion(f32[4,2,2,512,128]{4,3,1,2,0:T(8,128)} %gather_fusion.11, f32[4,2,2,512,128]{4,3,1,2,0:T(8,128)} %gather_fusion.7, f32[4,2,2,512,128]{4,3,1,2,0:T(8,128)} %gather_fusion.3, pred[4]{0:T(512)(128)(4,1)S(1)} %get-tuple-element.38, pred[4]{0:T(512)(128)(4,1)S(1)} %get-tuple-element.39, ...), kind=kLoop, calls=%fused_computation.16 | loop fusion | flops 5242880 | bytes 16777228 | tf_op jit(solution)/shard_map/add | solution.py:82
  395.4 5.3 %copy.36 = f32[2,2,512,4,128]{2,4,3,1,0:T(8,128)} copy(f32[2,2,512,4,128]{4,2,0,1,3:T(8,128)} %bitcast_add_fusion) | data formatting | bytes 8388608 | tf_op jit(solution)/shard_map/add | solution.py:82
  400.6 5.2 %copy.37 = f32[1,2,2,512,512]{4,3,2,1,0:T(8,128)} copy(f32[1,2,2,512,512]{3,4,2,1,0:T(8,128)} %bitcast.228) | data formatting | bytes 8388608 | tf_op jit(solution)/shard_map/add | solution.py:82
  (77 shorter events, 31.4 us)
Async XLA Ops:
  0.0 50.3 %copy-start.8 = (bf16[1,2,2,512,512]{4,3,2,1,0:T(8,128)(2,1)S(1)}, bf16[1,2,2,512,512]{4,3,2,1,0:T(8,128)(2,1)}, u32[]{:S(2)}) copy-start(bf16[1,2,2,512,512]{4,3,2,1,0:T(8,128)(2,1)} %param.12) | copy-start | bytes 6291460
  0.0 48.8 %collective-permute-start = (bf16[1,2,2,512,512]{4,3,2,1,0:T(8,128)(2,1)}, bf16[1,2,2,512,512]{4,3,2,1,0:T(8,128)(2,1)S(1)}, u32[]{:S(2)}, u32[]{:S(2)}) collective-permute-start(bf16[1,2,2,512,512]{4,3,2,1,0:T(8,128)(2,1)} %param.12), channel_id=1, source_target_pairs={{0,8},{8,16},{16,24},{24,0},{1,9},{9,17},{17,25},{25,1},{2,10},{10... | collective-permute-start | bytes 6291464 | tf_op jit(solution)/shard_map/ppermute | solution.py:17
  1.3 92.0 %collective-permute-start.1 = (bf16[1,2,2,512,512]{4,3,2,1,0:T(8,128)(2,1)}, bf16[1,2,2,512,512]{4,3,2,1,0:T(8,128)(2,1)S(1)}, u32[]{:S(2)}, u32[]{:S(2)}) collective-permute-start(bf16[1,2,2,512,512]{4,3,2,1,0:T(8,128)(2,1)} %param.12), channel_id=1, source_target_pairs={{8,0},{16,8},{24,16},{0,24},{9,1},{17,9},{25,17},{1,25},{10,2},{18... | collective-permute-start | bytes 6291464 | tf_op jit(solution)/shard_map/ppermute | solution.py:20
  51.7 49.5 %copy-start.10 = (s32[3]{0:T(128)S(1)}, s32[3]{0:T(128)}, u32[]{:S(2)}) copy-start(s32[3]{0:T(128)} %param.16) | copy-start | bytes 40
  51.7 52.7 %copy-start.11 = (s32[3]{0:T(128)S(1)}, s32[3]{0:T(128)}, u32[]{:S(2)}) copy-start(s32[3]{0:T(128)} %param.15) | copy-start | bytes 40
  51.8 61.8 %copy-start.12 = (f32[3]{0:T(128)S(1)}, f32[3]{0:T(128)}, u32[]{:S(2)}) copy-start(f32[3]{0:T(128)} %param.17) | copy-start | bytes 40
  51.8 64.3 %copy-start.13 = (s32[3,4,2]{1,2,0:T(2,128)S(1)}, s32[3,4,2]{1,2,0:T(2,128)}, u32[]{:S(2)}) copy-start(s32[3,4,2]{1,2,0:T(2,128)} %param.14) | copy-start | bytes 292
  51.8 64.7 %copy-start.9 = (f32[3,4,2,128,128]{4,3,2,1,0:T(8,128)S(1)}, f32[3,4,2,128,128]{4,3,2,1,0:T(8,128)}, u32[]{:S(2)}) copy-start(f32[3,4,2,128,128]{4,3,2,1,0:T(8,128)} %param.13) | copy-start | bytes 4718596
  94.8 138.4 %collective-permute-start.3 = (bf16[3,2,2,512,512]{4,3,2,1,0:T(8,128)(2,1)}, bf16[3,2,2,512,512]{4,3,2,1,0:T(8,128)(2,1)}, u32[]{:S(2)}, u32[]{:S(2)}) collective-permute-start(bf16[3,2,2,512,512]{4,3,2,1,0:T(8,128)(2,1)} %constant_dynamic-update-slice_fusion), channel_id=1, source_target_pairs={{1,0},{2,1},{3,2},{4,3},{5,4},{6,5},{7,6},{9,8},{10,9},{11,10},{12... | collective-permute-start | bytes 18874376 | tf_op jit(solution)/shard_map/ppermute | solution.py:20
  97.9 135.8 %collective-permute-start.2 = (bf16[3,2,2,512,512]{4,3,2,1,0:T(8,128)(2,1)}, bf16[3,2,2,512,512]{4,3,2,1,0:T(8,128)(2,1)}, u32[]{:S(2)}, u32[]{:S(2)}) collective-permute-start(bf16[3,2,2,512,512]{4,3,2,1,0:T(8,128)(2,1)} %constant_dynamic-update-slice_fusion), channel_id=1, source_target_pairs={{0,1},{1,2},{2,3},{3,4},{4,5},{5,6},{6,7},{8,9},{9,10},{10,11},{11... | collective-permute-start | bytes 18874376 | tf_op jit(solution)/shard_map/ppermute | solution.py:17
  313.3 3.8 copy-start
  353.9 3.8 copy-start.2
  356.0 2.0 copy-start.5
  358.0 1.6 copy-start.4
  362.3 5.1 %copy-start.1 = (bf16[2,2,512,4,128]{4,2,0,3,1:T(8,128)(2,1)S(1)}, bf16[2,2,512,4,128]{4,2,0,3,1:T(8,128)(2,1)}, u32[]{:S(2)}) copy-start(bf16[2,2,512,4,128]{4,2,0,3,1:T(8,128)(2,1)} %copy-done) | copy-start | bytes 6291460
  367.4 2.2 copy-start.6
  372.4 5.1 %copy-start.3 = (bf16[2,2,512,4,128]{4,2,0,3,1:T(8,128)(2,1)S(1)}, bf16[2,2,512,4,128]{4,2,0,3,1:T(8,128)(2,1)}, u32[]{:S(2)}) copy-start(bf16[2,2,512,4,128]{4,2,0,3,1:T(8,128)(2,1)} %copy-done.2) | copy-start | bytes 6291460
  377.6 2.2 copy-start.7
where the time goes:
time: 411 us; the launch traced here: 406 us
  waiting for transfers between devices  204 us (50%)
  local copies, waits for them, and re-layouts  105 us (26%)
  other arithmetic  51.5 us (13%)
  matrix products  22.5 us (5%)
  between operations  13.3 us (3%)
  starting transfers between devices  9.82 us (2%)
    ppermute x2, waiting for transfers between devices, padded(): lax.ppermute(lax.slice_in_dim(block, 0, width, axis=dim), axis, backward)  158 us
    ppermute x2, waiting for transfers between devices, padded(): lax.ppermute(lax.slice_in_dim(block, block.shape[dim] - width, None, axis...  46 us
    reshape x6, local copies, waits for them, and re-layouts, sandwich(): left_half.reshape(batch_count, 2, orbitals, block_count, block_size)  20.6 us
    gather x6, local copies, waits for them, and re-layouts, sandwich(): picked = jnp.take(row_blocks, column_index, axis=2)  20.5 us
    dot_general x12, matrix products, product_right(): jnp.einsum('lony,nxy->lonx', other, matrix, preferred_element_type=jnp.fl...  17.3 us
    gather x3, local copies, waits for them, and re-layouts, sandwich(): result = jnp.take(stacked, inverse, axis=3)  15.2 us
    select_n x3, local copies, waits for them, and re-layouts, sandwich(): left_half = jnp.take(products, inverse, axis=2)  10.7 us
    add x2, local copies, waits for them, and re-layouts, on_device(): sigma_sum = sigma_sum + term.reshape(green_lesser.shape)  10.5 us
  transfers between devices with their start and end apart: 4, of which 4 were waited for; matrix products, arithmetic and copies ran while one was open for 1% of the time, Pallas kernels for 0%

commit v1 on v0

v1 whole, which is shorter than its diff:
```python
import functools

import jax
import jax.numpy as jnp
from jax import lax
from jax.experimental import pallas as pl
from jax.experimental.pallas import tpu as pltpu
from jax.sharding import PartitionSpec as P

SMAX = 2
VMEM_LIMIT = 56 * 1024 * 1024


def ring(count, step, periodic):
    pairs = [(i, i + step) for i in range(count) if 0 <= i + step < count]
    if periodic:
        pairs += [(i, (i + step) % count) for i in range(count) if not 0 <= i + step < count]
    return pairs


def whole(count):
    return [pl.BlockSpec(memory_space=pltpu.VMEM)] * count


def scalars(count):
    return [pl.BlockSpec(memory_space=pltpu.SMEM)] * count


def factors_kernel(coupling_ref, left_ref, right_ref):
    block = coupling_ref.shape[-1]
    real = coupling_ref[0, 0, 0]
    imag = coupling_ref[0, 0, 1]
    real_t = real.T
    imag_t = imag.T
    low, high = pl.ds(0, block), pl.ds(block, block)

    def put(ref, rows, columns, value):
        ref[0, 0, rows, columns] = value.astype(jnp.bfloat16)

    put(left_ref, low, low, real)
    put(left_ref, low, high, -imag)
    put(left_ref, high, low, imag)
    put(left_ref, high, high, real)
    put(right_ref, low, low, real_t)
    put(right_ref, low, high, -imag_t)
    put(right_ref, high, low, imag_t)
    put(right_ref, high, high, real_t)


def factors(coupling):
    transfers, listed, _, block, _ = coupling.shape
    shape = jax.ShapeDtypeStruct((transfers, listed, 2 * block, 2 * block), jnp.bfloat16)
    out_spec = pl.BlockSpec((1, 1, 2 * block, 2 * block), lambda q, n: (q, n, 0, 0))
    return pl.pallas_call(
        factors_kernel,
        grid=(transfers, listed),
        in_specs=[pl.BlockSpec((1, 1, 2, block, block), lambda q, n: (q, n, 0, 0, 0))],
        out_specs=[out_spec, out_spec],
        out_shape=[shape, shape],
        name="factors",
    )(coupling)


def sandwich(left_ref, right_ref, q, lists_ref, mixed, half, total):
    listed, rows = left_ref.shape[1], left_ref.shape[2] // 2

    def entry(n, side):
        return lists_ref[(q * listed + n) * 2 + side]

    for n in range(listed):
        product = jnp.dot(left_ref[q, n], mixed[entry(n, 1)], preferred_element_type=jnp.float32)
        product = product.astype(jnp.bfloat16)
        target = pl.ds(pl.multiple_of(entry(n, 0) * rows, rows), rows)
        for column in range(listed):
            for part in range(2):
                half[column, target, pl.ds(part * rows, rows)] = product[
                    part * rows : (part + 1) * rows, column * rows : (column + 1) * rows
                ]
    for n in range(listed):
        total[entry(n, 0)] += jnp.dot(half[entry(n, 1)], right_ref[q, n], preferred_element_type=jnp.float32)


def accumulate(energy, groups, scalar_refs, left_ref, right_ref, mixed, half, total):
    lists_ref, offsets_ref, shifts_ref, occupation_ref = scalar_refs
    total[...] = jnp.zeros_like(total)

    @pl.loop(0, left_ref.shape[0])
    def _(q):
        weight = occupation_ref[q]
        listed, rows = left_ref.shape[1], left_ref.shape[2] // 2
        for offset, levels in groups:
            for shift in range(1, SMAX + 1):
                first, second = levels[energy - shift + SMAX], levels[energy + shift + SMAX]

                @pl.when((offsets_ref[q] == offset) & (shifts_ref[q] == shift))
                def _():
                    for m in range(listed):
                        for part in range(2):
                            here = pl.ds(m * rows, rows)
                            a = first[0][0, first[1], part, here, :].astype(jnp.float32)
                            b = second[0][0, second[1], part, here, :].astype(jnp.float32)
                            mixed[m, pl.ds(part * rows, rows), :] = (weight * a + (weight + 1.0) * b).astype(
                                jnp.bfloat16
                            )

        wanted = functools.reduce(lambda x, y: x | y, [offsets_ref[q] == offset for offset, _ in groups])

        @pl.when(wanted)
        def _():
            sandwich(left_ref, right_ref, q, lists_ref, mixed, half, total)


def scratch(listed, block):
    return [
        pltpu.VMEM((listed, 2 * block, listed * block), jnp.bfloat16),
        pltpu.VMEM((listed, listed * block, 2 * block), jnp.bfloat16),
        pltpu.VMEM((listed, listed * block, 2 * block), jnp.float32),
    ]


def message_kernel(energy, offset, pick, *refs):
    scalar_refs, refs = refs[:4], refs[4:]
    left_ref, right_ref, *sources = refs[: -4]
    message_ref, mixed, half, total = refs[-4:]
    accumulate(energy, [(offset, pick(sources))], scalar_refs, left_ref, right_ref, mixed, half, total)
    message_ref[...] = total[...].astype(jnp.bfloat16)


def result_kernel(energies, picks, *refs):
    scalar_refs, refs = refs[:4], refs[4:]
    left_ref, right_ref, *sources = refs[: -5]
    arrived, out_ref, mixed, half, total = refs[-5:]
    block = left_ref.shape[2] // 2
    for energy in range(energies):
        groups = [(offset, pick(sources)) for offset, pick in picks]
        accumulate(energy, groups, scalar_refs, left_ref, right_ref, mixed, half, total)
        for column in range(left_ref.shape[1]):
            for part in range(2):
                value = total[column, :, pl.ds(part * block, block)]
                if energy == 0:
                    value = value + arrived[column, :, pl.ds(part * block, block)].astype(jnp.float32)
                out_ref[0, energy, part, :, pl.ds(column * block, block)] = value


def final_kernel(sum_ref, arrived_ref, out_ref):
    block = arrived_ref.shape[-1] // 2
    for part in range(2):
        out_ref[0, 0, part] = sum_ref[0, 0, part] + arrived_ref[0, :, pl.ds(part * block, block)].astype(jnp.float32)


def final(energy, sums, arrived):
    listed, orbitals, _ = arrived.shape
    block = orbitals // listed
    sum_spec = pl.BlockSpec((1, 1, 2, orbitals, block), lambda c: (0, energy, 0, 0, c))
    return pl.pallas_call(
        final_kernel,
        grid=(listed,),
        in_specs=[sum_spec, pl.BlockSpec((1, orbitals, 2 * block), lambda c: (c, 0, 0))],
        out_specs=sum_spec,
        out_shape=jax.ShapeDtypeStruct(sums.shape, sums.dtype),
        input_output_aliases={0: 0},
        name="final",
    )(sums, arrived)


def on_device(green_lesser, coupling, block_list, offsets, shifts, occupation):
    _, energies, _, orbitals, _ = green_lesser.shape
    listed, block = coupling.shape[1], coupling.shape[-1]
    assert green_lesser.shape[0] == 1 and energies == SMAX
    momenta, ranks = lax.axis_size("kz"), lax.axis_size("en")
    up, down = ring(ranks, 1, False), ring(ranks, -1, False)

    near = lax.ppermute(green_lesser, "kz", ring(momenta, -1, True))
    low = lax.ppermute(green_lesser, "en", up)
    high0 = lax.ppermute(green_lesser[:, :1], "en", down)
    high1 = lax.ppermute(green_lesser[:, 1:], "en", down)
    left, right = factors(coupling)
    scalar_args = (block_list.reshape(-1), offsets, shifts, occupation)

    def message(energy, sources, pick):
        return pl.pallas_call(
            functools.partial(message_kernel, energy, 1, pick),
            in_specs=scalars(4) + whole(2 + len(sources)),
            out_specs=pl.BlockSpec(memory_space=pltpu.VMEM),
            out_shape=jax.ShapeDtypeStruct((listed, orbitals, 2 * block), jnp.bfloat16),
            scratch_shapes=scratch(listed, block),
            compiler_params=pltpu.CompilerParams(vmem_limit_bytes=VMEM_LIMIT),
            cost_estimate=pl.CostEstimate(flops=10**9, bytes_accessed=10 * 2**20, transcendentals=0),
            name="message%d" % energy,
        )(*scalar_args, left, right, *sources)

    forward = ring(momenta, 1, True)

    def pick0(refs):
        own, low, high0 = refs
        return [(low, 0), (low, 1), (own, 0), (own, 1), (high0, 0), None]

    def pick1(refs):
        own, low, high0, high1 = refs
        return [(low, 0), (low, 1), (own, 0), (own, 1), (high0, 0), (high1, 0)]

    sent0 = message(0, (green_lesser, low, high0), pick0)
    arrived0 = lax.ppermute(sent0, "kz", forward)
    near_low = lax.ppermute(near, "en", up)
    near_high = lax.ppermute(near, "en", down)
    sent1 = message(1, (green_lesser, low, high0, high1), pick1)
    arrived1 = lax.ppermute(sent1, "kz", forward)

    def pick_own(refs):
        return pick1(refs[:4])

    def pick_near(refs):
        own, low, high = refs[4:]
        return [(low, 0), (low, 1), (own, 0), (own, 1), (high, 0), (high, 1)]

    sums = pl.pallas_call(
        functools.partial(result_kernel, energies, [(0, pick_own), (-1, pick_near)]),
        in_specs=scalars(4) + whole(10),
        out_specs=pl.BlockSpec(memory_space=pltpu.VMEM),
        out_shape=jax.ShapeDtypeStruct(green_lesser.shape, jnp.float32),
        scratch_shapes=scratch(listed, block),
        compiler_params=pltpu.CompilerParams(vmem_limit_bytes=VMEM_LIMIT),
        cost_estimate=pl.CostEstimate(flops=2 * 10**9, bytes_accessed=20 * 2**20, transcendentals=0),
        name="result",
    )(*scalar_args, left, right, green_lesser, low, high0, high1, near, near_low, near_high, arrived0)
    return final(1, sums, arrived1)


def solution(mesh):
    placed = (P("kz", "en", None, None, None), P(), P(), P(), P(), P())
    return jax.shard_map(
        on_device,
        mesh=mesh,
        in_specs=placed,
        out_specs=P("kz", "en", None, None, None),
        check_vma=False,
    )
```

time: 411 us -> 149 us (0.36); the launches traced: 406 us -> 149 us
  waiting for transfers between devices: 204 us -> 84.8 us
  local copies, waits for them, and re-layouts: 105 us -> 7.34 us
  other arithmetic: 51.5 us -> 0 us
  Pallas kernels: 0 us -> 38.2 us
  matrix products: 22.5 us -> 0 us
  between operations: 13.3 us -> 0.08 us
  starting transfers between devices: 9.82 us -> 18.5 us
    ppermute x4 -> x8, waiting for transfers between devices: 204 us -> 84.8 us  [the longest x1 37.7 us: on_device(): high1 = lax.ppermute(green_lesser[:, 1:], 'en', down)]
    gather x15 -> x0, local copies, waits for them, and re-layouts: 55 us -> none  [the longest x6 20.5 us: sandwich(): picked = jnp.take(row_blocks, column_index, axis=2)]
    pallas_call x0 -> x5, Pallas kernels: none -> 38.2 us  [the longest x1 14 us: on_device(): pl.pallas_call(functools.partial(result_kernel, energies, [(0, pick_own),...]
    dot_general x24 -> x0, matrix products: 22.5 us -> none  [the longest x12 17.3 us: product_right(): jnp.einsum('lony,nxy->lonx', other, matrix, preferred_element_type=jnp.fl...]
    reshape x6 -> x1, local copies, waits for them, and re-layouts: 20.6 us -> 0.61 us  [on_device(): scalar_args = (block_list.reshape(-1), offsets, shifts, occupation)]
    select_n x11 -> x0, other arithmetic: 17.8 us -> none  [the longest x3 8.23 us: sandwich(): left_half = jnp.take(products, inverse, axis=2)]
    select_n x3 -> x0, local copies, waits for them, and re-layouts: 10.7 us -> none  [sandwich(): left_half = jnp.take(products, inverse, axis=2)]
    add x2 -> x0, local copies, waits for them, and re-layouts: 10.5 us -> none  [on_device(): sigma_sum = sigma_sum + term.reshape(green_lesser.shape)]
  transfers between devices with their start and end apart: 4 -> 8, of which waited for: 4 -> 3; matrix products, arithmetic and copies ran while one was open for 1% -> 3% of each run, Pallas kernels for 0% -> 23%
where the time goes in v1:
time: 149 us
  waiting for transfers between devices  84.8 us (57%)
  Pallas kernels  38.2 us (26%)
  starting transfers between devices  18.5 us (12%)
  local copies, waits for them, and re-layouts  7.34 us (5%)
    ppermute x1, waiting for transfers between devices, on_device(): high1 = lax.ppermute(green_lesser[:, 1:], 'en', down)  37.7 us
    ppermute x1, waiting for transfers between devices, on_device(): near = lax.ppermute(green_lesser, 'kz', ring(momenta, -1, True))  35.7 us
    pallas_call x1, Pallas kernels, on_device(): pl.pallas_call(functools.partial(result_kernel, energies, [(0, pick_own),...  14 us
    pallas_call x2, Pallas kernels, message(): pl.pallas_call(functools.partial(message_kernel, energy, 1, pick), in_spe...  12.3 us
    ppermute x1, waiting for transfers between devices, on_device(): arrived1 = lax.ppermute(sent1, 'kz', forward)  11.4 us
    pallas_call x1, Pallas kernels, factors(): pl.pallas_call(factors_kernel, grid=(transfers, listed), in_specs=[pl.Blo...  7.87 us
    ppermute x1, starting transfers between devices, on_device(): near_low = lax.ppermute(near, 'en', up)  4.54 us
    pallas_call x1, Pallas kernels, final(): pl.pallas_call(final_kernel, grid=(listed,), in_specs=[sum_spec, pl.Block...  3.97 us
  transfers between devices with their start and end apart: 8, of which 3 were waited for; matrix products, arithmetic and copies ran while one was open for 3% of the time, Pallas kernels for 23%

profile of v1, /device:TPU:3, one launch (start us, length us, event | category | flops | bytes accessed | tf_op | source)
XLA Modules:
  0.0 148.9 jit_solution(5216032317300286313)
XLA Ops:
  0.0 0.0 copy-start.4
  0.0 3.3 %collective-permute-start.3 = (bf16[1,2,2,512,512]{4,3,2,1,0:T(8,128)(2,1)}, bf16[1,2,2,512,512]{4,3,2,1,0:T(8,128)(2,1)}, u32[]{:S(2)}, u32[]{:S(2)}) collective-permute-start(bf16[1,2,2,512,512]{4,3,2,1,0:T(8,128)(2,1)} %refs_6_.5), channel_id=1, source_target_pairs={{8,0},{16,8},{24,16},{0,24},{9,1},{17,9},{25,17},{1,25},{10,2},{18... | collective-permute-start | bytes 6291464 | tf_op jit(solution)/shard_map/ppermute | solution.py:173
  3.3 4.0 %collective-permute-start = (bf16[1,2,2,512,512]{4,3,2,1,0:T(8,128)(2,1)}, bf16[1,2,2,512,512]{4,3,2,1,0:T(8,128)(2,1)S(1)}, u32[]{:S(2)}, u32[]{:S(2)}) collective-permute-start(bf16[1,2,2,512,512]{4,3,2,1,0:T(8,128)(2,1)} %refs_6_.5), channel_id=1, source_target_pairs={{0,1},{1,2},{2,3},{3,4},{4,5},{5,6},{6,7},{8,9},{9,10},{10,11},{11... | collective-permute-start | bytes 6291464 | tf_op jit(solution)/shard_map/ppermute | solution.py:174
  7.3 3.0 %fusion = (bf16[1,1,2,512,512]{4,3,2,1,0:T(8,128)(2,1)}, bf16[1,1,2,512,512]{4,3,2,1,0:T(8,128)(2,1)}) fusion(bf16[1,2,2,512,512]{4,3,2,1,0:T(8,128)(2,1)} %refs_6_.5), kind=kLoop, calls=%fused_computation | loop fusion | bytes 4194304 | tf_op jit(solution)/shard_map/slice | solution.py:176
  10.3 1.9 %collective-permute-start.1 = (bf16[1,1,2,512,512]{4,3,2,1,0:T(8,128)(2,1)}, bf16[1,1,2,512,512]{4,3,2,1,0:T(8,128)(2,1)S(1)}, u32[]{:S(2)}, u32[]{:S(2)}) collective-permute-start(bf16[1,1,2,512,512]{4,3,2,1,0:T(8,128)(2,1)} %get-tuple-element.10), channel_id=1, source_target_pairs={{1,0},{2,1},{3,2},{4,3},{5,4},{6,5},{7,6},{9,8},{10,9},{11,10},{12... | collective-permute-start | bytes 3145736 | tf_op jit(solution)/shard_map/ppermute | solution.py:175
  12.2 35.7 %collective-permute-done.3.refs_10_ = bf16[1,2,2,512,512]{4,3,2,1,0:T(8,128)(2,1)} collective-permute-done((bf16[1,2,2,512,512]{4,3,2,1,0:T(8,128)(2,1)}, bf16[1,2,2,512,512]{4,3,2,1,0:T(8,128)(2,1)}, u32[]{:S(2)}, u32[]{:S(2)}) %collective-permute-start.3) | collective-permute-done | bytes 2097184 | tf_op jit(solution)/shard_map/ppermute | solution.py:173
  47.9 4.5 %collective-permute-start.4 = (bf16[1,2,2,512,512]{4,3,2,1,0:T(8,128)(2,1)}, bf16[1,2,2,512,512]{4,3,2,1,0:T(8,128)(2,1)}, u32[]{:S(2)}, u32[]{:S(2)}) collective-permute-start(bf16[1,2,2,512,512]{4,3,2,1,0:T(8,128)(2,1)} %collective-permute-done.3.refs_10_), channel_id=1, source_target_pairs={{0,1},{1,2},{2,3},{3,4},{4,5},{5,6},{6,7},{8,9},{9,10},{10,11},{11... | collective-permute-start | bytes 6291464 | tf_op jit(solution)/shard_map/ppermute | solution.py:204
  52.5 1.9 %collective-permute-start.5 = (bf16[1,2,2,512,512]{4,3,2,1,0:T(8,128)(2,1)}, bf16[1,2,2,512,512]{4,3,2,1,0:T(8,128)(2,1)}, u32[]{:S(2)}, u32[]{:S(2)}) collective-permute-start(bf16[1,2,2,512,512]{4,3,2,1,0:T(8,128)(2,1)} %collective-permute-done.3.refs_10_), channel_id=1, source_target_pairs={{1,0},{2,1},{3,2},{4,3},{5,4},{6,5},{7,6},{9,8},{10,9},{11,10},{12... | collective-permute-start | bytes 6291464 | tf_op jit(solution)/shard_map/ppermute | solution.py:205
  54.4 2.5 %collective-permute-start.2 = (bf16[1,1,2,512,512]{4,3,2,1,0:T(8,128)(2,1)}, bf16[1,1,2,512,512]{4,3,2,1,0:T(8,128)(2,1)}, u32[]{:S(2)}, u32[]{:S(2)}) collective-permute-start(bf16[1,1,2,512,512]{4,3,2,1,0:T(8,128)(2,1)} %get-tuple-element.9), channel_id=1, source_target_pairs={{1,0},{2,1},{3,2},{4,3},{5,4},{6,5},{7,6},{9,8},{10,9},{11,10},{12... | collective-permute-start | bytes 3145736 | tf_op jit(solution)/shard_map/ppermute | solution.py:176
  57.0 7.9 %factors.1 = (bf16[3,4,256,256]{3,2,1,0:T(8,128)(2,1)}, bf16[3,4,256,256]{3,2,1,0:T(8,128)(2,1)}) custom-call(f32[3,4,2,128,128]{4,3,2,1,0:T(8,128)} %coupling_ref.1), custom_call_target="tpu_custom_call" | custom-call | tf_op jit(solution)/shard_map/factors/pallas_call | solution.py:54
  64.8 0.0 copy-done.4
  64.8 0.1 copy.9
  65.0 0.6 reshape.3.refs_0_
  65.6 0.0 collective-permute-done.1.refs_8_
  65.6 0.0 copy-start.1
  65.6 0.0 collective-permute-done.refs_7_
  65.6 0.0 copy-start
  65.6 1.0 copy-done.1
  66.6 0.6 copy-done
  67.2 6.0 %message0.1 = bf16[4,512,256]{2,1,0:T(8,128)(2,1)} custom-call(s32[24]{0:T(128)} %reshape.3.refs_0_, s32[3]{0:T(128)} %refs_1_.5, s32[3]{0:T(128)} %refs_2_.5, f32[3]{0:T(128)} %refs_3_.5, bf16[3,4,256,256]{3,2,1,0:T(8,128)(2,1)} %get-tuple-element.7.refs_4_, bf16[3,4,256,256]{3,2,1,0:T(8,128)(2,1)} %get-tuple-element.8.refs_5_, ...), custom_call_target="tpu_custom_call" | custom-call | flops 1000000000 | bytes 10485760 | tf_op jit(solution)/shard_map/message0/pallas_call | solution.py:181
  73.2 0.2 collective-permute-start.6
  73.4 37.7 %collective-permute-done.2.refs_9_ = bf16[1,1,2,512,512]{4,3,2,1,0:T(8,128)(2,1)} collective-permute-done((bf16[1,1,2,512,512]{4,3,2,1,0:T(8,128)(2,1)}, bf16[1,1,2,512,512]{4,3,2,1,0:T(8,128)(2,1)}, u32[]{:S(2)}, u32[]{:S(2)}) %collective-permute-start.2) | collective-permute-done | bytes 1048608 | tf_op jit(solution)/shard_map/ppermute | solution.py:176
  111.1 6.3 %message1.1 = bf16[4,512,256]{2,1,0:T(8,128)(2,1)} custom-call(s32[24]{0:T(128)} %reshape.3.refs_0_, s32[3]{0:T(128)} %refs_1_.5, s32[3]{0:T(128)} %refs_2_.5, f32[3]{0:T(128)} %refs_3_.5, bf16[3,4,256,256]{3,2,1,0:T(8,128)(2,1)} %get-tuple-element.7.refs_4_, bf16[3,4,256,256]{3,2,1,0:T(8,128)(2,1)} %get-tuple-element.8.refs_5_, ...), custom_call_target="tpu_custom_call" | custom-call | flops 1000000000 | bytes 10485760 | tf_op jit(solution)/shard_map/message1/pallas_call | solution.py:181
  117.4 0.2 collective-permute-start.7
  117.6 0.0 collective-permute-done.6.refs_13_
  117.6 0.0 copy-start.3
  117.6 0.0 collective-permute-done.4.refs_11_
  117.6 0.0 collective-permute-done.5.refs_12_
  117.6 1.0 copy-done.3
  118.6 14.0 %result.1.sum_ref = f32[1,2,2,512,512]{4,3,2,1,0:T(8,128)} custom-call(s32[24]{0:T(128)} %reshape.3.refs_0_, s32[3]{0:T(128)} %refs_1_.5, s32[3]{0:T(128)} %refs_2_.5, f32[3]{0:T(128)} %refs_3_.5, bf16[3,4,256,256]{3,2,1,0:T(8,128)(2,1)} %get-tuple-element.7.refs_4_, bf16[3,4,256,256]{3,2,1,0:T(8,128)(2,1)} %get-tuple-element.8.refs_5_, ...), custom_call_target="tpu_custom_call" | custom-call | flops 2000000000 | bytes 20971520 | tf_op jit(solution)/shard_map/result/pallas_call | solution.py:216
  132.6 11.4 %collective-permute-done.7.arrived_ref = bf16[4,512,256]{2,1,0:T(8,128)(2,1)S(1)} collective-permute-done((bf16[4,512,256]{2,1,0:T(8,128)(2,1)}, bf16[4,512,256]{2,1,0:T(8,128)(2,1)S(1)}, u32[]{:S(2)}, u32[]{:S(2)}) %collective-permute-start.7) | collective-permute-done | bytes 1048608 | tf_op jit(solution)/shard_map/ppermute | solution.py:207
  144.0 0.0 copy-start.2
  144.0 1.0 copy-done.2
  144.9 4.0 %final.1 = f32[1,2,2,512,512]{4,3,2,1,0:T(8,128)} custom-call(f32[1,2,2,512,512]{4,3,2,1,0:T(8,128)} %result.1.sum_ref, bf16[4,512,256]{2,1,0:T(8,128)(2,1)} %copy-done.2), custom_call_target="tpu_custom_call", output_to_operand_aliasing={{}: (0, {})} | custom-call | tf_op jit(solution)/shard_map/final/pallas_call | solution.py:155
Async XLA Ops:
  0.0 64.8 %copy-start.4 = (s32[3,4,2]{1,2,0:T(2,128)S(1)}, s32[3,4,2]{1,2,0:T(2,128)}, u32[]{:S(2)}) copy-start(s32[3,4,2]{1,2,0:T(2,128)} %param.8) | copy-start | bytes 292
  0.0 47.9 %collective-permute-start.3 = (bf16[1,2,2,512,512]{4,3,2,1,0:T(8,128)(2,1)}, bf16[1,2,2,512,512]{4,3,2,1,0:T(8,128)(2,1)}, u32[]{:S(2)}, u32[]{:S(2)}) collective-permute-start(bf16[1,2,2,512,512]{4,3,2,1,0:T(8,128)(2,1)} %refs_6_.5), channel_id=1, source_target_pairs={{8,0},{16,8},{24,16},{0,24},{9,1},{17,9},{25,17},{1,25},{10,2},{18... | collective-permute-start | bytes 6291464 | tf_op jit(solution)/shard_map/ppermute | solution.py:173
  3.3 62.2 %collective-permute-start = (bf16[1,2,2,512,512]{4,3,2,1,0:T(8,128)(2,1)}, bf16[1,2,2,512,512]{4,3,2,1,0:T(8,128)(2,1)S(1)}, u32[]{:S(2)}, u32[]{:S(2)}) collective-permute-start(bf16[1,2,2,512,512]{4,3,2,1,0:T(8,128)(2,1)} %refs_6_.5), channel_id=1, source_target_pairs={{0,1},{1,2},{2,3},{3,4},{4,5},{5,6},{6,7},{8,9},{9,10},{10,11},{11... | collective-permute-start | bytes 6291464 | tf_op jit(solution)/shard_map/ppermute | solution.py:174
  10.3 55.3 %collective-permute-start.1 = (bf16[1,1,2,512,512]{4,3,2,1,0:T(8,128)(2,1)}, bf16[1,1,2,512,512]{4,3,2,1,0:T(8,128)(2,1)S(1)}, u32[]{:S(2)}, u32[]{:S(2)}) collective-permute-start(bf16[1,1,2,512,512]{4,3,2,1,0:T(8,128)(2,1)} %get-tuple-element.10), channel_id=1, source_target_pairs={{1,0},{2,1},{3,2},{4,3},{5,4},{6,5},{7,6},{9,8},{10,9},{11,10},{12... | collective-permute-start | bytes 3145736 | tf_op jit(solution)/shard_map/ppermute | solution.py:175
  47.9 69.7 %collective-permute-start.4 = (bf16[1,2,2,512,512]{4,3,2,1,0:T(8,128)(2,1)}, bf16[1,2,2,512,512]{4,3,2,1,0:T(8,128)(2,1)}, u32[]{:S(2)}, u32[]{:S(2)}) collective-permute-start(bf16[1,2,2,512,512]{4,3,2,1,0:T(8,128)(2,1)} %collective-permute-done.3.refs_10_), channel_id=1, source_target_pairs={{0,1},{1,2},{2,3},{3,4},{4,5},{5,6},{6,7},{8,9},{9,10},{10,11},{11... | collective-permute-start | bytes 6291464 | tf_op jit(solution)/shard_map/ppermute | solution.py:204
  52.5 65.1 %collective-permute-start.5 = (bf16[1,2,2,512,512]{4,3,2,1,0:T(8,128)(2,1)}, bf16[1,2,2,512,512]{4,3,2,1,0:T(8,128)(2,1)}, u32[]{:S(2)}, u32[]{:S(2)}) collective-permute-start(bf16[1,2,2,512,512]{4,3,2,1,0:T(8,128)(2,1)} %collective-permute-done.3.refs_10_), channel_id=1, source_target_pairs={{1,0},{2,1},{3,2},{4,3},{5,4},{6,5},{7,6},{9,8},{10,9},{11,10},{12... | collective-permute-start | bytes 6291464 | tf_op jit(solution)/shard_map/ppermute | solution.py:205
  54.4 56.7 %collective-permute-start.2 = (bf16[1,1,2,512,512]{4,3,2,1,0:T(8,128)(2,1)}, bf16[1,1,2,512,512]{4,3,2,1,0:T(8,128)(2,1)}, u32[]{:S(2)}, u32[]{:S(2)}) collective-permute-start(bf16[1,1,2,512,512]{4,3,2,1,0:T(8,128)(2,1)} %get-tuple-element.9), channel_id=1, source_target_pairs={{1,0},{2,1},{3,2},{4,3},{5,4},{6,5},{7,6},{9,8},{10,9},{11,10},{12... | collective-permute-start | bytes 3145736 | tf_op jit(solution)/shard_map/ppermute | solution.py:176
  65.6 1.1 copy-start.1
  65.6 1.6 %copy-start = (bf16[1,2,2,512,512]{4,3,2,1,0:T(8,128)(2,1)}, bf16[1,2,2,512,512]{4,3,2,1,0:T(8,128)(2,1)S(1)}, u32[]{:S(2)}) copy-start(bf16[1,2,2,512,512]{4,3,2,1,0:T(8,128)(2,1)S(1)} %collective-permute-done.refs_7_) | copy-start | bytes 6291460
  73.2 44.4 %collective-permute-start.6 = (bf16[4,512,256]{2,1,0:T(8,128)(2,1)}, bf16[4,512,256]{2,1,0:T(8,128)(2,1)S(1)}, u32[]{:S(2)}, u32[]{:S(2)}) collective-permute-start(bf16[4,512,256]{2,1,0:T(8,128)(2,1)} %message0.1), channel_id=1, source_target_pairs={{0,8},{8,16},{16,24},{24,0},{1,9},{9,17},{17,25},{25,1},{2,10},{10... | collective-permute-start | bytes 3145736 | tf_op jit(solution)/shard_map/ppermute | solution.py:203
  117.4 26.6 %collective-permute-start.7 = (bf16[4,512,256]{2,1,0:T(8,128)(2,1)}, bf16[4,512,256]{2,1,0:T(8,128)(2,1)S(1)}, u32[]{:S(2)}, u32[]{:S(2)}) collective-permute-start(bf16[4,512,256]{2,1,0:T(8,128)(2,1)} %message1.1), channel_id=1, source_target_pairs={{0,8},{8,16},{16,24},{24,0},{1,9},{9,17},{17,25},{25,1},{2,10},{10... | collective-permute-start | bytes 3145736 | tf_op jit(solution)/shard_map/ppermute | solution.py:207
  117.6 1.0 copy-start.3
  144.0 1.0 copy-start.2

commit v2 on v0

v2 whole, which is shorter than its diff:
```python
import functools

import jax
import jax.numpy as jnp
from jax import lax
from jax.experimental import pallas as pl
from jax.experimental.pallas import tpu as pltpu
from jax.sharding import PartitionSpec as P

SMAX = 2
VMEM_LIMIT = 16 * 1024 * 1024
ANY = pl.BlockSpec(memory_space=pl.ANY)
SMEM = pl.BlockSpec(memory_space=pltpu.SMEM)
VMEM = pl.BlockSpec(memory_space=pltpu.VMEM)
PARAMS = pltpu.CompilerParams(vmem_limit_bytes=VMEM_LIMIT)
CHEAP = pl.CostEstimate(flops=1, bytes_accessed=1, transcendentals=0)


def ring(count, step, periodic):
    pairs = [(i, i + step) for i in range(count) if 0 <= i + step < count]
    if periodic:
        pairs += [(i, (i + step) % count) for i in range(count) if not 0 <= i + step < count]
    return pairs


def pinned(x):
    return pltpu.with_memory_space_constraint(x, pltpu.VMEM)


def after(value, *earlier):
    return pl.pallas_call(
        lambda *refs: None,
        in_specs=[ANY] * (1 + len(earlier)),
        out_specs=ANY,
        out_shape=jax.ShapeDtypeStruct(value.shape, value.dtype),
        input_output_aliases={0: 0},
        compiler_params=PARAMS,
        cost_estimate=CHEAP,
        name="after",
    )(value, *earlier)


def take_kernel(energy, green_ref, out_ref, sem):
    copy = pltpu.make_async_copy(green_ref.at[:, pl.ds(energy, 1)], out_ref, sem)
    copy.start()
    copy.wait()


def take(green, energy):
    return pl.pallas_call(
        functools.partial(take_kernel, energy),
        in_specs=[ANY],
        out_specs=VMEM,
        out_shape=pltpu.VMEM((1, 1, *green.shape[2:]), green.dtype),
        scratch_shapes=[pltpu.SemaphoreType.DMA],
        compiler_params=PARAMS,
        cost_estimate=CHEAP,
        name="take",
    )(green)


def prepare_kernel(energy, green_ref, coupling_ref, out_ref, left_ref, right_ref, sem):
    copy = pltpu.make_async_copy(green_ref.at[:, pl.ds(energy, 1)], out_ref, sem)
    copy.start()
    transfers, listed, _, block, _ = coupling_ref.shape
    low, high = pl.ds(0, block), pl.ds(block, block)

    @pl.loop(0, transfers)
    def _(q):
        for n in range(listed):
            real, imag = coupling_ref[q, n, 0], coupling_ref[q, n, 1]
            for ref, a, b in ((left_ref, real, imag), (right_ref, real.T, imag.T)):
                ref[q, n, low, low] = a.astype(jnp.bfloat16)
                ref[q, n, low, high] = (-b).astype(jnp.bfloat16)
                ref[q, n, high, low] = b.astype(jnp.bfloat16)
                ref[q, n, high, high] = a.astype(jnp.bfloat16)

    copy.wait()


def prepare(green, energy, coupling):
    transfers, listed, _, block, _ = coupling.shape
    factor = pltpu.VMEM((transfers, listed, 2 * block, 2 * block), jnp.bfloat16)
    return pl.pallas_call(
        functools.partial(prepare_kernel, energy),
        in_specs=[ANY, VMEM],
        out_specs=[VMEM, VMEM, VMEM],
        out_shape=[pltpu.VMEM((1, 1, *green.shape[2:]), green.dtype), factor, factor],
        scratch_shapes=[pltpu.SemaphoreType.DMA],
        compiler_params=PARAMS,
        cost_estimate=CHEAP,
        name="prepare",
    )(green, coupling)


class Terms:
    def __init__(self, scalar_refs, factor_refs, scratch):
        self.lists, self.offsets, self.shifts, self.occupation = scalar_refs
        self.left, self.right = factor_refs
        self.mixed, self.half = scratch
        self.transfers, self.listed = self.left.shape[0], self.left.shape[1]
        self.block = self.left.shape[2] // 2

    def entry(self, q, n, side):
        return self.lists[(q * self.listed + n) * 2 + side]

    def mix(self, q, first, second):
        weight = self.occupation[q]
        block = self.block

        @pl.loop(0, self.listed)
        def _(m):
            here = pl.ds(pl.multiple_of(m * block, block), block)
            for part in range(2):
                a = first[part, here, :].astype(jnp.float32)
                b = second[part, here, :].astype(jnp.float32)
                self.mixed[m, pl.ds(part * block, block), :] = (weight * a + (weight + 1.0) * b).astype(jnp.bfloat16)

    def multiply(self, q, emit):
        block = self.block
        for n in range(self.listed):
            product = jnp.dot(self.left[q, n], self.mixed[self.entry(q, n, 1)], preferred_element_type=jnp.float32)
            product = product.astype(jnp.bfloat16)
            target = pl.ds(pl.multiple_of(self.entry(q, n, 0) * block, block), block)
            for column in range(self.listed):
                for part in range(2):
                    self.half[column, target, pl.ds(part * block, block)] = product[
                        part * block : (part + 1) * block, column * block : (column + 1) * block
                    ]
        for n in range(self.listed):
            product = jnp.dot(self.half[self.entry(q, n, 1)], self.right[q, n], preferred_element_type=jnp.float32)
            emit(self.entry(q, n, 0), product)


def term_scratch(coupling_shape, orbitals):
    _, listed, _, block, _ = coupling_shape
    return [
        pltpu.VMEM((listed, 2 * block, orbitals), jnp.bfloat16),
        pltpu.VMEM((listed, orbitals, 2 * block), jnp.bfloat16),
    ]


def pair_of(energy, shift, own0, own1, low, high0, high1):
    last = None if high1 is None else high1.at[0, 0]
    levels = [low.at[0, 0], low.at[0, 1], own0.at[0, 0], own1.at[0, 0], high0.at[0, 0], last]
    return levels[energy - shift + SMAX], levels[energy + shift + SMAX]


def message_kernel(energy, offset, *refs):
    terms = Terms(refs[:4], refs[4:6], refs[-2:])
    own0, own1, low, high0 = refs[6:10]
    high1 = refs[10] if energy else None
    message_ref, total = refs[-4:-2]
    total[...] = jnp.zeros_like(total)

    @pl.loop(0, terms.transfers)
    def _(q):
        wanted = terms.offsets[q] == offset
        for shift in range(1, SMAX + 1):

            @pl.when(wanted & (terms.shifts[q] == shift))
            def _():
                terms.mix(q, *pair_of(energy, shift, own0, own1, low, high0, high1))

        @pl.when(wanted)
        def _():
            def emit(place, product):
                total[place] += product

            terms.multiply(q, emit)

    message_ref[...] = total[...].astype(jnp.bfloat16)


def add_to(total, energy, block):
    def emit(place, product):
        columns = pl.ds(pl.multiple_of(place * block, block), block)
        for part in range(2):
            total[0, energy, part, :, columns] += product[:, part * block : (part + 1) * block]

    return emit


def first_kernel(own_offset, near_offset, *refs):
    terms = Terms(refs[:4], refs[4:6], refs[-2:])
    own0, own1, low, high0, high1, near0, near_low0, near_high0, total = refs[6:-2]
    energies = total.shape[1]
    total[...] = jnp.zeros_like(total)
    near_sources = {1: near0, 2: near_low0}

    @pl.loop(0, terms.transfers * energies)
    def _(step):
        q = step // energies
        energy = step - q * energies
        own = terms.offsets[q] == own_offset
        near = (terms.offsets[q] == near_offset) & (energy == SMAX - terms.shifts[q])
        for shift in range(1, SMAX + 1):

            @pl.when(near & (terms.shifts[q] == shift))
            def _():
                terms.mix(q, near_sources[shift].at[0, 0], near_high0.at[0, 0])

            for e in range(energies):

                @pl.when(own & (terms.shifts[q] == shift) & (energy == e))
                def _():
                    terms.mix(q, *pair_of(e, shift, own0, own1, low, high0, high1))

        @pl.when(own | near)
        def _():
            terms.multiply(q, add_to(total, energy, terms.block))


def second_kernel(near_offset, *refs):
    terms = Terms(refs[:4], refs[4:6], refs[-3:-1])
    sum_ref, arrived, near1, near_low1, near_high1, total, out_ref = refs[6:-3]
    sem = refs[-1]
    block = terms.block
    total[0, 1] = sum_ref[0, 1]
    for column in range(terms.listed):
        columns = pl.ds(column * block, block)
        for part in range(2):
            total[0, 0, part, :, columns] = sum_ref[0, 0, part, :, columns] + arrived[
                column, :, pl.ds(part * block, block)
            ].astype(jnp.float32)
    near_sources = {1: near1, 2: near_high1}

    @pl.loop(0, terms.transfers)
    def _(q):
        near = terms.offsets[q] == near_offset
        for shift in range(1, SMAX + 1):

            @pl.when(near & (terms.shifts[q] == shift))
            def _():
                terms.mix(q, near_low1.at[0, 0], near_sources[shift].at[0, 0])

        @pl.when(near)
        def _():
            terms.multiply(q, add_to(total, terms.shifts[q] - 1, block))

    copy = pltpu.make_async_copy(total.at[:, pl.ds(0, 1)], out_ref.at[:, pl.ds(0, 1)], sem)
    copy.start()
    copy.wait()


def final_kernel(sum_ref, arrived, _, out_ref, held, sems):
    listed, orbitals, width = arrived.shape
    block = width // 2
    copies = []
    for piece in range(orbitals // block):
        rows = pl.ds(piece * block, block)
        for column in range(listed):
            columns = pl.ds(column * block, block)
            for part in range(2):
                held[part, rows, columns] = sum_ref[0, 1, part, rows, columns] + arrived[
                    column, rows, pl.ds(part * block, block)
                ].astype(jnp.float32)
        copies.append(pltpu.make_async_copy(held.at[:, rows, :], out_ref.at[0, 1, :, rows, :], sems.at[piece]))
        copies[-1].start()
    for copy in copies:
        copy.wait()


def on_device(green_lesser, coupling, block_list, offsets, shifts, occupation):
    _, energies, _, orbitals, _ = green_lesser.shape
    transfers, listed, _, block, _ = coupling.shape
    assert green_lesser.shape[0] == 1 and energies == SMAX
    momenta, ranks = lax.axis_size("kz"), lax.axis_size("en")
    up, down = ring(ranks, 1, False), ring(ranks, -1, False)
    forward, backward = ring(momenta, 1, True), ring(momenta, -1, True)
    scalar_args = (block_list.reshape(-1), offsets, shifts, occupation)
    result = jax.ShapeDtypeStruct(green_lesser.shape, jnp.float32)
    result_held = pltpu.VMEM(green_lesser.shape, jnp.float32)

    green0 = take(green_lesser, 0)
    near0 = lax.ppermute(green0, "kz", backward)
    low = lax.ppermute(green_lesser, "en", up)
    high0 = lax.ppermute(green0, "en", down)
    green1, left, right = prepare(green_lesser, 1, coupling)
    near1 = lax.ppermute(green1, "kz", backward)
    high1 = lax.ppermute(green1, "en", down)
    near_low0 = lax.ppermute(near0, "en", up)
    near_high0 = lax.ppermute(near0, "en", down)
    factors = (pinned(left), pinned(right))

    def call(kernel, out_shape, scratch, name, *operands):
        out_specs = VMEM
        if isinstance(out_shape, tuple):
            out_specs = (VMEM, ANY)
        return pl.pallas_call(
            kernel,
            in_specs=[SMEM] * 4 + [VMEM] * (2 + len(operands)),
            out_specs=out_specs,
            out_shape=out_shape,
            scratch_shapes=scratch,
            compiler_params=PARAMS,
            cost_estimate=CHEAP,
            name=name,
        )(*scalar_args, *factors, *[pinned(x) for x in operands])

    def message(energy, *operands):
        total = pltpu.VMEM((listed, orbitals, 2 * block), jnp.float32)
        sent = pltpu.VMEM(total.shape, jnp.bfloat16)
        scratch = [total, *term_scratch(coupling.shape, orbitals)]
        return call(functools.partial(message_kernel, energy, 1), sent, scratch, "message%d" % energy, *operands)

    sent0 = message(0, green0, green1, low, high0)
    arrived0 = lax.ppermute(sent0, "kz", forward)
    near1 = after(near1, sent0)
    near_low1 = lax.ppermute(near1, "en", up)
    near_high1 = lax.ppermute(near1, "en", down)
    sent1 = message(1, green0, green1, low, high0, high1)
    arrived1 = lax.ppermute(sent1, "kz", forward)

    scratch = term_scratch(coupling.shape, orbitals)
    sums = call(
        functools.partial(first_kernel, 0, -1),
        result_held,
        scratch,
        "first",
        *(green0, green1, low, high0, high1, near0, near_low0, near_high0),
    )
    sums, partial = call(
        functools.partial(second_kernel, -1),
        (result_held, result),
        [*scratch, pltpu.SemaphoreType.DMA],
        "second",
        *(sums, arrived0, near1, near_low1, near_high1),
    )
    return pl.pallas_call(
        final_kernel,
        in_specs=[VMEM, VMEM, ANY],
        out_specs=ANY,
        out_shape=result,
        scratch_shapes=[
            pltpu.VMEM(green_lesser.shape[2:], jnp.float32),
            pltpu.SemaphoreType.DMA((orbitals // block,)),
        ],
        input_output_aliases={2: 0},
        compiler_params=PARAMS,
        cost_estimate=CHEAP,
        name="final",
    )(pinned(sums), pinned(arrived1), partial)


def solution(mesh):
    placed = (P("kz", "en", None, None, None), P(), P(), P(), P(), P())
    return jax.shard_map(
        on_device,
        mesh=mesh,
        in_specs=placed,
        out_specs=P("kz", "en", None, None, None),
        check_vma=False,
    )
```

time: 411 us -> 109 us (0.27); the launches traced: 406 us -> 109 us
  waiting for transfers between devices: 204 us -> 57.5 us
  local copies, waits for them, and re-layouts: 105 us -> 1.82 us
  other arithmetic: 51.5 us -> 0 us
  Pallas kernels: 0 us -> 25.3 us
  matrix products: 22.5 us -> 0 us
  starting transfers between devices: 9.82 us -> 24.1 us
  between operations: 13.3 us -> 0.18 us
    ppermute x4 -> x11, waiting for transfers between devices: 204 us -> 57.5 us  [the longest x1 16.6 us: on_device(): near0 = lax.ppermute(green0, 'kz', backward)]
    gather x15 -> x0, local copies, waits for them, and re-layouts: 55 us -> none  [the longest x6 20.5 us: sandwich(): picked = jnp.take(row_blocks, column_index, axis=2)]
    pallas_call x0 -> x8, Pallas kernels: none -> 25.3 us  [the longest x4 21.2 us: call(): pl.pallas_call(kernel, in_specs=[SMEM] * 4 + [VMEM] * (2 + len(operands))...]
    dot_general x24 -> x0, matrix products: 22.5 us -> none  [the longest x12 17.3 us: product_right(): jnp.einsum('lony,nxy->lonx', other, matrix, preferred_element_type=jnp.fl...]
    reshape x6 -> x1, local copies, waits for them, and re-layouts: 20.6 us -> 0.09 us  [on_device(): scalar_args = (block_list.reshape(-1), offsets, shifts, occupation)]
    select_n x11 -> x0, other arithmetic: 17.8 us -> none  [the longest x3 8.23 us: sandwich(): left_half = jnp.take(products, inverse, axis=2)]
    ppermute x4 -> x11, starting transfers between devices: 9.82 us -> 24.1 us  [the longest x1 4.5 us: on_device(): arrived0 = lax.ppermute(sent0, 'kz', forward)]
    select_n x3 -> x0, local copies, waits for them, and re-layouts: 10.7 us -> none  [sandwich(): left_half = jnp.take(products, inverse, axis=2)]
  transfers between devices with their start and end apart: 4 -> 11, of which waited for: 4 -> 8; matrix products, arithmetic and copies ran while one was open for 1% -> 0% of each run, Pallas kernels for 0% -> 22%
where the time goes in v2:
time: 109 us
  waiting for transfers between devices  57.5 us (53%)
  Pallas kernels  25.3 us (23%)
  starting transfers between devices  24.1 us (22%)
  local copies, waits for them, and re-layouts  1.82 us (2%)
    pallas_call x4, Pallas kernels, call(): pl.pallas_call(kernel, in_specs=[SMEM] * 4 + [VMEM] * (2 + len(operands))...  21.2 us
    ppermute x1, waiting for transfers between devices, on_device(): near0 = lax.ppermute(green0, 'kz', backward)  16.6 us
    ppermute x1, waiting for transfers between devices, on_device(): near_high0 = lax.ppermute(near0, 'en', down)  14.6 us
    ppermute x1, waiting for transfers between devices, on_device(): near_high1 = lax.ppermute(near1, 'en', down)  7.32 us
    ppermute x1, waiting for transfers between devices, on_device(): arrived1 = lax.ppermute(sent1, 'kz', forward)  6.77 us
    ppermute x1, waiting for transfers between devices, on_device(): near1 = lax.ppermute(green1, 'kz', backward)  5.07 us
    ppermute x1, starting transfers between devices, on_device(): arrived0 = lax.ppermute(sent0, 'kz', forward)  4.5 us
    ppermute x1, starting transfers between devices, on_device(): low = lax.ppermute(green_lesser, 'en', up)  3.67 us
  transfers between devices with their start and end apart: 11, of which 8 were waited for; matrix products, arithmetic and copies ran while one was open for 0% of the time, Pallas kernels for 22%

profile of v2, /device:TPU:3, one launch (start us, length us, event | category | flops | bytes accessed | tf_op | source)
XLA Modules:
  0.0 108.9 jit_solution(10989378127888773736)
XLA Ops:
  0.0 3.7 %collective-permute-start = (bf16[1,2,2,512,512]{4,3,2,1,0:T(8,128)(2,1)}, bf16[1,2,2,512,512]{4,3,2,1,0:T(8,128)(2,1)}, u32[]{:S(2)}, u32[]{:S(2)}) collective-permute-start(bf16[1,2,2,512,512]{4,3,2,1,0:T(8,128)(2,1)} %green_ref.3), channel_id=1, source_target_pairs={{0,1},{1,2},{2,3},{3,4},{4,5},{5,6},{6,7},{8,9},{9,10},{10,11},{11... | collective-permute-start | bytes 6291464 | tf_op jit(solution)/shard_map/ppermute | solution.py:277
  3.7 0.0 copy-start
  3.7 1.6 %copy-done = bf16[1,2,2,512,512]{4,3,2,1,0:T(8,128)(2,1)S(1)} copy-done((bf16[1,2,2,512,512]{4,3,2,1,0:T(8,128)(2,1)S(1)}, bf16[1,2,2,512,512]{4,3,2,1,0:T(8,128)(2,1)}, u32[]{:S(2)}) %copy-start) | copy-done | bytes 2097176
  5.3 0.0 copy-start.1
  5.3 1.1 take.1.refs_6_
  6.3 0.0 copy-start.5
  6.4 0.0 copy-start.2
  6.4 0.0 copy-start.3
  6.4 0.0 copy-start.4
  6.4 3.4 %collective-permute-start.3 = (bf16[1,1,2,512,512]{4,3,2,1,0:T(8,128)(2,1)}, bf16[1,1,2,512,512]{4,3,2,1,0:T(8,128)(2,1)}, u32[]{:S(2)}, u32[]{:S(2)}) collective-permute-start(bf16[1,1,2,512,512]{4,3,2,1,0:T(8,128)(2,1)} %take.1.refs_6_), channel_id=1, source_target_pairs={{8,0},{16,8},{24,16},{0,24},{9,1},{17,9},{25,17},{1,25},{10,2},{18... | collective-permute-start | bytes 3145736 | tf_op jit(solution)/shard_map/ppermute | solution.py:276
  9.8 1.9 %collective-permute-start.1 = (bf16[1,1,2,512,512]{4,3,2,1,0:T(8,128)(2,1)}, bf16[1,1,2,512,512]{4,3,2,1,0:T(8,128)(2,1)}, u32[]{:S(2)}, u32[]{:S(2)}) collective-permute-start(bf16[1,1,2,512,512]{4,3,2,1,0:T(8,128)(2,1)} %take.1.refs_6_), channel_id=1, source_target_pairs={{1,0},{2,1},{3,2},{4,3},{5,4},{6,5},{7,6},{9,8},{10,9},{11,10},{12... | collective-permute-start | bytes 3145736 | tf_op jit(solution)/shard_map/ppermute | solution.py:278
  11.7 0.0 copy-done.1
  11.7 1.7 %prepare.1 = (bf16[1,1,2,512,512]{4,3,2,1,0:T(8,128)(2,1)}, bf16[3,4,256,256]{3,2,1,0:T(8,128)(2,1)S(1)}, bf16[3,4,256,256]{3,2,1,0:T(8,128)(2,1)S(1)}) custom-call(bf16[1,2,2,512,512]{4,3,2,1,0:T(8,128)(2,1)S(1)} %copy-done, f32[3,4,2,128,128]{4,3,2,1,0:T(8,128)S(1)} %copy-done.1), custom_call_target="tpu_custom_call" | custom-call | flops 1 | bytes 1 | tf_op jit(solution)/shard_map/prepare/pallas_call | solution.py:84
  13.4 0.2 collective-permute-start.7
  13.6 2.8 %collective-permute-start.2 = (bf16[1,1,2,512,512]{4,3,2,1,0:T(8,128)(2,1)}, bf16[1,1,2,512,512]{4,3,2,1,0:T(8,128)(2,1)}, u32[]{:S(2)}, u32[]{:S(2)}) collective-permute-start(bf16[1,1,2,512,512]{4,3,2,1,0:T(8,128)(2,1)} %get-tuple-element.12.refs_7_), channel_id=1, source_target_pairs={{1,0},{2,1},{3,2},{4,3},{5,4},{6,5},{7,6},{9,8},{10,9},{11,10},{12... | collective-permute-start | bytes 3145736 | tf_op jit(solution)/shard_map/ppermute | solution.py:281
  16.4 16.6 %collective-permute-done.3.refs_11_ = bf16[1,1,2,512,512]{4,3,2,1,0:T(8,128)(2,1)} collective-permute-done((bf16[1,1,2,512,512]{4,3,2,1,0:T(8,128)(2,1)}, bf16[1,1,2,512,512]{4,3,2,1,0:T(8,128)(2,1)}, u32[]{:S(2)}, u32[]{:S(2)}) %collective-permute-start.3) | collective-permute-done | bytes 1048608 | tf_op jit(solution)/shard_map/ppermute | solution.py:276
  33.0 1.9 %collective-permute-start.5 = (bf16[1,1,2,512,512]{4,3,2,1,0:T(8,128)(2,1)}, bf16[1,1,2,512,512]{4,3,2,1,0:T(8,128)(2,1)}, u32[]{:S(2)}, u32[]{:S(2)}) collective-permute-start(bf16[1,1,2,512,512]{4,3,2,1,0:T(8,128)(2,1)} %collective-permute-done.3.refs_11_), channel_id=1, source_target_pairs={{1,0},{2,1},{3,2},{4,3},{5,4},{6,5},{7,6},{9,8},{10,9},{11,10},{12... | collective-permute-start | bytes 3145736 | tf_op jit(solution)/shard_map/ppermute | solution.py:283
  34.9 0.0 copy-done.5
  34.9 0.1 copy.10
  35.0 0.1 reshape.3.refs_0_
  35.1 3.3 %collective-permute-done.1.refs_9_ = bf16[1,1,2,512,512]{4,3,2,1,0:T(8,128)(2,1)} collective-permute-done((bf16[1,1,2,512,512]{4,3,2,1,0:T(8,128)(2,1)}, bf16[1,1,2,512,512]{4,3,2,1,0:T(8,128)(2,1)}, u32[]{:S(2)}, u32[]{:S(2)}) %collective-permute-start.1) | collective-permute-done | bytes 1048608 | tf_op jit(solution)/shard_map/ppermute | solution.py:278
  38.4 1.9 %collective-permute-start.4 = (bf16[1,1,2,512,512]{4,3,2,1,0:T(8,128)(2,1)}, bf16[1,1,2,512,512]{4,3,2,1,0:T(8,128)(2,1)S(1)}, u32[]{:S(2)}, u32[]{:S(2)}) collective-permute-start(bf16[1,1,2,512,512]{4,3,2,1,0:T(8,128)(2,1)} %collective-permute-done.3.refs_11_), channel_id=1, source_target_pairs={{0,1},{1,2},{2,3},{3,4},{4,5},{5,6},{6,7},{8,9},{9,10},{10,11},{11... | collective-permute-start | bytes 3145736 | tf_op jit(solution)/shard_map/ppermute | solution.py:282
  40.3 0.2 collective-permute-done.refs_8_
  40.5 0.0 copy-done.2
  40.5 0.0 copy-done.3
  40.5 0.0 copy-done.4
  40.5 5.4 %message0.1.refs_1_ = bf16[4,512,256]{2,1,0:T(8,128)(2,1)S(1)} custom-call(s32[24]{0:T(128)S(1)} %reshape.3.refs_0_, s32[3]{0:T(128)S(1)} %copy-done.2, s32[3]{0:T(128)S(1)} %copy-done.3, f32[3]{0:T(128)S(1)} %copy-done.4, bf16[3,4,256,256]{3,2,1,0:T(8,128)(2,1)S(1)} %get-tuple-element.10.refs_4_, bf16[3,4,256,256]{3,2,1,0:T(8,128)(2,1)S(1)} %get-tuple-element.11.refs_5_, ...), custom_call_target="tpu_custom_call" | custom-call | flops 1 | bytes 1 | tf_op jit(solution)/shard_map/message0/pallas_call | solution.py:290
  46.0 4.5 %collective-permute-start.6 = (bf16[4,512,256]{2,1,0:T(8,128)(2,1)S(1)}, bf16[4,512,256]{2,1,0:T(8,128)(2,1)S(1)}, u32[]{:S(2)}, u32[]{:S(2)}) collective-permute-start(bf16[4,512,256]{2,1,0:T(8,128)(2,1)S(1)} %message0.1.refs_1_), channel_id=1, source_target_pairs={{0,8},{8,16},{16,24},{24,0},{1,9},{9,17},{17,25},{25,1},{2,10},{10... | collective-permute-start | bytes 3145736 | tf_op jit(solution)/shard_map/ppermute | solution.py:308
  50.5 5.1 %collective-permute-done.7.refs_0_ = bf16[1,1,2,512,512]{4,3,2,1,0:T(8,128)(2,1)} collective-permute-done((bf16[1,1,2,512,512]{4,3,2,1,0:T(8,128)(2,1)}, bf16[1,1,2,512,512]{4,3,2,1,0:T(8,128)(2,1)}, u32[]{:S(2)}, u32[]{:S(2)}) %collective-permute-start.7) | collective-permute-done | bytes 1048608 | tf_op jit(solution)/shard_map/ppermute | solution.py:280
  55.5 1.9 %collective-permute-start.9 = (bf16[1,1,2,512,512]{4,3,2,1,0:T(8,128)(2,1)}, bf16[1,1,2,512,512]{4,3,2,1,0:T(8,128)(2,1)S(1)}, u32[]{:S(2)}, u32[]{:S(2)}) collective-permute-start(bf16[1,1,2,512,512]{4,3,2,1,0:T(8,128)(2,1)} %after.1.refs_8_), channel_id=1, source_target_pairs={{1,0},{2,1},{3,2},{4,3},{5,4},{6,5},{7,6},{9,8},{10,9},{11,10},{12... | collective-permute-start | bytes 3145736 | tf_op jit(solution)/shard_map/ppermute | solution.py:311
  57.4 3.6 %collective-permute-done.2.refs_10_ = bf16[1,1,2,512,512]{4,3,2,1,0:T(8,128)(2,1)} collective-permute-done((bf16[1,1,2,512,512]{4,3,2,1,0:T(8,128)(2,1)}, bf16[1,1,2,512,512]{4,3,2,1,0:T(8,128)(2,1)}, u32[]{:S(2)}, u32[]{:S(2)}) %collective-permute-start.2) | collective-permute-done | bytes 1048608 | tf_op jit(solution)/shard_map/ppermute | solution.py:281
  61.0 1.9 %collective-permute-start.8 = (bf16[1,1,2,512,512]{4,3,2,1,0:T(8,128)(2,1)}, bf16[1,1,2,512,512]{4,3,2,1,0:T(8,128)(2,1)S(1)}, u32[]{:S(2)}, u32[]{:S(2)}) collective-permute-start(bf16[1,1,2,512,512]{4,3,2,1,0:T(8,128)(2,1)} %after.1.refs_8_), channel_id=1, source_target_pairs={{0,1},{1,2},{2,3},{3,4},{4,5},{5,6},{6,7},{8,9},{9,10},{10,11},{11... | collective-permute-start | bytes 3145736 | tf_op jit(solution)/shard_map/ppermute | solution.py:310
  63.0 5.7 %message1.1 = bf16[4,512,256]{2,1,0:T(8,128)(2,1)S(1)} custom-call(s32[24]{0:T(128)S(1)} %reshape.3.refs_0_, s32[3]{0:T(128)S(1)} %copy-done.2, s32[3]{0:T(128)S(1)} %copy-done.3, f32[3]{0:T(128)S(1)} %copy-done.4, bf16[3,4,256,256]{3,2,1,0:T(8,128)(2,1)S(1)} %get-tuple-element.10.refs_4_, bf16[3,4,256,256]{3,2,1,0:T(8,128)(2,1)S(1)} %get-tuple-element.11.refs_5_, ...), custom_call_target="tpu_custom_call" | custom-call | flops 1 | bytes 1 | tf_op jit(solution)/shard_map/message1/pallas_call | solution.py:290
  68.7 14.6 %collective-permute-done.5.refs_13_ = bf16[1,1,2,512,512]{4,3,2,1,0:T(8,128)(2,1)} collective-permute-done((bf16[1,1,2,512,512]{4,3,2,1,0:T(8,128)(2,1)}, bf16[1,1,2,512,512]{4,3,2,1,0:T(8,128)(2,1)}, u32[]{:S(2)}, u32[]{:S(2)}) %collective-permute-start.5) | collective-permute-done | bytes 1048608 | tf_op jit(solution)/shard_map/ppermute | solution.py:283
  83.3 0.0 collective-permute-start.10
  83.3 0.0 collective-permute-done.4.refs_12_
  83.3 5.5 %first.1.refs_6_ = f32[1,2,2,512,512]{4,3,2,1,0:T(8,128)S(1)} custom-call(s32[24]{0:T(128)S(1)} %reshape.3.refs_0_, s32[3]{0:T(128)S(1)} %copy-done.2, s32[3]{0:T(128)S(1)} %copy-done.3, f32[3]{0:T(128)S(1)} %copy-done.4, bf16[3,4,256,256]{3,2,1,0:T(8,128)(2,1)S(1)} %get-tuple-element.10.refs_4_, bf16[3,4,256,256]{3,2,1,0:T(8,128)(2,1)S(1)} %get-tuple-element.11.refs_5_, ...), custom_call_target="tpu_custom_call" | custom-call | flops 1 | bytes 1 | tf_op jit(solution)/shard_map/first/pallas_call | solution.py:290
  88.9 0.0 collective-permute-done.6.refs_7_
  88.9 7.3 %collective-permute-done.9.refs_10_ = bf16[1,1,2,512,512]{4,3,2,1,0:T(8,128)(2,1)S(1)} collective-permute-done((bf16[1,1,2,512,512]{4,3,2,1,0:T(8,128)(2,1)}, bf16[1,1,2,512,512]{4,3,2,1,0:T(8,128)(2,1)S(1)}, u32[]{:S(2)}, u32[]{:S(2)}) %collective-permute-start.9) | collective-permute-done | bytes 1048608 | tf_op jit(solution)/shard_map/ppermute | solution.py:311
  96.2 0.0 collective-permute-done.8.refs_9_
  96.2 4.5 %second.1 = (f32[1,2,2,512,512]{4,3,2,1,0:T(8,128)S(1)}, f32[1,2,2,512,512]{4,3,2,1,0:T(8,128)}) custom-call(s32[24]{0:T(128)S(1)} %reshape.3.refs_0_, s32[3]{0:T(128)S(1)} %copy-done.2, s32[3]{0:T(128)S(1)} %copy-done.3, f32[3]{0:T(128)S(1)} %copy-done.4, bf16[3,4,256,256]{3,2,1,0:T(8,128)(2,1)S(1)} %get-tuple-element.10.refs_4_, ...), custom_call_target="tpu_custom_call" | custom-call | flops 1 | bytes 1 | tf_op jit(solution)/shard_map/second/pallas_call | solution.py:290
  100.7 6.8 %collective-permute-done.10.arrived = bf16[4,512,256]{2,1,0:T(8,128)(2,1)S(1)} collective-permute-done((bf16[4,512,256]{2,1,0:T(8,128)(2,1)S(1)}, bf16[4,512,256]{2,1,0:T(8,128)(2,1)S(1)}, u32[]{:S(2)}, u32[]{:S(2)}) %collective-permute-start.10) | collective-permute-done | bytes 1048608 | tf_op jit(solution)/shard_map/ppermute | solution.py:313
  107.5 1.4 %final.1 = f32[1,2,2,512,512]{4,3,2,1,0:T(8,128)} custom-call(f32[1,2,2,512,512]{4,3,2,1,0:T(8,128)S(1)} %get-tuple-element.13.sum_ref, bf16[4,512,256]{2,1,0:T(8,128)(2,1)S(1)} %collective-permute-done.10.arrived, f32[1,2,2,512,512]{4,3,2,1,0:T(8,128)} %get-tuple-element.14._), custom_call_target="tpu_custom_call", output_to_operand_aliasing={{}: (2, {})} | custom-call | flops 1 | bytes 1 | tf_op jit(solution)/shard_map/final/pallas_call | solution.py:330
  (1 shorter events, 0.0 us)
Async XLA Ops:
  0.0 40.5 %collective-permute-start = (bf16[1,2,2,512,512]{4,3,2,1,0:T(8,128)(2,1)}, bf16[1,2,2,512,512]{4,3,2,1,0:T(8,128)(2,1)}, u32[]{:S(2)}, u32[]{:S(2)}) collective-permute-start(bf16[1,2,2,512,512]{4,3,2,1,0:T(8,128)(2,1)} %green_ref.3), channel_id=1, source_target_pairs={{0,1},{1,2},{2,3},{3,4},{4,5},{5,6},{6,7},{8,9},{9,10},{10,11},{11... | collective-permute-start | bytes 6291464 | tf_op jit(solution)/shard_map/ppermute | solution.py:277
  3.7 1.6 %copy-start = (bf16[1,2,2,512,512]{4,3,2,1,0:T(8,128)(2,1)S(1)}, bf16[1,2,2,512,512]{4,3,2,1,0:T(8,128)(2,1)}, u32[]{:S(2)}) copy-start(bf16[1,2,2,512,512]{4,3,2,1,0:T(8,128)(2,1)} %green_ref.3) | copy-start | bytes 6291460
  5.3 6.4 %copy-start.1 = (f32[3,4,2,128,128]{4,3,2,1,0:T(8,128)S(1)}, f32[3,4,2,128,128]{4,3,2,1,0:T(8,128)}, u32[]{:S(2)}) copy-start(f32[3,4,2,128,128]{4,3,2,1,0:T(8,128)} %coupling_ref.1) | copy-start | bytes 4718596
  6.3 28.6 %copy-start.5 = (s32[3,4,2]{1,2,0:T(2,128)S(1)}, s32[3,4,2]{1,2,0:T(2,128)}, u32[]{:S(2)}) copy-start(s32[3,4,2]{1,2,0:T(2,128)} %param.8) | copy-start | bytes 292
  6.4 34.2 %copy-start.2 = (s32[3]{0:T(128)S(1)}, s32[3]{0:T(128)}, u32[]{:S(2)}) copy-start(s32[3]{0:T(128)} %refs_1_.7) | copy-start | bytes 40
  6.4 34.2 %copy-start.3 = (s32[3]{0:T(128)S(1)}, s32[3]{0:T(128)}, u32[]{:S(2)}) copy-start(s32[3]{0:T(128)} %refs_2_.7) | copy-start | bytes 40
  6.4 34.2 %copy-start.4 = (f32[3]{0:T(128)S(1)}, f32[3]{0:T(128)}, u32[]{:S(2)}) copy-start(f32[3]{0:T(128)} %refs_3_.7) | copy-start | bytes 40
  6.4 26.6 %collective-permute-start.3 = (bf16[1,1,2,512,512]{4,3,2,1,0:T(8,128)(2,1)}, bf16[1,1,2,512,512]{4,3,2,1,0:T(8,128)(2,1)}, u32[]{:S(2)}, u32[]{:S(2)}) collective-permute-start(bf16[1,1,2,512,512]{4,3,2,1,0:T(8,128)(2,1)} %take.1.refs_6_), channel_id=1, source_target_pairs={{8,0},{16,8},{24,16},{0,24},{9,1},{17,9},{25,17},{1,25},{10,2},{18... | collective-permute-start | bytes 3145736 | tf_op jit(solution)/shard_map/ppermute | solution.py:276
  9.8 28.6 %collective-permute-start.1 = (bf16[1,1,2,512,512]{4,3,2,1,0:T(8,128)(2,1)}, bf16[1,1,2,512,512]{4,3,2,1,0:T(8,128)(2,1)}, u32[]{:S(2)}, u32[]{:S(2)}) collective-permute-start(bf16[1,1,2,512,512]{4,3,2,1,0:T(8,128)(2,1)} %take.1.refs_6_), channel_id=1, source_target_pairs={{1,0},{2,1},{3,2},{4,3},{5,4},{6,5},{7,6},{9,8},{10,9},{11,10},{12... | collective-permute-start | bytes 3145736 | tf_op jit(solution)/shard_map/ppermute | solution.py:278
  13.4 42.2 %collective-permute-start.7 = (bf16[1,1,2,512,512]{4,3,2,1,0:T(8,128)(2,1)}, bf16[1,1,2,512,512]{4,3,2,1,0:T(8,128)(2,1)}, u32[]{:S(2)}, u32[]{:S(2)}) collective-permute-start(bf16[1,1,2,512,512]{4,3,2,1,0:T(8,128)(2,1)} %get-tuple-element.12.refs_7_), channel_id=1, source_target_pairs={{8,0},{16,8},{24,16},{0,24},{9,1},{17,9},{25,17},{1,25},{10,2},{18... | collective-permute-start | bytes 3145736 | tf_op jit(solution)/shard_map/ppermute | solution.py:280
  13.6 47.5 %collective-permute-start.2 = (bf16[1,1,2,512,512]{4,3,2,1,0:T(8,128)(2,1)}, bf16[1,1,2,512,512]{4,3,2,1,0:T(8,128)(2,1)}, u32[]{:S(2)}, u32[]{:S(2)}) collective-permute-start(bf16[1,1,2,512,512]{4,3,2,1,0:T(8,128)(2,1)} %get-tuple-element.12.refs_7_), channel_id=1, source_target_pairs={{1,0},{2,1},{3,2},{4,3},{5,4},{6,5},{7,6},{9,8},{10,9},{11,10},{12... | collective-permute-start | bytes 3145736 | tf_op jit(solution)/shard_map/ppermute | solution.py:281
  33.0 50.3 %collective-permute-start.5 = (bf16[1,1,2,512,512]{4,3,2,1,0:T(8,128)(2,1)}, bf16[1,1,2,512,512]{4,3,2,1,0:T(8,128)(2,1)}, u32[]{:S(2)}, u32[]{:S(2)}) collective-permute-start(bf16[1,1,2,512,512]{4,3,2,1,0:T(8,128)(2,1)} %collective-permute-done.3.refs_11_), channel_id=1, source_target_pairs={{1,0},{2,1},{3,2},{4,3},{5,4},{6,5},{7,6},{9,8},{10,9},{11,10},{12... | collective-permute-start | bytes 3145736 | tf_op jit(solution)/shard_map/ppermute | solution.py:283
  38.4 44.9 %collective-permute-start.4 = (bf16[1,1,2,512,512]{4,3,2,1,0:T(8,128)(2,1)}, bf16[1,1,2,512,512]{4,3,2,1,0:T(8,128)(2,1)S(1)}, u32[]{:S(2)}, u32[]{:S(2)}) collective-permute-start(bf16[1,1,2,512,512]{4,3,2,1,0:T(8,128)(2,1)} %collective-permute-done.3.refs_11_), channel_id=1, source_target_pairs={{0,1},{1,2},{2,3},{3,4},{4,5},{5,6},{6,7},{8,9},{9,10},{10,11},{11... | collective-permute-start | bytes 3145736 | tf_op jit(solution)/shard_map/ppermute | solution.py:282
  46.0 42.9 %collective-permute-start.6 = (bf16[4,512,256]{2,1,0:T(8,128)(2,1)S(1)}, bf16[4,512,256]{2,1,0:T(8,128)(2,1)S(1)}, u32[]{:S(2)}, u32[]{:S(2)}) collective-permute-start(bf16[4,512,256]{2,1,0:T(8,128)(2,1)S(1)} %message0.1.refs_1_), channel_id=1, source_target_pairs={{0,8},{8,16},{16,24},{24,0},{1,9},{9,17},{17,25},{25,1},{2,10},{10... | collective-permute-start | bytes 3145736 | tf_op jit(solution)/shard_map/ppermute | solution.py:308
  55.5 40.7 %collective-permute-start.9 = (bf16[1,1,2,512,512]{4,3,2,1,0:T(8,128)(2,1)}, bf16[1,1,2,512,512]{4,3,2,1,0:T(8,128)(2,1)S(1)}, u32[]{:S(2)}, u32[]{:S(2)}) collective-permute-start(bf16[1,1,2,512,512]{4,3,2,1,0:T(8,128)(2,1)} %after.1.refs_8_), channel_id=1, source_target_pairs={{1,0},{2,1},{3,2},{4,3},{5,4},{6,5},{7,6},{9,8},{10,9},{11,10},{12... | collective-permute-start | bytes 3145736 | tf_op jit(solution)/shard_map/ppermute | solution.py:311
  61.0 35.2 %collective-permute-start.8 = (bf16[1,1,2,512,512]{4,3,2,1,0:T(8,128)(2,1)}, bf16[1,1,2,512,512]{4,3,2,1,0:T(8,128)(2,1)S(1)}, u32[]{:S(2)}, u32[]{:S(2)}) collective-permute-start(bf16[1,1,2,512,512]{4,3,2,1,0:T(8,128)(2,1)} %after.1.refs_8_), channel_id=1, source_target_pairs={{0,1},{1,2},{2,3},{3,4},{4,5},{5,6},{6,7},{8,9},{9,10},{10,11},{11... | collective-permute-start | bytes 3145736 | tf_op jit(solution)/shard_map/ppermute | solution.py:310
  83.3 24.2 %collective-permute-start.10 = (bf16[4,512,256]{2,1,0:T(8,128)(2,1)S(1)}, bf16[4,512,256]{2,1,0:T(8,128)(2,1)S(1)}, u32[]{:S(2)}, u32[]{:S(2)}) collective-permute-start(bf16[4,512,256]{2,1,0:T(8,128)(2,1)S(1)} %message1.1), channel_id=1, source_target_pairs={{0,8},{8,16},{16,24},{24,0},{1,9},{9,17},{17,25},{25,1},{2,10},{10... | collective-permute-start | bytes 3145736 | tf_op jit(solution)/shard_map/ppermute | solution.py:313

commit v3 on v2

v3 whole, which is shorter than its diff:
```python
import functools

import jax
import jax.numpy as jnp
from jax import lax
from jax.experimental import pallas as pl
from jax.experimental.pallas import tpu as pltpu
from jax.sharding import PartitionSpec as P

SMAX = 2
PIECES = 4
VMEM_LIMIT = 12 * 1024 * 1024
ANY = pl.BlockSpec(memory_space=pl.ANY)
SMEM = pl.BlockSpec(memory_space=pltpu.SMEM)
VMEM = pl.BlockSpec(memory_space=pltpu.VMEM)
PARAMS = pltpu.CompilerParams(vmem_limit_bytes=VMEM_LIMIT)
DEAR = pl.CostEstimate(flops=2 * 10**11, bytes_accessed=1, transcendentals=0)
CHEAP = pl.CostEstimate(flops=1, bytes_accessed=1, transcendentals=0)


def ring(count, step):
    return [(i, (i + step) % count) for i in range(count)]


def both_ways(pairs):
    return [*pairs, *[(j, i) for i, j in pairs]]


def pinned(x):
    return pltpu.with_memory_space_constraint(x, pltpu.VMEM)


def after(value, *earlier):
    return pl.pallas_call(
        lambda *refs: None,
        in_specs=[ANY] * (1 + len(earlier)),
        out_specs=ANY,
        out_shape=jax.ShapeDtypeStruct(value.shape, value.dtype),
        input_output_aliases={0: 0},
        compiler_params=PARAMS,
        cost_estimate=DEAR,
        name="after",
    )(value, *earlier)


def odd():
    return lax.axis_index("en") % 2


def fetch(green_ref, energy, out_ref, sems):
    rows = out_ref.shape[1] // sems.shape[1]
    copies = []
    for part in range(sems.shape[0]):
        for piece in range(sems.shape[1]):
            here = pl.ds(piece * rows, rows)
            copies.append(
                pltpu.make_async_copy(
                    green_ref.at[0, energy, part, here, :], out_ref.at[part, here, :], sems.at[part, piece]
                )
            )
            copies[-1].start()
    return copies


def take_kernel(green_ref, out_ref, sems):
    for copy in fetch(green_ref, odd(), out_ref, sems):
        copy.wait()


def take(green):
    return pl.pallas_call(
        take_kernel,
        in_specs=[ANY],
        out_specs=VMEM,
        out_shape=pltpu.VMEM(green.shape[2:], green.dtype),
        scratch_shapes=[pltpu.SemaphoreType.DMA((2, PIECES))],
        compiler_params=PARAMS,
        cost_estimate=CHEAP,
        name="take",
    )(pltpu.with_memory_space_constraint(green, pltpu.HBM))


def prepare_kernel(green_ref, coupling_ref, _, out_ref, left_ref, right_ref, sems):
    copies = fetch(green_ref, 1 - odd(), out_ref, sems)
    transfers, listed, _, block, _ = coupling_ref.shape
    low, high = pl.ds(0, block), pl.ds(block, block)

    @pl.loop(0, transfers)
    def _(q):
        for n in range(listed):
            real, imag = coupling_ref[q, n, 0], coupling_ref[q, n, 1]
            for ref, a, b in ((left_ref, real, imag), (right_ref, real.T, imag.T)):
                ref[q, n, low, low] = a.astype(jnp.bfloat16)
                ref[q, n, low, high] = (-b).astype(jnp.bfloat16)
                ref[q, n, high, low] = b.astype(jnp.bfloat16)
                ref[q, n, high, high] = a.astype(jnp.bfloat16)

    for copy in copies:
        copy.wait()


def prepare(green, coupling, earlier):
    transfers, listed, _, block, _ = coupling.shape
    factor = pltpu.VMEM((transfers, listed, 2 * block, 2 * block), jnp.bfloat16)
    return pl.pallas_call(
        prepare_kernel,
        in_specs=[ANY, VMEM, ANY],
        out_specs=[VMEM, VMEM, VMEM],
        out_shape=[pltpu.VMEM(green.shape[2:], green.dtype), factor, factor],
        scratch_shapes=[pltpu.SemaphoreType.DMA((2, PIECES))],
        compiler_params=PARAMS,
        cost_estimate=CHEAP,
        name="prepare",
    )(pltpu.with_memory_space_constraint(green, pltpu.HBM), coupling, earlier)


class Terms:
    def __init__(self, scalar_refs, factor_refs, scratch):
        self.lists, self.offsets, self.shifts, self.occupation = scalar_refs
        self.left, self.right = factor_refs
        self.mixed, self.half = scratch
        self.transfers, self.listed = self.left.shape[0], self.left.shape[1]
        self.block = self.left.shape[2] // 2

    def entry(self, q, n, side):
        return self.lists[(q * self.listed + n) * 2 + side]

    def mix(self, q, first, second):
        away = self.occupation[q] + jnp.where(odd() == 1, 0.0, 1.0)
        towards = self.occupation[q] + jnp.where(odd() == 1, 1.0, 0.0)
        block = self.block

        @pl.loop(0, self.listed)
        def _(m):
            here = pl.ds(pl.multiple_of(m * block, block), block)
            for part in range(2):
                a = first[part, here, :].astype(jnp.float32)
                b = second[part, here, :].astype(jnp.float32)
                self.mixed[m, pl.ds(part * block, block), :] = (away * a + towards * b).astype(jnp.bfloat16)

    def multiply(self, q, emit):
        block = self.block
        for n in range(self.listed):
            product = jnp.dot(self.left[q, n], self.mixed[self.entry(q, n, 1)], preferred_element_type=jnp.float32)
            product = product.astype(jnp.bfloat16)
            target = pl.ds(pl.multiple_of(self.entry(q, n, 0) * block, block), block)
            for column in range(self.listed):
                for part in range(2):
                    self.half[column, target, pl.ds(part * block, block)] = product[
                        part * block : (part + 1) * block, column * block : (column + 1) * block
                    ]
        for n in range(self.listed):
            product = jnp.dot(self.half[self.entry(q, n, 1)], self.right[q, n], preferred_element_type=jnp.float32)
            emit(self.entry(q, n, 0), product)


def term_scratch(coupling_shape, orbitals):
    _, listed, _, block, _ = coupling_shape
    return [
        pltpu.VMEM((listed, 2 * block, orbitals), jnp.bfloat16),
        pltpu.VMEM((listed, orbitals, 2 * block), jnp.bfloat16),
    ]


def levels_of(chip_mate, *others):
    return (chip_mate.at[0, 1 - odd()], chip_mate.at[0, odd()], *others)


def pair_of(place, shift, levels):
    return levels[place - shift + SMAX], levels[place + shift + SMAX]


def message_kernel(place, offset, *refs):
    terms = Terms(refs[:4], refs[4:6], refs[-2:])
    levels = levels_of(*refs[6:-4])
    message_ref, total = refs[-4:-2]
    total[...] = jnp.zeros_like(total)

    @pl.loop(0, terms.transfers)
    def _(q):
        wanted = terms.offsets[q] == offset
        for shift in range(1, SMAX + 1):

            @pl.when(wanted & (terms.shifts[q] == shift))
            def _():
                terms.mix(q, *pair_of(place, shift, levels))

        @pl.when(wanted)
        def _():
            def emit(row, product):
                total[row] += product

            terms.multiply(q, emit)

    message_ref[...] = total[...].astype(jnp.bfloat16)


def add_to(total, block):
    def emit(row, product):
        columns = pl.ds(pl.multiple_of(row * block, block), block)
        for part in range(2):
            total[part, :, columns] += product[:, part * block : (part + 1) * block]

    return emit


def first_kernel(own_offset, near_offset, *refs):
    terms = Terms(refs[:4], refs[4:6], refs[-2:])
    own, near, totals = levels_of(*refs[6:11]), (*refs[11:16], None), refs[17:-2]
    for total in totals:
        total[...] = jnp.zeros_like(total)

    @pl.loop(0, terms.transfers)
    def _(q):
        is_own = terms.offsets[q] == own_offset
        is_near = terms.offsets[q] == near_offset
        for place, total in enumerate(totals):
            for shift in range(1, SMAX + 1):
                here = terms.shifts[q] == shift

                @pl.when(is_own & here)
                def _():
                    terms.mix(q, *pair_of(place, shift, own))

                if place + shift <= SMAX:

                    @pl.when(is_near & here)
                    def _():
                        terms.mix(q, *pair_of(place, shift, near))

            @pl.when(is_own | (is_near & (terms.shifts[q] + place <= SMAX)))
            def _():
                terms.multiply(q, add_to(total, terms.block))


def second_kernel(near_offset, *refs):
    terms = Terms(refs[:4], refs[4:6], refs[-2:])
    sum_ref, first, second, total = refs[6:-2]
    total[...] = sum_ref[...]

    @pl.loop(0, terms.transfers)
    def _(q):
        @pl.when((terms.offsets[q] == near_offset) & (terms.shifts[q] == SMAX))
        def _():
            terms.mix(q, first, second)
            terms.multiply(q, add_to(total, terms.block))


def store_kernel(place, sum_ref, arrived, *refs):
    out_ref, held, sems = refs[-3:]
    listed, orbitals, width = arrived.shape
    block = width // 2
    energy = odd() * place + (1 - odd()) * (1 - place)
    copies = []
    for piece in range(orbitals // block):
        rows = pl.ds(piece * block, block)
        for column in range(listed):
            columns = pl.ds(column * block, block)
            for part in range(2):
                held[part, rows, columns] = sum_ref[part, rows, columns] + arrived[
                    column, rows, pl.ds(part * block, block)
                ].astype(jnp.float32)
        copies.append(pltpu.make_async_copy(held.at[:, rows, :], out_ref.at[0, energy, :, rows, :], sems.at[piece]))
        copies[-1].start()
    for copy in copies:
        copy.wait()


def store(place, sums, arrived, result, *earlier):
    return pl.pallas_call(
        functools.partial(store_kernel, place),
        in_specs=[VMEM, VMEM] + [ANY] * len(earlier),
        out_specs=ANY,
        out_shape=result,
        scratch_shapes=[
            pltpu.VMEM(result.shape[2:], jnp.float32),
            pltpu.SemaphoreType.DMA((2 * arrived.shape[1] // arrived.shape[2],)),
        ],
        input_output_aliases={2: 0} if earlier else {},
        compiler_params=PARAMS,
        cost_estimate=CHEAP,
        name="store%d" % place,
    )(pinned(sums), pinned(arrived), *earlier)


def on_device(green_lesser, coupling, block_list, offsets, shifts, occupation):
    _, energies, _, orbitals, _ = green_lesser.shape
    transfers, listed, _, block, _ = coupling.shape
    assert green_lesser.shape[0] == 1 and energies == SMAX
    momenta, ranks = lax.axis_size("kz"), lax.axis_size("en")
    forward, backward = ring(momenta, 1), ring(momenta, -1)
    scalar_args = (block_list.reshape(-1), offsets, shifts, occupation)
    result = jax.ShapeDtypeStruct(green_lesser.shape, jnp.float32)
    held = pltpu.VMEM(green_lesser.shape[2:], jnp.float32)

    on_chip = both_ways([(i, i + 1) for i in range(0, ranks - 1, 2)])
    between = both_ways([(i, i + 1) for i in range(1, ranks - 1, 2)])

    def call(kernel, out_shape, name, *operands, scratch=()):
        return pl.pallas_call(
            kernel,
            in_specs=[SMEM] * 4 + [VMEM] * (2 + len(operands)),
            out_specs=[VMEM] * len(out_shape),
            out_shape=out_shape,
            scratch_shapes=[*scratch, *term_scratch(coupling.shape, orbitals)],
            compiler_params=PARAMS,
            cost_estimate=CHEAP,
            name=name,
        )(*scalar_args, pinned(left), pinned(right), *[pinned(x) for x in operands])

    def message(place, *operands):
        total = pltpu.VMEM((listed, orbitals, 2 * block), jnp.float32)
        sent = pltpu.VMEM(total.shape, jnp.bfloat16)
        kernel = functools.partial(message_kernel, place, 1)
        return call(kernel, [sent], "message%d" % place, *operands, scratch=[total])[0]

    own1 = take(green_lesser)
    near1 = lax.ppermute(own1, "kz", backward)
    own2 = lax.ppermute(own1, "en", between)
    own0, left, right = prepare(green_lesser, coupling, own1)
    near0 = lax.ppermute(own0, "kz", backward)
    own3 = lax.ppermute(own0, "en", between)
    own_ = lax.ppermute(green_lesser, "en", on_chip)
    own = (own_, own0, own1, own2, own3)

    sent0 = message(0, *own[:-1])
    arrived0 = lax.ppermute(sent0, "kz", forward)
    near1 = after(near1, sent0)
    near2 = lax.ppermute(near1, "en", between)
    mate1 = lax.ppermute(near1, "en", on_chip)

    sent1 = message(1, *own)
    arrived1 = lax.ppermute(sent1, "kz", forward)
    near0 = after(near0, sent1, mate1)
    near3 = lax.ppermute(near0, "en", between)
    mate0 = lax.ppermute(near0, "en", on_chip)

    first = functools.partial(first_kernel, 0, -1)
    sums0, sums1 = call(first, [held, held], "first", *own, mate1, mate0, near0, near1, near2, arrived0)
    partial = store(0, sums0, arrived0, result)
    second = functools.partial(second_kernel, -1)
    (sums1,) = call(second, [held], "second", sums1, mate0, near3)
    return store(1, sums1, arrived1, result, partial)


def solution(mesh):
    placed = (P("kz", "en", None, None, None), P(), P(), P(), P(), P())
    return jax.shard_map(
        on_device,
        mesh=mesh,
        in_specs=placed,
        out_specs=P("kz", "en", None, None, None),
        check_vma=False,
    )
```

time: 109 us -> 102 us (0.936)
  waiting for transfers between devices: 57.5 us -> 50.8 us
  starting transfers between devices: 24.1 us -> 20.2 us
  Pallas kernels: 25.3 us -> 27.2 us
    ppermute x1, waiting for transfers between devices: 6.77 us -> 0.01 us  [on_device(): arrived1 = lax.ppermute(sent1, 'kz', forward)]
    pallas_call x3 -> x4, Pallas kernels: 4.13 us -> 7.74 us  [the longest x2 4.05 us: store(): pl.pallas_call(functools.partial(store_kernel, place), in_specs=[VMEM, VM...]
    ppermute x1, starting transfers between devices: 4.5 us -> 1.28 us  [on_device(): arrived0 = lax.ppermute(sent0, 'kz', forward)]
    ppermute x9, starting transfers between devices: 19.6 us -> 17.7 us  [the longest x1 3.6 us: on_device(): own3 = lax.ppermute(own0, 'en', between)]
    ppermute x1, waiting for transfers between devices: 0.01 us -> 1.81 us  [on_device(): arrived0 = lax.ppermute(sent0, 'kz', forward)]
    pallas_call x4, Pallas kernels: 21.2 us -> 19.4 us  [call(): pl.pallas_call(kernel, in_specs=[SMEM] * 4 + [VMEM] * (2 + len(operands))...]
    ppermute x9, waiting for transfers between devices: 50.7 us -> 49 us  [the longest x1 14.2 us: on_device(): own2 = lax.ppermute(own1, 'en', between)]
    ppermute x1, starting transfers between devices: 0.01 us -> 1.28 us  [on_device(): arrived1 = lax.ppermute(sent1, 'kz', forward)]
  transfers between devices with their start and end apart: 11 -> 11, of which waited for: 8 -> 5; matrix products, arithmetic and copies ran while one was open for 0% -> 0% of each run, Pallas kernels for 22% -> 25%
where the time goes in v3:
time: 102 us; the launch traced here: 101 us
  waiting for transfers between devices  50.8 us (50%)
  Pallas kernels  27.2 us (27%)
  starting transfers between devices  20.2 us (20%)
  local copies, waits for them, and re-layouts  2.77 us (3%)
    pallas_call x4, Pallas kernels, call(): pl.pallas_call(kernel, in_specs=[SMEM] * 4 + [VMEM] * (2 + len(operands))...  19.4 us
    ppermute x1, waiting for transfers between devices, on_device(): own2 = lax.ppermute(own1, 'en', between)  14.2 us
    ppermute x1, waiting for transfers between devices, on_device(): near2 = lax.ppermute(near1, 'en', between)  13.9 us
    ppermute x1, waiting for transfers between devices, on_device(): own3 = lax.ppermute(own0, 'en', between)  11.7 us
    ppermute x1, waiting for transfers between devices, on_device(): near3 = lax.ppermute(near0, 'en', between)  9.13 us
    pallas_call x2, Pallas kernels, store(): pl.pallas_call(functools.partial(store_kernel, place), in_specs=[VMEM, VM...  4.05 us
    ppermute x1, starting transfers between devices, on_device(): own3 = lax.ppermute(own0, 'en', between)  3.6 us
    ppermute x1, starting transfers between devices, on_device(): near1 = lax.ppermute(own1, 'kz', backward)  3.37 us
  transfers between devices with their start and end apart: 11, of which 5 were waited for; matrix products, arithmetic and copies ran while one was open for 0% of the time, Pallas kernels for 25%

profile of v3, /device:TPU:3, one launch (start us, length us, event | category | flops | bytes accessed | tf_op | source)
XLA Modules:
  0.0 101.2 jit_solution(15667210124735861870)
XLA Ops:
  0.0 0.0 copy-start.3
  0.0 0.7 collective-permute-start
  0.7 1.3 %take.1._.refs_8_ = bf16[2,512,512]{2,1,0:T(8,128)(2,1)S(1)} custom-call(bf16[1,2,2,512,512]{4,3,2,1,0:T(8,128)(2,1)} %green_ref.3), custom_call_target="tpu_custom_call" | custom-call | flops 1 | bytes 1 | tf_op jit(solution)/shard_map/take/pallas_call | solution.py:71
  2.0 0.0 copy-start.7
  2.0 0.0 copy-start.4
  2.1 0.0 copy-start.5
  2.1 0.0 copy-start.6
  2.1 3.3 %collective-permute-start.1 = (bf16[2,512,512]{2,1,0:T(8,128)(2,1)S(1)}, bf16[2,512,512]{2,1,0:T(8,128)(2,1)}, u32[]{:S(2)}, u32[]{:S(2)}) collective-permute-start(bf16[2,512,512]{2,1,0:T(8,128)(2,1)S(1)} %take.1._.refs_8_), channel_id=1, source_target_pairs={{1,2},{3,4},{5,6},{2,1},{4,3},{6,5},{9,10},{11,12},{13,14},{10,9},... | collective-permute-start | bytes 3145736 | tf_op jit(solution)/shard_map/ppermute | solution.py:319
  5.3 3.4 %collective-permute-start.3 = (bf16[2,512,512]{2,1,0:T(8,128)(2,1)S(1)}, bf16[2,512,512]{2,1,0:T(8,128)(2,1)}, u32[]{:S(2)}, u32[]{:S(2)}) collective-permute-start(bf16[2,512,512]{2,1,0:T(8,128)(2,1)S(1)} %take.1._.refs_8_), channel_id=1, source_target_pairs={{0,24},{8,0},{16,8},{24,16},{1,25},{9,1},{17,9},{25,17},{2,26},{10... | collective-permute-start | bytes 3145736 | tf_op jit(solution)/shard_map/ppermute | solution.py:318
  8.7 0.0 copy-done.3
  8.7 2.3 %prepare.1 = (bf16[2,512,512]{2,1,0:T(8,128)(2,1)}, bf16[3,4,256,256]{3,2,1,0:T(8,128)(2,1)S(1)}, bf16[3,4,256,256]{3,2,1,0:T(8,128)(2,1)S(1)}) custom-call(bf16[1,2,2,512,512]{4,3,2,1,0:T(8,128)(2,1)} %green_ref.3, f32[3,4,2,128,128]{4,3,2,1,0:T(8,128)S(1)} %copy-done.3, bf16[2,512,512]{2,1,0:T(8,128)(2,1)S(1)} %take.1._.refs_8_), custom_call_target="tpu_custom_call" | custom-call | flops 1 | bytes 1 | tf_op jit(solution)/shard_map/prepare/pallas_call | solution.py:105
  11.1 0.0 copy-start
  11.1 1.1 %copy-done = bf16[3,4,256,256]{3,2,1,0:T(8,128)(2,1)} copy-done((bf16[3,4,256,256]{3,2,1,0:T(8,128)(2,1)}, bf16[3,4,256,256]{3,2,1,0:T(8,128)(2,1)S(1)}, u32[]{:S(2)}) %copy-start) | copy-done | bytes 1572888
  12.2 3.6 %collective-permute-start.2 = (bf16[2,512,512]{2,1,0:T(8,128)(2,1)}, bf16[2,512,512]{2,1,0:T(8,128)(2,1)}, u32[]{:S(2)}, u32[]{:S(2)}) collective-permute-start(bf16[2,512,512]{2,1,0:T(8,128)(2,1)} %get-tuple-element.12.refs_7_), channel_id=1, source_target_pairs={{1,2},{3,4},{5,6},{2,1},{4,3},{6,5},{9,10},{11,12},{13,14},{10,9},... | collective-permute-start | bytes 3145736 | tf_op jit(solution)/shard_map/ppermute | solution.py:322
  15.8 0.2 collective-permute-start.5
  16.1 0.0 copy-done.7
  16.1 0.1 copy.11
  16.2 0.1 reshape.3.refs_0_
  16.3 14.2 %collective-permute-done.1.refs_9_ = bf16[2,512,512]{2,1,0:T(8,128)(2,1)} collective-permute-done((bf16[2,512,512]{2,1,0:T(8,128)(2,1)S(1)}, bf16[2,512,512]{2,1,0:T(8,128)(2,1)}, u32[]{:S(2)}, u32[]{:S(2)}) %collective-permute-start.1) | collective-permute-done | bytes 1048608 | tf_op jit(solution)/shard_map/ppermute | solution.py:319
  30.5 0.0 collective-permute-done.refs_6_
  30.5 0.0 copy-done.4
  30.5 0.0 copy-done.5
  30.5 0.0 copy-done.6
  30.5 0.0 copy-start.1
  30.5 1.4 %copy-done.1 = bf16[3,4,256,256]{3,2,1,0:T(8,128)(2,1)S(1)} copy-done((bf16[3,4,256,256]{3,2,1,0:T(8,128)(2,1)S(1)}, bf16[3,4,256,256]{3,2,1,0:T(8,128)(2,1)}, u32[]{:S(2)}) %copy-start.1) | copy-done | bytes 1572888
  31.9 4.8 %message0.1.refs_1_ = bf16[4,512,256]{2,1,0:T(8,128)(2,1)} custom-call(s32[24]{0:T(128)S(1)} %reshape.3.refs_0_, s32[3]{0:T(128)S(1)} %copy-done.4, s32[3]{0:T(128)S(1)} %copy-done.5, f32[3]{0:T(128)S(1)} %copy-done.6, bf16[3,4,256,256]{3,2,1,0:T(8,128)(2,1)S(1)} %get-tuple-element.10.refs_4_, bf16[3,4,256,256]{3,2,1,0:T(8,128)(2,1)S(1)} %copy-done.1, ...), custom_call_target="tpu_custom_call" | custom-call | flops 1 | bytes 1 | tf_op jit(solution)/shard_map/message0/pallas_call | solution.py:300
  36.8 0.0 collective-permute-done.3.refs_0_
  36.8 0.0 collective-permute-start.4
  36.8 3.2 %collective-permute-start.7 = (bf16[2,512,512]{2,1,0:T(8,128)(2,1)}, bf16[2,512,512]{2,1,0:T(8,128)(2,1)}, u32[]{:S(2)}, u32[]{:S(2)}) collective-permute-start(bf16[2,512,512]{2,1,0:T(8,128)(2,1)} %after.2.refs_14_), channel_id=1, source_target_pairs={{1,2},{3,4},{5,6},{2,1},{4,3},{6,5},{9,10},{11,12},{13,14},{10,9},... | collective-permute-start | bytes 3145736 | tf_op jit(solution)/shard_map/ppermute | solution.py:329
  40.0 1.3 %collective-permute-start.8 = (bf16[4,512,256]{2,1,0:T(8,128)(2,1)}, bf16[4,512,256]{2,1,0:T(8,128)(2,1)}, u32[]{:S(2)}, u32[]{:S(2)}) collective-permute-start(bf16[4,512,256]{2,1,0:T(8,128)(2,1)} %message0.1.refs_1_), channel_id=1, source_target_pairs={{0,8},{8,16},{16,24},{24,0},{1,9},{9,17},{17,25},{25,1},{2,10},{10... | collective-permute-start | bytes 3145736 | tf_op jit(solution)/shard_map/ppermute | solution.py:327
  41.3 11.7 %collective-permute-done.2.refs_10_ = bf16[2,512,512]{2,1,0:T(8,128)(2,1)} collective-permute-done((bf16[2,512,512]{2,1,0:T(8,128)(2,1)}, bf16[2,512,512]{2,1,0:T(8,128)(2,1)}, u32[]{:S(2)}, u32[]{:S(2)}) %collective-permute-start.2) | collective-permute-done | bytes 1048608 | tf_op jit(solution)/shard_map/ppermute | solution.py:322
  53.0 4.1 %message1.1.refs_1_ = bf16[4,512,256]{2,1,0:T(8,128)(2,1)S(1)} custom-call(s32[24]{0:T(128)S(1)} %reshape.3.refs_0_, s32[3]{0:T(128)S(1)} %copy-done.4, s32[3]{0:T(128)S(1)} %copy-done.5, f32[3]{0:T(128)S(1)} %copy-done.6, bf16[3,4,256,256]{3,2,1,0:T(8,128)(2,1)S(1)} %get-tuple-element.10.refs_4_, bf16[3,4,256,256]{3,2,1,0:T(8,128)(2,1)S(1)} %copy-done.1, ...), custom_call_target="tpu_custom_call" | custom-call | flops 1 | bytes 1 | tf_op jit(solution)/shard_map/message1/pallas_call | solution.py:300
  57.1 0.0 collective-permute-done.5.refs_0_
  57.1 0.0 collective-permute-done.4.refs_2_.refs_11_
  57.1 0.0 copy-start.2
  57.1 0.1 collective-permute-start.6
  57.2 3.3 %collective-permute-start.9 = (bf16[2,512,512]{2,1,0:T(8,128)(2,1)}, bf16[2,512,512]{2,1,0:T(8,128)(2,1)S(1)}, u32[]{:S(2)}, u32[]{:S(2)}) collective-permute-start(bf16[2,512,512]{2,1,0:T(8,128)(2,1)} %after.3.refs_13_), channel_id=1, source_target_pairs={{1,2},{3,4},{5,6},{2,1},{4,3},{6,5},{9,10},{11,12},{13,14},{10,9},... | collective-permute-start | bytes 3145736 | tf_op jit(solution)/shard_map/ppermute | solution.py:335
  60.5 1.3 %collective-permute-start.10 = (bf16[4,512,256]{2,1,0:T(8,128)(2,1)S(1)}, bf16[4,512,256]{2,1,0:T(8,128)(2,1)S(1)}, u32[]{:S(2)}, u32[]{:S(2)}) collective-permute-start(bf16[4,512,256]{2,1,0:T(8,128)(2,1)S(1)} %message1.1.refs_1_), channel_id=1, source_target_pairs={{0,8},{8,16},{16,24},{24,0},{1,9},{9,17},{17,25},{25,1},{2,10},{10... | collective-permute-start | bytes 3145736 | tf_op jit(solution)/shard_map/ppermute | solution.py:333
  61.8 13.9 %collective-permute-done.7.refs_15_ = bf16[2,512,512]{2,1,0:T(8,128)(2,1)} collective-permute-done((bf16[2,512,512]{2,1,0:T(8,128)(2,1)}, bf16[2,512,512]{2,1,0:T(8,128)(2,1)}, u32[]{:S(2)}, u32[]{:S(2)}) %collective-permute-start.7) | collective-permute-done | bytes 1048608 | tf_op jit(solution)/shard_map/ppermute | solution.py:329
  75.7 1.8 %collective-permute-done.8.refs_16_.arrived = bf16[4,512,256]{2,1,0:T(8,128)(2,1)} collective-permute-done((bf16[4,512,256]{2,1,0:T(8,128)(2,1)}, bf16[4,512,256]{2,1,0:T(8,128)(2,1)}, u32[]{:S(2)}, u32[]{:S(2)}) %collective-permute-start.8) | collective-permute-done | bytes 1048608 | tf_op jit(solution)/shard_map/ppermute | solution.py:327
  77.5 0.0 collective-permute-done.6.refs_12_.refs_7_
  77.5 0.0 copy-done.2
  77.6 8.3 %first.1 = (f32[2,512,512]{2,1,0:T(8,128)S(1)}, f32[2,512,512]{2,1,0:T(8,128)S(1)}) custom-call(s32[24]{0:T(128)S(1)} %reshape.3.refs_0_, s32[3]{0:T(128)S(1)} %copy-done.4, s32[3]{0:T(128)S(1)} %copy-done.5, f32[3]{0:T(128)S(1)} %copy-done.6, bf16[3,4,256,256]{3,2,1,0:T(8,128)(2,1)S(1)} %get-tuple-element.10.refs_4_, ...), custom_call_target="tpu_custom_call" | custom-call | flops 1 | bytes 1 | tf_op jit(solution)/shard_map/first/pallas_call | solution.py:300
  85.9 2.6 %store0.1.refs_0_ = f32[1,2,2,512,512]{4,3,2,1,0:T(8,128)} custom-call(f32[2,512,512]{2,1,0:T(8,128)S(1)} %get-tuple-element.14.sum_ref, bf16[4,512,256]{2,1,0:T(8,128)(2,1)} %collective-permute-done.8.refs_16_.arrived), custom_call_target="tpu_custom_call" | custom-call | flops 1 | bytes 1 | tf_op jit(solution)/shard_map/store0/pallas_call | solution.py:270
  88.5 9.1 %collective-permute-done.9.refs_8_ = bf16[2,512,512]{2,1,0:T(8,128)(2,1)S(1)} collective-permute-done((bf16[2,512,512]{2,1,0:T(8,128)(2,1)}, bf16[2,512,512]{2,1,0:T(8,128)(2,1)S(1)}, u32[]{:S(2)}, u32[]{:S(2)}) %collective-permute-start.9) | collective-permute-done | bytes 1048608 | tf_op jit(solution)/shard_map/ppermute | solution.py:335
  97.7 2.1 %second.1.sum_ref = f32[2,512,512]{2,1,0:T(8,128)S(1)} custom-call(s32[24]{0:T(128)S(1)} %reshape.3.refs_0_, s32[3]{0:T(128)S(1)} %copy-done.4, s32[3]{0:T(128)S(1)} %copy-done.5, f32[3]{0:T(128)S(1)} %copy-done.6, bf16[3,4,256,256]{3,2,1,0:T(8,128)(2,1)S(1)} %get-tuple-element.10.refs_4_, bf16[3,4,256,256]{3,2,1,0:T(8,128)(2,1)S(1)} %copy-done.2, ...), custom_call_target="tpu_custom_call" | custom-call | flops 1 | bytes 1 | tf_op jit(solution)/shard_map/second/pallas_call | solution.py:300
  99.8 0.0 collective-permute-done.10.arrived
  99.8 1.4 %store1.1 = f32[1,2,2,512,512]{4,3,2,1,0:T(8,128)} custom-call(f32[2,512,512]{2,1,0:T(8,128)S(1)} %second.1.sum_ref, bf16[4,512,256]{2,1,0:T(8,128)(2,1)S(1)} %collective-permute-done.10.arrived, f32[1,2,2,512,512]{4,3,2,1,0:T(8,128)} %store0.1.refs_0_), custom_call_target="tpu_custom_call", output_to_operand_aliasing={{}: (2, {})} | custom-call | flops 1 | bytes 1 | tf_op jit(solution)/shard_map/store1/pallas_call | solution.py:270
  (2 shorter events, 0.0 us)
Async XLA Ops:
  0.0 8.7 %copy-start.3 = (f32[3,4,2,128,128]{4,3,2,1,0:T(8,128)S(1)}, f32[3,4,2,128,128]{4,3,2,1,0:T(8,128)}, u32[]{:S(2)}) copy-start(f32[3,4,2,128,128]{4,3,2,1,0:T(8,128)} %coupling_ref.1) | copy-start | bytes 4718596
  0.0 30.5 %collective-permute-start = (bf16[1,2,2,512,512]{4,3,2,1,0:T(8,128)(2,1)}, bf16[1,2,2,512,512]{4,3,2,1,0:T(8,128)(2,1)}, u32[]{:S(2)}, u32[]{:S(2)}) collective-permute-start(bf16[1,2,2,512,512]{4,3,2,1,0:T(8,128)(2,1)} %green_ref.3), channel_id=1, source_target_pairs={{0,1},{2,3},{4,5},{6,7},{1,0},{3,2},{5,4},{7,6},{8,9},{10,11},{12,... | collective-permute-start | bytes 6291464 | tf_op jit(solution)/shard_map/ppermute | solution.py:323
  2.0 14.0 %copy-start.7 = (s32[3,4,2]{1,2,0:T(2,128)S(1)}, s32[3,4,2]{1,2,0:T(2,128)}, u32[]{:S(2)}) copy-start(s32[3,4,2]{1,2,0:T(2,128)} %param.8) | copy-start | bytes 292
  2.0 28.5 %copy-start.4 = (s32[3]{0:T(128)S(1)}, s32[3]{0:T(128)}, u32[]{:S(2)}) copy-start(s32[3]{0:T(128)} %refs_1_.7) | copy-start | bytes 40
  2.1 28.5 %copy-start.5 = (s32[3]{0:T(128)S(1)}, s32[3]{0:T(128)}, u32[]{:S(2)}) copy-start(s32[3]{0:T(128)} %refs_2_.7) | copy-start | bytes 40
  2.1 28.4 %copy-start.6 = (f32[3]{0:T(128)S(1)}, f32[3]{0:T(128)}, u32[]{:S(2)}) copy-start(f32[3]{0:T(128)} %refs_3_.7) | copy-start | bytes 40
  2.1 28.4 %collective-permute-start.1 = (bf16[2,512,512]{2,1,0:T(8,128)(2,1)S(1)}, bf16[2,512,512]{2,1,0:T(8,128)(2,1)}, u32[]{:S(2)}, u32[]{:S(2)}) collective-permute-start(bf16[2,512,512]{2,1,0:T(8,128)(2,1)S(1)} %take.1._.refs_8_), channel_id=1, source_target_pairs={{1,2},{3,4},{5,6},{2,1},{4,3},{6,5},{9,10},{11,12},{13,14},{10,9},... | collective-permute-start | bytes 3145736 | tf_op jit(solution)/shard_map/ppermute | solution.py:319
  5.3 31.4 %collective-permute-start.3 = (bf16[2,512,512]{2,1,0:T(8,128)(2,1)S(1)}, bf16[2,512,512]{2,1,0:T(8,128)(2,1)}, u32[]{:S(2)}, u32[]{:S(2)}) collective-permute-start(bf16[2,512,512]{2,1,0:T(8,128)(2,1)S(1)} %take.1._.refs_8_), channel_id=1, source_target_pairs={{0,24},{8,0},{16,8},{24,16},{1,25},{9,1},{17,9},{25,17},{2,26},{10... | collective-permute-start | bytes 3145736 | tf_op jit(solution)/shard_map/ppermute | solution.py:318
  11.1 1.1 %copy-start = (bf16[3,4,256,256]{3,2,1,0:T(8,128)(2,1)}, bf16[3,4,256,256]{3,2,1,0:T(8,128)(2,1)S(1)}, u32[]{:S(2)}) copy-start(bf16[3,4,256,256]{3,2,1,0:T(8,128)(2,1)S(1)} %get-tuple-element.11.refs_5_) | copy-start | bytes 4718596
  12.2 40.8 %collective-permute-start.2 = (bf16[2,512,512]{2,1,0:T(8,128)(2,1)}, bf16[2,512,512]{2,1,0:T(8,128)(2,1)}, u32[]{:S(2)}, u32[]{:S(2)}) collective-permute-start(bf16[2,512,512]{2,1,0:T(8,128)(2,1)} %get-tuple-element.12.refs_7_), channel_id=1, source_target_pairs={{1,2},{3,4},{5,6},{2,1},{4,3},{6,5},{9,10},{11,12},{13,14},{10,9},... | collective-permute-start | bytes 3145736 | tf_op jit(solution)/shard_map/ppermute | solution.py:322
  15.8 41.3 %collective-permute-start.5 = (bf16[2,512,512]{2,1,0:T(8,128)(2,1)}, bf16[2,512,512]{2,1,0:T(8,128)(2,1)}, u32[]{:S(2)}, u32[]{:S(2)}) collective-permute-start(bf16[2,512,512]{2,1,0:T(8,128)(2,1)} %get-tuple-element.12.refs_7_), channel_id=1, source_target_pairs={{0,24},{8,0},{16,8},{24,16},{1,25},{9,1},{17,9},{25,17},{2,26},{10... | collective-permute-start | bytes 3145736 | tf_op jit(solution)/shard_map/ppermute | solution.py:321
  30.5 1.4 %copy-start.1 = (bf16[3,4,256,256]{3,2,1,0:T(8,128)(2,1)S(1)}, bf16[3,4,256,256]{3,2,1,0:T(8,128)(2,1)}, u32[]{:S(2)}) copy-start(bf16[3,4,256,256]{3,2,1,0:T(8,128)(2,1)} %copy-done) | copy-start | bytes 4718596
  36.8 20.3 %collective-permute-start.4 = (bf16[2,512,512]{2,1,0:T(8,128)(2,1)}, bf16[2,512,512]{2,1,0:T(8,128)(2,1)S(1)}, u32[]{:S(2)}, u32[]{:S(2)}) collective-permute-start(bf16[2,512,512]{2,1,0:T(8,128)(2,1)} %after.2.refs_14_), channel_id=1, source_target_pairs={{0,1},{2,3},{4,5},{6,7},{1,0},{3,2},{5,4},{7,6},{8,9},{10,11},{12,... | collective-permute-start | bytes 3145736 | tf_op jit(solution)/shard_map/ppermute | solution.py:330
  36.8 38.9 %collective-permute-start.7 = (bf16[2,512,512]{2,1,0:T(8,128)(2,1)}, bf16[2,512,512]{2,1,0:T(8,128)(2,1)}, u32[]{:S(2)}, u32[]{:S(2)}) collective-permute-start(bf16[2,512,512]{2,1,0:T(8,128)(2,1)} %after.2.refs_14_), channel_id=1, source_target_pairs={{1,2},{3,4},{5,6},{2,1},{4,3},{6,5},{9,10},{11,12},{13,14},{10,9},... | collective-permute-start | bytes 3145736 | tf_op jit(solution)/shard_map/ppermute | solution.py:329
  40.0 37.6 %collective-permute-start.8 = (bf16[4,512,256]{2,1,0:T(8,128)(2,1)}, bf16[4,512,256]{2,1,0:T(8,128)(2,1)}, u32[]{:S(2)}, u32[]{:S(2)}) collective-permute-start(bf16[4,512,256]{2,1,0:T(8,128)(2,1)} %message0.1.refs_1_), channel_id=1, source_target_pairs={{0,8},{8,16},{16,24},{24,0},{1,9},{9,17},{17,25},{25,1},{2,10},{10... | collective-permute-start | bytes 3145736 | tf_op jit(solution)/shard_map/ppermute | solution.py:327
  57.1 20.4 %copy-start.2 = (bf16[3,4,256,256]{3,2,1,0:T(8,128)(2,1)S(1)}, bf16[3,4,256,256]{3,2,1,0:T(8,128)(2,1)}, u32[]{:S(2)}) copy-start(bf16[3,4,256,256]{3,2,1,0:T(8,128)(2,1)} %copy-done) | copy-start | bytes 4718596
  57.1 20.4 %collective-permute-start.6 = (bf16[2,512,512]{2,1,0:T(8,128)(2,1)}, bf16[2,512,512]{2,1,0:T(8,128)(2,1)S(1)}, u32[]{:S(2)}, u32[]{:S(2)}) collective-permute-start(bf16[2,512,512]{2,1,0:T(8,128)(2,1)} %after.3.refs_13_), channel_id=1, source_target_pairs={{0,1},{2,3},{4,5},{6,7},{1,0},{3,2},{5,4},{7,6},{8,9},{10,11},{12,... | collective-permute-start | bytes 3145736 | tf_op jit(solution)/shard_map/ppermute | solution.py:336
  57.2 40.4 %collective-permute-start.9 = (bf16[2,512,512]{2,1,0:T(8,128)(2,1)}, bf16[2,512,512]{2,1,0:T(8,128)(2,1)S(1)}, u32[]{:S(2)}, u32[]{:S(2)}) collective-permute-start(bf16[2,512,512]{2,1,0:T(8,128)(2,1)} %after.3.refs_13_), channel_id=1, source_target_pairs={{1,2},{3,4},{5,6},{2,1},{4,3},{6,5},{9,10},{11,12},{13,14},{10,9},... | collective-permute-start | bytes 3145736 | tf_op jit(solution)/shard_map/ppermute | solution.py:335
  60.5 39.3 %collective-permute-start.10 = (bf16[4,512,256]{2,1,0:T(8,128)(2,1)S(1)}, bf16[4,512,256]{2,1,0:T(8,128)(2,1)S(1)}, u32[]{:S(2)}, u32[]{:S(2)}) collective-permute-start(bf16[4,512,256]{2,1,0:T(8,128)(2,1)S(1)} %message1.1.refs_1_), channel_id=1, source_target_pairs={{0,8},{8,16},{16,24},{24,0},{1,9},{9,17},{17,25},{25,1},{2,10},{10... | collective-permute-start | bytes 3145736 | tf_op jit(solution)/shard_map/ppermute | solution.py:333

commit v4 on v3

v4 whole, which is shorter than its diff:
```python
import functools
import math

import jax
import jax.numpy as jnp
from jax import lax
from jax.experimental import pallas as pl
from jax.experimental.pallas import tpu as pltpu
from jax.sharding import PartitionSpec as P

SMAX = 2
PIECES = 4
MIB = 1024 * 1024
SMALL = pltpu.CompilerParams(vmem_limit_bytes=6 * MIB)
LARGE = pltpu.CompilerParams(vmem_limit_bytes=24 * MIB)
ANY = pl.BlockSpec(memory_space=pl.ANY)
SMEM = pl.BlockSpec(memory_space=pltpu.SMEM)
VMEM = pl.BlockSpec(memory_space=pltpu.VMEM)
DEAR = pl.CostEstimate(flops=2 * 10**11, bytes_accessed=1, transcendentals=0)
CHEAP = pl.CostEstimate(flops=1, bytes_accessed=1, transcendentals=0)


def ring(count, step):
    return [(i, (i + step) % count) for i in range(count)]


def both_ways(pairs):
    return [*pairs, *[(j, i) for i, j in pairs]]


def in_vmem(x):
    return pltpu.with_memory_space_constraint(x, pltpu.VMEM)


def in_hbm(x):
    return pltpu.with_memory_space_constraint(x, pltpu.HBM)


def after(value, *earlier):
    return pl.pallas_call(
        lambda *refs: None,
        in_specs=[ANY] * (1 + len(earlier)),
        out_specs=ANY,
        out_shape=jax.ShapeDtypeStruct(value.shape, value.dtype),
        input_output_aliases={0: 0},
        compiler_params=SMALL,
        cost_estimate=DEAR,
        name="after",
    )(value, *earlier)


def odd():
    return lax.axis_index("en") % 2


def pieces_of(ref, count):
    rows = ref.shape[-2] // count
    return [(part, pl.ds(piece * rows, rows)) for part in range(2) for piece in range(count)]


def carry(green_ref, energy, out_ref, held, sems):
    places = pieces_of(held, PIECES)

    def copy(i, way):
        part, here = places[i]
        ends = (green_ref.at[0, energy, part, here, :], held.at[part, here, :], out_ref.at[part, here, :])
        return pltpu.make_async_copy(ends[way], ends[way + 1], sems.at[way, i])

    for i in range(len(places)):
        copy(i, 0).start()

    def finish():
        for i in range(len(places)):
            copy(i, 0).wait()
            copy(i, 1).start()
        for i in range(len(places)):
            copy(i, 1).wait()

    return finish


def carry_scratch(green):
    return [pltpu.VMEM(green.shape[2:], green.dtype), pltpu.SemaphoreType.DMA((2, 2 * PIECES))]


def take_kernel(green_ref, out_ref, sems):
    copies = []
    for i, (part, here) in enumerate(pieces_of(out_ref, PIECES)):
        copies.append(
            pltpu.make_async_copy(green_ref.at[0, odd(), part, here, :], out_ref.at[part, here, :], sems.at[i])
        )
        copies[-1].start()
    for copy in copies:
        copy.wait()


def take(green):
    return pl.pallas_call(
        take_kernel,
        in_specs=[ANY],
        out_specs=VMEM,
        out_shape=pltpu.VMEM(green.shape[2:], green.dtype),
        scratch_shapes=[pltpu.SemaphoreType.DMA((2 * PIECES,))],
        compiler_params=SMALL,
        cost_estimate=CHEAP,
        name="take",
    )(in_hbm(green))


def prepare_kernel(green_ref, coupling_ref, _, out_ref, left_ref, right_ref, held, sems):
    finish = carry(green_ref, 1 - odd(), out_ref, held, sems)
    transfers, listed, _, block, _ = coupling_ref.shape
    low, high = pl.ds(0, block), pl.ds(block, block)

    @pl.loop(0, transfers)
    def _(q):
        for n in range(listed):
            real, imag = coupling_ref[q, n, 0], coupling_ref[q, n, 1]
            for ref, a, b in ((left_ref, real, imag), (right_ref, real.T, imag.T)):
                ref[q, n, low, low] = a.astype(jnp.bfloat16)
                ref[q, n, low, high] = (-b).astype(jnp.bfloat16)
                ref[q, n, high, low] = b.astype(jnp.bfloat16)
                ref[q, n, high, high] = a.astype(jnp.bfloat16)

    finish()


def prepare(green, coupling, earlier):
    transfers, listed, _, block, _ = coupling.shape
    factor = pltpu.VMEM((transfers, listed, 2 * block, 2 * block), jnp.bfloat16)
    return pl.pallas_call(
        prepare_kernel,
        in_specs=[ANY, VMEM, ANY],
        out_specs=[ANY, VMEM, VMEM],
        out_shape=[jax.ShapeDtypeStruct(green.shape[2:], green.dtype), factor, factor],
        scratch_shapes=carry_scratch(green),
        compiler_params=SMALL,
        cost_estimate=CHEAP,
        name="prepare",
    )(in_hbm(green), coupling, earlier)


class Terms:
    def __init__(self, scalar_refs, factor_refs, scratch):
        self.lists, self.offsets, self.shifts, self.occupation = scalar_refs
        self.left, self.right = factor_refs
        self.half, self.held, self.sems = scratch
        self.transfers, self.listed = self.left.shape[0], self.left.shape[1]
        self.block = self.left.shape[2] // 2

    def entry(self, q, n, side):
        return self.lists[(q * self.listed + n) * 2 + side]

    def fetch(self, wanted, slot, pairs):
        for holds, *blocks in pairs:

            @pl.when(wanted & holds)
            def _():
                for i, ref in enumerate(blocks):
                    pltpu.make_async_copy(ref, self.held.at[slot, i], self.sems.at[slot, i]).start()

    def arrive(self, slot):
        for i in range(2):
            pltpu.make_async_copy(self.held.at[slot, i], self.held.at[slot, i], self.sems.at[slot, i]).wait()

    def mixed(self, q, slot, m):
        away = self.occupation[q] + jnp.where(odd() == 1, 0.0, 1.0)
        towards = self.occupation[q] + jnp.where(odd() == 1, 1.0, 0.0)
        here = pl.ds(pl.multiple_of(m * self.block, self.block), self.block)

        def part(p):
            a = self.held[slot, 0, p, here, :].astype(jnp.float32)
            b = self.held[slot, 1, p, here, :].astype(jnp.float32)
            return (away * a + towards * b).astype(jnp.bfloat16)

        return jnp.concatenate([part(0), part(1)], axis=0)

    def multiply(self, q, slot, emit):
        block = self.block
        for n in range(self.listed):
            rows = self.mixed(q, slot, self.entry(q, n, 1))
            product = jnp.dot(self.left[q, n], rows, preferred_element_type=jnp.float32).astype(jnp.bfloat16)
            target = pl.ds(pl.multiple_of(self.entry(q, n, 0) * block, block), block)
            for column in range(self.listed):
                for part in range(2):
                    self.half[column, target, pl.ds(part * block, block)] = product[
                        part * block : (part + 1) * block, column * block : (column + 1) * block
                    ]
        for n in range(self.listed):
            product = jnp.dot(self.half[self.entry(q, n, 1)], self.right[q, n], preferred_element_type=jnp.float32)
            emit(self.entry(q, n, 0), product)


def term_scratch(slots, coupling_shape, orbitals):
    _, listed, _, block, _ = coupling_shape
    return [
        pltpu.VMEM((listed, orbitals, 2 * block), jnp.bfloat16),
        pltpu.VMEM((slots, 2, 2, orbitals, orbitals), jnp.bfloat16),
        pltpu.SemaphoreType.DMA((slots, 2)),
    ]


def levels_of(chip_mate, *others):
    return (chip_mate.at[0, 1 - odd()], chip_mate.at[0, odd()], *others)


def at_row_end(row):
    place, count = lax.axis_index("en"), lax.axis_size("en")
    if count % row:
        return place < 0
    return (place % row == 0) | (place % row == row - 1)


def pairs_of(place, shift, levels, row=None):
    first, second = levels[place - shift + SMAX], levels[place + shift + SMAX]
    if row is None or place + shift != SMAX:
        return [(True, first, second)]
    return [(jnp.logical_not(at_row_end(row)), first, second), (at_row_end(row), first, levels[-1])]


def message_kernel(place, offset, row, *refs):
    terms = Terms(refs[:4], refs[4:6], refs[-3:])
    levels = levels_of(*refs[6:-5])
    message_ref, total = refs[-5:-3]
    for q in range(terms.transfers):
        for shift in range(1, SMAX + 1):
            wanted = (terms.offsets[q] == offset) & (terms.shifts[q] == shift)
            terms.fetch(wanted, q, pairs_of(place, shift, levels, row))
    total[...] = jnp.zeros_like(total)

    @pl.loop(0, terms.transfers)
    def _(q):
        @pl.when(terms.offsets[q] == offset)
        def _():
            def emit(column, product):
                total[column] += product

            terms.arrive(q)
            terms.multiply(q, q, emit)

    message_ref[...] = total[...].astype(jnp.bfloat16)


def add_to(total, place, block):
    def emit(column, product):
        columns = pl.ds(pl.multiple_of(column * block, block), block)
        for part in range(2):
            total[place, part, :, columns] += product[:, part * block : (part + 1) * block]

    return emit


def first_kernel(own_offset, near_offset, row, *refs):
    terms = Terms(refs[:4], refs[4:6], refs[-3:])
    own, near, totals = levels_of(*refs[6:12]), refs[12:17], refs[17]
    places = totals.shape[0]
    for q in range(terms.transfers):
        for place in range(places):
            for shift in range(1, SMAX + 1):
                slot, here = q * places + place, terms.shifts[q] == shift
                terms.fetch(here & (terms.offsets[q] == own_offset), slot, pairs_of(place, shift, own, row))
                if place + shift <= SMAX:
                    terms.fetch(here & (terms.offsets[q] == near_offset), slot, pairs_of(place, shift, near))
    totals[...] = jnp.zeros_like(totals)

    @pl.loop(0, terms.transfers * places)
    def _(slot):
        q = slot // places
        place = slot - q * places
        is_near = (terms.offsets[q] == near_offset) & (terms.shifts[q] + place <= SMAX)

        @pl.when((terms.offsets[q] == own_offset) | is_near)
        def _():
            terms.arrive(slot)
            terms.multiply(q, slot, add_to(totals, place, terms.block))


def second_kernel(near_offset, place, *refs):
    terms = Terms(refs[:4], refs[4:6], refs[-3:])
    first, second, sum_ref, total = refs[6:-3]

    def wanted(q):
        return (terms.offsets[q] == near_offset) & (terms.shifts[q] + place > SMAX)

    any_wanted = functools.reduce(jnp.logical_or, [wanted(q) for q in range(terms.transfers)])
    terms.fetch(any_wanted, 0, [(True, first, second)])
    total[0] = sum_ref[place]

    @pl.when(any_wanted)
    def _():
        terms.arrive(0)

    @pl.loop(0, terms.transfers)
    def _(q):
        @pl.when(wanted(q))
        def _():
            terms.multiply(q, 0, add_to(total, 0, terms.block))


def store_kernel(place, sum_ref, arrived_ref, *refs):
    out_ref, held, arrived, sems = refs[-4:]
    listed, orbitals, width = arrived.shape
    block = width // 2
    energy = odd() * place + (1 - odd()) * (1 - place)
    step = orbitals // sems.shape[1]
    rows = [pl.ds(piece * step, step) for piece in range(sems.shape[1])]

    def read(i):
        return pltpu.make_async_copy(arrived_ref.at[:, rows[i], :], arrived.at[:, rows[i], :], sems.at[0, i])

    def write(i):
        return pltpu.make_async_copy(held.at[:, rows[i], :], out_ref.at[0, energy, :, rows[i], :], sems.at[1, i])

    for i in range(len(rows)):
        read(i).start()
    for i, here in enumerate(rows):
        read(i).wait()
        for column in range(listed):
            columns = pl.ds(column * block, block)
            for part in range(2):
                held[part, here, columns] = sum_ref[0, part, here, columns] + arrived[
                    column, here, pl.ds(part * block, block)
                ].astype(jnp.float32)
        write(i).start()
    for i in range(len(rows)):
        write(i).wait()


def store(place, sums, arrived, result, *earlier):
    return pl.pallas_call(
        functools.partial(store_kernel, place),
        in_specs=[VMEM, ANY] + [ANY] * len(earlier),
        out_specs=ANY,
        out_shape=result,
        scratch_shapes=[
            pltpu.VMEM(result.shape[2:], jnp.float32),
            pltpu.VMEM(arrived.shape, arrived.dtype),
            pltpu.SemaphoreType.DMA((2, 2 * PIECES)),
        ],
        input_output_aliases={2: 0} if earlier else {},
        compiler_params=SMALL,
        cost_estimate=CHEAP,
        name="store%d" % place,
    )(in_vmem(sums), arrived, *earlier)


def on_device(green_lesser, coupling, block_list, offsets, shifts, occupation):
    _, energies, _, orbitals, _ = green_lesser.shape
    transfers, listed, _, block, _ = coupling.shape
    assert green_lesser.shape[0] == 1 and energies == SMAX
    momenta, ranks = lax.axis_size("kz"), lax.axis_size("en")
    forward, backward = ring(momenta, 1), ring(momenta, -1)
    scalar_args = (block_list.reshape(-1), offsets, shifts, occupation)
    result = jax.ShapeDtypeStruct(green_lesser.shape, jnp.float32)

    on_chip = both_ways([(i, i + 1) for i in range(0, ranks - 1, 2)])
    between = both_ways([(i, i + 1) for i in range(1, ranks - 1, 2)])
    row = 2 ** math.ceil(math.log2(ranks) / 2)
    turns = [i for i in range(row - 1, ranks - 1, row) if ranks % row == 0]
    across = [(i, j) for i, j in between if min(i, j) not in turns]
    across += [(i, i + row) for i in turns] + [(i + 1, i + 1 - row) for i in turns]
    arriving = [(i + row, i + 1) for i in turns] + [(i + 1 - row, i) for i in turns]

    def call(kernel, out_shape, slots, name, *operands, sums=(), scratch=()):
        return pl.pallas_call(
            kernel,
            in_specs=[SMEM] * 4 + [VMEM] * 2 + [ANY] * len(operands) + [VMEM] * len(sums),
            out_specs=VMEM,
            out_shape=out_shape,
            scratch_shapes=[*scratch, *term_scratch(slots, coupling.shape, orbitals)],
            compiler_params=LARGE,
            cost_estimate=CHEAP,
            name=name,
        )(*scalar_args, in_vmem(left), in_vmem(right), *operands, *[in_vmem(x) for x in sums])

    def message(place, *operands):
        total = pltpu.VMEM((listed, orbitals, 2 * block), jnp.float32)
        kernel = functools.partial(message_kernel, place, 1, row)
        return call(
            kernel,
            jax.ShapeDtypeStruct(total.shape, jnp.bfloat16),
            transfers,
            "message%d" % place,
            *operands,
            scratch=[total],
        )

    def sums_at(count):
        return pltpu.VMEM((count, *green_lesser.shape[2:]), jnp.float32)

    own1 = take(green_lesser)
    near1 = lax.ppermute(own1, "kz", backward)
    own2 = lax.ppermute(own1, "en", across)
    own0, left, right = prepare(green_lesser, coupling, own1)
    near0 = lax.ppermute(own0, "kz", backward)
    own3 = lax.ppermute(own0, "en", between)
    own_ = lax.ppermute(green_lesser, "en", on_chip)

    mate1 = lax.ppermute(near1, "en", on_chip)
    own_ = after(own_, near1)
    own2 = after(own2, near1)
    relayed2 = lax.ppermute(own2, "en", arriving)
    own = (own_, own0, own1, own2, own3, relayed2)
    sent0 = message(0, *own[:-2], relayed2)
    arrived0 = lax.ppermute(sent0, "kz", forward)
    near1 = after(near1, sent0, mate1)
    near2 = lax.ppermute(near1, "en", between)
    sent1 = message(1, *own)
    arrived1 = lax.ppermute(sent1, "kz", forward)
    near0 = after(near0, sent1, sent0, mate1)
    near3 = lax.ppermute(near0, "en", between)
    mate0 = lax.ppermute(near0, "en", on_chip)
    near2 = after(near2, arrived0)

    near = (mate1, mate0, near0, near1, near2)
    first = functools.partial(first_kernel, 0, -1, row)
    sums = call(first, sums_at(energies), transfers * energies, "first", *own, *near)
    partial = store(0, sums, arrived0, result)
    second = functools.partial(second_kernel, -1, 1)
    sums = call(second, sums_at(1), 1, "second", mate0, near3, sums=[sums])
    return store(1, sums, arrived1, result, partial)


def solution(mesh):
    placed = (P("kz", "en", None, None, None), P(), P(), P(), P(), P())
    return jax.shard_map(
        on_device,
        mesh=mesh,
        in_specs=placed,
        out_specs=P("kz", "en", None, None, None),
        check_vma=False,
    )
```

time: 102 us -> 100 us (0.980)
  waiting for transfers between devices: 50.8 us -> 46.9 us
  starting transfers between devices: 20.2 us -> 22.3 us
    ppermute x1, waiting for transfers between devices: 11.7 us -> 0.01 us  [on_device(): own3 = lax.ppermute(own0, 'en', between)]
    ppermute x1, waiting for transfers between devices: 0.01 us -> 10.6 us  [on_device(): near1 = lax.ppermute(own1, 'kz', backward)]
    ppermute x1, waiting for transfers between devices: 9.13 us -> 2.52 us  [on_device(): near3 = lax.ppermute(near0, 'en', between)]
    ppermute x1, waiting for transfers between devices: 1.81 us -> 5.74 us  [on_device(): arrived0 = lax.ppermute(sent0, 'kz', forward)]
    ppermute x1, starting transfers between devices: 0.01 us -> 3.05 us  [on_device(): mate1 = lax.ppermute(near1, 'en', on_chip)]
    ppermute x1, waiting for transfers between devices: 13.9 us -> 11.2 us  [on_device(): near2 = lax.ppermute(near1, 'en', between)]
    ppermute x1 -> x2, starting transfers between devices: 3.26 us -> 5.4 us  [the longest x1 4.12 us: on_device(): own2 = lax.ppermute(own1, 'en', across)]
    ppermute x1, waiting for transfers between devices: 0.01 us -> 2.06 us  [on_device(): arrived1 = lax.ppermute(sent1, 'kz', forward)]
  transfers between devices with their start and end apart: 11 -> 12, of which waited for: 5 -> 6; matrix products, arithmetic and copies ran while one was open for 0% -> 0% of each run, Pallas kernels for 25% -> 23%
where the time goes in v4:
time: 100 us; the launch traced here: 98.3 us
  waiting for transfers between devices  46.9 us (47%)
  Pallas kernels  26.8 us (27%)
  starting transfers between devices  22.3 us (22%)
  local copies, waits for them, and re-layouts  2.04 us (2%)
    pallas_call x4, Pallas kernels, call(): pl.pallas_call(kernel, in_specs=[SMEM] * 4 + [VMEM] * 2 + [ANY] * len(ope...  18.4 us
    ppermute x1, waiting for transfers between devices, on_device(): relayed2 = lax.ppermute(own2, 'en', arriving)  14.8 us
    ppermute x1, waiting for transfers between devices, on_device(): near2 = lax.ppermute(near1, 'en', between)  11.2 us
    ppermute x1, waiting for transfers between devices, on_device(): near1 = lax.ppermute(own1, 'kz', backward)  10.6 us
    ppermute x1, waiting for transfers between devices, on_device(): arrived0 = lax.ppermute(sent0, 'kz', forward)  5.74 us
    pallas_call x2, Pallas kernels, store(): pl.pallas_call(functools.partial(store_kernel, place), in_specs=[VMEM, AN...  4.88 us
    ppermute x1, starting transfers between devices, on_device(): own2 = lax.ppermute(own1, 'en', across)  4.12 us
    ppermute x1, starting transfers between devices, on_device(): near2 = lax.ppermute(near1, 'en', between)  4.07 us
  transfers between devices with their start and end apart: 12, of which 6 were waited for; matrix products, arithmetic and copies ran while one was open for 0% of the time, Pallas kernels for 23%

profile of v4, /device:TPU:3, one launch (start us, length us, event | category | flops | bytes accessed | tf_op | source)
XLA Modules:
  0.0 98.3 jit_solution(12358290845750377291)
XLA Ops:
  0.0 1.5 %take.1._.refs_8_ = bf16[2,512,512]{2,1,0:T(8,128)(2,1)S(1)} custom-call(bf16[1,2,2,512,512]{4,3,2,1,0:T(8,128)(2,1)} %green_ref.3), custom_call_target="tpu_custom_call" | custom-call | flops 1 | bytes 1 | tf_op jit(solution)/shard_map/take/pallas_call | solution.py:98
  1.5 0.0 copy-start.10
  1.5 3.4 %collective-permute-start.2 = (bf16[2,512,512]{2,1,0:T(8,128)(2,1)S(1)}, bf16[2,512,512]{2,1,0:T(8,128)(2,1)}, u32[]{:S(2)}, u32[]{:S(2)}) collective-permute-start(bf16[2,512,512]{2,1,0:T(8,128)(2,1)S(1)} %take.1._.refs_8_), channel_id=1, source_target_pairs={{0,24},{8,0},{16,8},{24,16},{1,25},{9,1},{17,9},{25,17},{2,26},{10... | collective-permute-start | bytes 3145736 | tf_op jit(solution)/shard_map/ppermute | solution.py:392
  4.9 4.1 %collective-permute-start.3 = (bf16[2,512,512]{2,1,0:T(8,128)(2,1)S(1)}, bf16[2,512,512]{2,1,0:T(8,128)(2,1)}, u32[]{:S(2)}, u32[]{:S(2)}) collective-permute-start(bf16[2,512,512]{2,1,0:T(8,128)(2,1)S(1)} %take.1._.refs_8_), channel_id=1, source_target_pairs={{1,2},{5,6},{2,1},{6,5},{3,7},{4,0},{9,10},{13,14},{10,9},{14,13},... | collective-permute-start | bytes 3145736 | tf_op jit(solution)/shard_map/ppermute | solution.py:393
  9.0 0.0 collective-permute-start.1
  9.0 0.0 copy-done.3
  9.0 2.1 %prepare.1 = (bf16[2,512,512]{2,1,0:T(8,128)(2,1)}, bf16[3,4,256,256]{3,2,1,0:T(8,128)(2,1)S(1)}, bf16[3,4,256,256]{3,2,1,0:T(8,128)(2,1)S(1)}) custom-call(bf16[1,2,2,512,512]{4,3,2,1,0:T(8,128)(2,1)} %green_ref.3, f32[3,4,2,128,128]{4,3,2,1,0:T(8,128)S(1)} %copy-done.3, bf16[2,512,512]{2,1,0:T(8,128)(2,1)S(1)} %take.1._.refs_8_), custom_call_target="tpu_custom_call" | custom-call | flops 1 | bytes 1 | tf_op jit(solution)/shard_map/prepare/pallas_call | solution.py:131
  11.1 0.0 copy-start
  11.1 1.1 %copy-done = bf16[3,4,256,256]{3,2,1,0:T(8,128)(2,1)} copy-done((bf16[3,4,256,256]{3,2,1,0:T(8,128)(2,1)}, bf16[3,4,256,256]{3,2,1,0:T(8,128)(2,1)S(1)}, u32[]{:S(2)}) %copy-start) | copy-done | bytes 1572888
  12.2 3.4 %collective-permute-start.4 = (bf16[2,512,512]{2,1,0:T(8,128)(2,1)}, bf16[2,512,512]{2,1,0:T(8,128)(2,1)}, u32[]{:S(2)}, u32[]{:S(2)}) collective-permute-start(bf16[2,512,512]{2,1,0:T(8,128)(2,1)} %get-tuple-element.10.refs_7_), channel_id=1, source_target_pairs={{1,2},{3,4},{5,6},{2,1},{4,3},{6,5},{9,10},{11,12},{13,14},{10,9},... | collective-permute-start | bytes 3145736 | tf_op jit(solution)/shard_map/ppermute | solution.py:396
  15.6 0.2 collective-permute-start
  15.9 0.0 copy-done.10
  15.9 0.1 copy.14
  16.0 0.1 reshape.3.refs_0_
  16.1 10.6 %collective-permute-done.2.refs_1_.refs_0_ = bf16[2,512,512]{2,1,0:T(8,128)(2,1)} collective-permute-done((bf16[2,512,512]{2,1,0:T(8,128)(2,1)S(1)}, bf16[2,512,512]{2,1,0:T(8,128)(2,1)}, u32[]{:S(2)}, u32[]{:S(2)}) %collective-permute-start.2) | collective-permute-done | bytes 1048608 | tf_op jit(solution)/shard_map/ppermute | solution.py:392
  26.7 0.0 collective-permute-done.3.refs_0_
  26.7 1.3 %collective-permute-start.5 = (bf16[2,512,512]{2,1,0:T(8,128)(2,1)}, bf16[2,512,512]{2,1,0:T(8,128)(2,1)}, u32[]{:S(2)}, u32[]{:S(2)}) collective-permute-start(bf16[2,512,512]{2,1,0:T(8,128)(2,1)} %after.6.refs_9_), channel_id=1, source_target_pairs={{7,4},{0,3},{15,12},{8,11},{23,20},{16,19},{31,28},{24,27}} | collective-permute-start | bytes 3145736 | tf_op jit(solution)/shard_map/ppermute | solution.py:402
  28.0 3.0 %collective-permute-start.6 = (bf16[2,512,512]{2,1,0:T(8,128)(2,1)}, bf16[2,512,512]{2,1,0:T(8,128)(2,1)}, u32[]{:S(2)}, u32[]{:S(2)}) collective-permute-start(bf16[2,512,512]{2,1,0:T(8,128)(2,1)} %collective-permute-done.2.refs_1_.refs_0_), channel_id=1, source_target_pairs={{0,1},{2,3},{4,5},{6,7},{1,0},{3,2},{5,4},{7,6},{8,9},{10,11},{12,... | collective-permute-start | bytes 3145736 | tf_op jit(solution)/shard_map/ppermute | solution.py:399
  31.0 0.0 collective-permute-done.1.refs_0_
  31.0 0.0 copy-start.8
  31.1 14.8 %collective-permute-done.5.refs_11_.refs_10_ = bf16[2,512,512]{2,1,0:T(8,128)(2,1)} collective-permute-done((bf16[2,512,512]{2,1,0:T(8,128)(2,1)}, bf16[2,512,512]{2,1,0:T(8,128)(2,1)}, u32[]{:S(2)}, u32[]{:S(2)}) %collective-permute-start.5) | collective-permute-done | bytes 1048608 | tf_op jit(solution)/shard_map/ppermute | solution.py:402
  45.8 0.0 copy-done.1
  45.8 0.0 copy-done.4
  45.9 0.0 copy-done.6
  45.9 0.0 copy-done.8
  45.9 4.4 %message0.1.refs_2_.refs_1_ = bf16[4,512,256]{2,1,0:T(8,128)(2,1)} custom-call(s32[24]{0:T(128)S(1)} %reshape.3.refs_0_, s32[3]{0:T(128)S(1)} %copy-done.4, s32[3]{0:T(128)S(1)} %copy-done.6, f32[3]{0:T(128)S(1)} %copy-done.8, bf16[3,4,256,256]{3,2,1,0:T(8,128)(2,1)S(1)} %get-tuple-element.8.refs_4_, bf16[3,4,256,256]{3,2,1,0:T(8,128)(2,1)S(1)} %copy-done.1, ...), custom_call_target="tpu_custom_call" | custom-call | flops 1 | bytes 1 | tf_op jit(solution)/shard_map/message0/pallas_call | solution.py:365
  50.3 0.1 collective-permute-start.10
  50.4 0.0 collective-permute-done.6.refs_3_.refs_2_.refs_12_
  50.4 4.1 %collective-permute-start.9 = (bf16[2,512,512]{2,1,0:T(8,128)(2,1)}, bf16[2,512,512]{2,1,0:T(8,128)(2,1)}, u32[]{:S(2)}, u32[]{:S(2)}) collective-permute-start(bf16[2,512,512]{2,1,0:T(8,128)(2,1)} %after.8.refs_15_), channel_id=1, source_target_pairs={{1,2},{3,4},{5,6},{2,1},{4,3},{6,5},{9,10},{11,12},{13,14},{10,9},... | collective-permute-start | bytes 3145736 | tf_op jit(solution)/shard_map/ppermute | solution.py:407
  54.5 0.0 collective-permute-done.4.refs_10_
  54.5 4.4 %message1.1.refs_1_ = bf16[4,512,256]{2,1,0:T(8,128)(2,1)} custom-call(s32[24]{0:T(128)S(1)} %reshape.3.refs_0_, s32[3]{0:T(128)S(1)} %copy-done.4, s32[3]{0:T(128)S(1)} %copy-done.6, f32[3]{0:T(128)S(1)} %copy-done.8, bf16[3,4,256,256]{3,2,1,0:T(8,128)(2,1)S(1)} %get-tuple-element.8.refs_4_, bf16[3,4,256,256]{3,2,1,0:T(8,128)(2,1)S(1)} %copy-done.1, ...), custom_call_target="tpu_custom_call" | custom-call | flops 1 | bytes 1 | tf_op jit(solution)/shard_map/message1/pallas_call | solution.py:365
  58.9 0.0 collective-permute-done.refs_0_
  59.0 0.1 collective-permute-start.7
  59.0 2.4 %collective-permute-start.8 = (bf16[2,512,512]{2,1,0:T(8,128)(2,1)}, bf16[2,512,512]{2,1,0:T(8,128)(2,1)}, u32[]{:S(2)}, u32[]{:S(2)}) collective-permute-start(bf16[2,512,512]{2,1,0:T(8,128)(2,1)} %after.7.refs_14_), channel_id=1, source_target_pairs={{1,2},{3,4},{5,6},{2,1},{4,3},{6,5},{9,10},{11,12},{13,14},{10,9},... | collective-permute-start | bytes 3145736 | tf_op jit(solution)/shard_map/ppermute | solution.py:411
  61.4 0.3 collective-permute-start.11
  61.7 11.2 %collective-permute-done.9.refs_0_ = bf16[2,512,512]{2,1,0:T(8,128)(2,1)} collective-permute-done((bf16[2,512,512]{2,1,0:T(8,128)(2,1)}, bf16[2,512,512]{2,1,0:T(8,128)(2,1)}, u32[]{:S(2)}, u32[]{:S(2)}) %collective-permute-start.9) | collective-permute-done | bytes 1048608 | tf_op jit(solution)/shard_map/ppermute | solution.py:407
  72.9 5.7 %collective-permute-done.10.refs_1_.arrived_ref = bf16[4,512,256]{2,1,0:T(8,128)(2,1)} collective-permute-done((bf16[4,512,256]{2,1,0:T(8,128)(2,1)}, bf16[4,512,256]{2,1,0:T(8,128)(2,1)}, u32[]{:S(2)}, u32[]{:S(2)}) %collective-permute-start.10) | collective-permute-done | bytes 1048608 | tf_op jit(solution)/shard_map/ppermute | solution.py:405
  78.6 0.0 collective-permute-done.7.refs_13_.refs_6_
  78.7 0.6 copy-done.5
  79.3 0.0 copy-done.7
  79.3 0.0 copy-done.9
  79.3 6.1 %first.1.refs_8_.sum_ref = f32[2,2,512,512]{3,2,1,0:T(8,128)S(1)} custom-call(s32[24]{0:T(128)S(1)} %reshape.3.refs_0_, s32[3]{0:T(128)S(1)} %copy-done.5, s32[3]{0:T(128)S(1)} %copy-done.7, f32[3]{0:T(128)S(1)} %copy-done.9, bf16[3,4,256,256]{3,2,1,0:T(8,128)(2,1)S(1)} %get-tuple-element.8.refs_4_, bf16[3,4,256,256]{3,2,1,0:T(8,128)(2,1)S(1)} %copy-done.1, ...), custom_call_target="tpu_custom_call" | custom-call | flops 1 | bytes 1 | tf_op jit(solution)/shard_map/first/pallas_call | solution.py:365
  85.5 0.0 copy-start.2
  85.5 2.5 %store0.1.refs_0_ = f32[1,2,2,512,512]{4,3,2,1,0:T(8,128)} custom-call(f32[2,2,512,512]{3,2,1,0:T(8,128)S(1)} %first.1.refs_8_.sum_ref, bf16[4,512,256]{2,1,0:T(8,128)(2,1)} %collective-permute-done.10.refs_1_.arrived_ref), custom_call_target="tpu_custom_call" | custom-call | flops 1 | bytes 1 | tf_op jit(solution)/shard_map/store0/pallas_call | solution.py:330
  88.0 2.5 %collective-permute-done.8.refs_7_ = bf16[2,512,512]{2,1,0:T(8,128)(2,1)} collective-permute-done((bf16[2,512,512]{2,1,0:T(8,128)(2,1)}, bf16[2,512,512]{2,1,0:T(8,128)(2,1)}, u32[]{:S(2)}, u32[]{:S(2)}) %collective-permute-start.8) | collective-permute-done | bytes 1048608 | tf_op jit(solution)/shard_map/ppermute | solution.py:411
  90.5 3.4 %second.1.sum_ref = f32[1,2,512,512]{3,2,1,0:T(8,128)S(1)} custom-call(s32[24]{0:T(128)S(1)} %reshape.3.refs_0_, s32[3]{0:T(128)S(1)} %copy-done.5, s32[3]{0:T(128)S(1)} %copy-done.7, f32[3]{0:T(128)S(1)} %copy-done.9, bf16[3,4,256,256]{3,2,1,0:T(8,128)(2,1)S(1)} %get-tuple-element.8.refs_4_, bf16[3,4,256,256]{3,2,1,0:T(8,128)(2,1)S(1)} %copy-done.2, ...), custom_call_target="tpu_custom_call" | custom-call | flops 1 | bytes 1 | tf_op jit(solution)/shard_map/second/pallas_call | solution.py:365
  93.9 2.1 %collective-permute-done.11.arrived_ref = bf16[4,512,256]{2,1,0:T(8,128)(2,1)} collective-permute-done((bf16[4,512,256]{2,1,0:T(8,128)(2,1)}, bf16[4,512,256]{2,1,0:T(8,128)(2,1)}, u32[]{:S(2)}, u32[]{:S(2)}) %collective-permute-start.11) | collective-permute-done | bytes 1048608 | tf_op jit(solution)/shard_map/ppermute | solution.py:409
  96.0 2.4 %store1.1 = f32[1,2,2,512,512]{4,3,2,1,0:T(8,128)} custom-call(f32[1,2,512,512]{3,2,1,0:T(8,128)S(1)} %second.1.sum_ref, bf16[4,512,256]{2,1,0:T(8,128)(2,1)} %collective-permute-done.11.arrived_ref, f32[1,2,2,512,512]{4,3,2,1,0:T(8,128)} %store0.1.refs_0_), custom_call_target="tpu_custom_call", output_to_operand_aliasing={{}: (2, {})} | custom-call | flops 1 | bytes 1 | tf_op jit(solution)/shard_map/store1/pallas_call | solution.py:330
  (13 shorter events, 0.0 us)
Async XLA Ops:
  0.0 9.0 %copy-start.3 = (f32[3,4,2,128,128]{4,3,2,1,0:T(8,128)S(1)}, f32[3,4,2,128,128]{4,3,2,1,0:T(8,128)}, u32[]{:S(2)}) copy-start(f32[3,4,2,128,128]{4,3,2,1,0:T(8,128)} %coupling_ref.1) | copy-start | bytes 4718596
  1.5 14.4 %copy-start.10 = (s32[3,4,2]{1,2,0:T(2,128)S(1)}, s32[3,4,2]{1,2,0:T(2,128)}, u32[]{:S(2)}) copy-start(s32[3,4,2]{1,2,0:T(2,128)} %param.8) | copy-start | bytes 292
  1.5 25.2 %collective-permute-start.2 = (bf16[2,512,512]{2,1,0:T(8,128)(2,1)S(1)}, bf16[2,512,512]{2,1,0:T(8,128)(2,1)}, u32[]{:S(2)}, u32[]{:S(2)}) collective-permute-start(bf16[2,512,512]{2,1,0:T(8,128)(2,1)S(1)} %take.1._.refs_8_), channel_id=1, source_target_pairs={{0,24},{8,0},{16,8},{24,16},{1,25},{9,1},{17,9},{25,17},{2,26},{10... | collective-permute-start | bytes 3145736 | tf_op jit(solution)/shard_map/ppermute | solution.py:392
  4.9 21.8 %collective-permute-start.3 = (bf16[2,512,512]{2,1,0:T(8,128)(2,1)S(1)}, bf16[2,512,512]{2,1,0:T(8,128)(2,1)}, u32[]{:S(2)}, u32[]{:S(2)}) collective-permute-start(bf16[2,512,512]{2,1,0:T(8,128)(2,1)S(1)} %take.1._.refs_8_), channel_id=1, source_target_pairs={{1,2},{5,6},{2,1},{6,5},{3,7},{4,0},{9,10},{13,14},{10,9},{14,13},... | collective-permute-start | bytes 3145736 | tf_op jit(solution)/shard_map/ppermute | solution.py:393
  9.0 22.0 %collective-permute-start.1 = (bf16[1,2,2,512,512]{4,3,2,1,0:T(8,128)(2,1)}, bf16[1,2,2,512,512]{4,3,2,1,0:T(8,128)(2,1)}, u32[]{:S(2)}, u32[]{:S(2)}) collective-permute-start(bf16[1,2,2,512,512]{4,3,2,1,0:T(8,128)(2,1)} %green_ref.3), channel_id=1, source_target_pairs={{0,1},{2,3},{4,5},{6,7},{1,0},{3,2},{5,4},{7,6},{8,9},{10,11},{12,... | collective-permute-start | bytes 6291464 | tf_op jit(solution)/shard_map/ppermute | solution.py:397
  11.1 1.1 %copy-start = (bf16[3,4,256,256]{3,2,1,0:T(8,128)(2,1)}, bf16[3,4,256,256]{3,2,1,0:T(8,128)(2,1)S(1)}, u32[]{:S(2)}) copy-start(bf16[3,4,256,256]{3,2,1,0:T(8,128)(2,1)S(1)} %get-tuple-element.9.refs_5_) | copy-start | bytes 4718596
  12.2 42.2 %collective-permute-start.4 = (bf16[2,512,512]{2,1,0:T(8,128)(2,1)}, bf16[2,512,512]{2,1,0:T(8,128)(2,1)}, u32[]{:S(2)}, u32[]{:S(2)}) collective-permute-start(bf16[2,512,512]{2,1,0:T(8,128)(2,1)} %get-tuple-element.10.refs_7_), channel_id=1, source_target_pairs={{1,2},{3,4},{5,6},{2,1},{4,3},{6,5},{9,10},{11,12},{13,14},{10,9},... | collective-permute-start | bytes 3145736 | tf_op jit(solution)/shard_map/ppermute | solution.py:396
  15.6 43.3 %collective-permute-start = (bf16[2,512,512]{2,1,0:T(8,128)(2,1)}, bf16[2,512,512]{2,1,0:T(8,128)(2,1)}, u32[]{:S(2)}, u32[]{:S(2)}) collective-permute-start(bf16[2,512,512]{2,1,0:T(8,128)(2,1)} %get-tuple-element.10.refs_7_), channel_id=1, source_target_pairs={{0,24},{8,0},{16,8},{24,16},{1,25},{9,1},{17,9},{25,17},{2,26},{10... | collective-permute-start | bytes 3145736 | tf_op jit(solution)/shard_map/ppermute | solution.py:395
  26.7 19.2 %collective-permute-start.5 = (bf16[2,512,512]{2,1,0:T(8,128)(2,1)}, bf16[2,512,512]{2,1,0:T(8,128)(2,1)}, u32[]{:S(2)}, u32[]{:S(2)}) collective-permute-start(bf16[2,512,512]{2,1,0:T(8,128)(2,1)} %after.6.refs_9_), channel_id=1, source_target_pairs={{7,4},{0,3},{15,12},{8,11},{23,20},{16,19},{31,28},{24,27}} | collective-permute-start | bytes 3145736 | tf_op jit(solution)/shard_map/ppermute | solution.py:402
  28.0 22.4 %collective-permute-start.6 = (bf16[2,512,512]{2,1,0:T(8,128)(2,1)}, bf16[2,512,512]{2,1,0:T(8,128)(2,1)}, u32[]{:S(2)}, u32[]{:S(2)}) collective-permute-start(bf16[2,512,512]{2,1,0:T(8,128)(2,1)} %collective-permute-done.2.refs_1_.refs_0_), channel_id=1, source_target_pairs={{0,1},{2,3},{4,5},{6,7},{1,0},{3,2},{5,4},{7,6},{8,9},{10,11},{12,... | collective-permute-start | bytes 3145736 | tf_op jit(solution)/shard_map/ppermute | solution.py:399
  31.0 14.8 %copy-start.1 = (bf16[3,4,256,256]{3,2,1,0:T(8,128)(2,1)S(1)}, bf16[3,4,256,256]{3,2,1,0:T(8,128)(2,1)}, u32[]{:S(2)}) copy-start(bf16[3,4,256,256]{3,2,1,0:T(8,128)(2,1)} %copy-done) | copy-start | bytes 4718596
  31.0 14.8 %copy-start.4 = (s32[3]{0:T(128)S(1)}, s32[3]{0:T(128)}, u32[]{:S(2)}) copy-start(s32[3]{0:T(128)} %refs_1_.7) | copy-start | bytes 40
  31.0 14.8 %copy-start.6 = (s32[3]{0:T(128)S(1)}, s32[3]{0:T(128)}, u32[]{:S(2)}) copy-start(s32[3]{0:T(128)} %refs_2_.7) | copy-start | bytes 40
  31.0 14.8 %copy-start.8 = (f32[3]{0:T(128)S(1)}, f32[3]{0:T(128)}, u32[]{:S(2)}) copy-start(f32[3]{0:T(128)} %refs_3_.7) | copy-start | bytes 40
  50.3 28.3 %collective-permute-start.10 = (bf16[4,512,256]{2,1,0:T(8,128)(2,1)}, bf16[4,512,256]{2,1,0:T(8,128)(2,1)}, u32[]{:S(2)}, u32[]{:S(2)}) collective-permute-start(bf16[4,512,256]{2,1,0:T(8,128)(2,1)} %message0.1.refs_2_.refs_1_), channel_id=1, source_target_pairs={{0,8},{8,16},{16,24},{24,0},{1,9},{9,17},{17,25},{25,1},{2,10},{10... | collective-permute-start | bytes 3145736 | tf_op jit(solution)/shard_map/ppermute | solution.py:405
  50.4 22.5 %collective-permute-start.9 = (bf16[2,512,512]{2,1,0:T(8,128)(2,1)}, bf16[2,512,512]{2,1,0:T(8,128)(2,1)}, u32[]{:S(2)}, u32[]{:S(2)}) collective-permute-start(bf16[2,512,512]{2,1,0:T(8,128)(2,1)} %after.8.refs_15_), channel_id=1, source_target_pairs={{1,2},{3,4},{5,6},{2,1},{4,3},{6,5},{9,10},{11,12},{13,14},{10,9},... | collective-permute-start | bytes 3145736 | tf_op jit(solution)/shard_map/ppermute | solution.py:407
  59.0 19.7 %collective-permute-start.7 = (bf16[2,512,512]{2,1,0:T(8,128)(2,1)}, bf16[2,512,512]{2,1,0:T(8,128)(2,1)}, u32[]{:S(2)}, u32[]{:S(2)}) collective-permute-start(bf16[2,512,512]{2,1,0:T(8,128)(2,1)} %after.7.refs_14_), channel_id=1, source_target_pairs={{0,1},{2,3},{4,5},{6,7},{1,0},{3,2},{5,4},{7,6},{8,9},{10,11},{12,... | collective-permute-start | bytes 3145736 | tf_op jit(solution)/shard_map/ppermute | solution.py:412
  59.0 31.5 %collective-permute-start.8 = (bf16[2,512,512]{2,1,0:T(8,128)(2,1)}, bf16[2,512,512]{2,1,0:T(8,128)(2,1)}, u32[]{:S(2)}, u32[]{:S(2)}) collective-permute-start(bf16[2,512,512]{2,1,0:T(8,128)(2,1)} %after.7.refs_14_), channel_id=1, source_target_pairs={{1,2},{3,4},{5,6},{2,1},{4,3},{6,5},{9,10},{11,12},{13,14},{10,9},... | collective-permute-start | bytes 3145736 | tf_op jit(solution)/shard_map/ppermute | solution.py:411
  61.4 34.5 %collective-permute-start.11 = (bf16[4,512,256]{2,1,0:T(8,128)(2,1)}, bf16[4,512,256]{2,1,0:T(8,128)(2,1)}, u32[]{:S(2)}, u32[]{:S(2)}) collective-permute-start(bf16[4,512,256]{2,1,0:T(8,128)(2,1)} %message1.1.refs_1_), channel_id=1, source_target_pairs={{0,8},{8,16},{16,24},{24,0},{1,9},{9,17},{17,25},{25,1},{2,10},{10... | collective-permute-start | bytes 3145736 | tf_op jit(solution)/shard_map/ppermute | solution.py:409
  78.6 0.7 copy-start.5
  78.6 0.7 copy-start.7
  78.6 0.7 copy-start.9
  85.5 5.0 %copy-start.2 = (bf16[3,4,256,256]{3,2,1,0:T(8,128)(2,1)S(1)}, bf16[3,4,256,256]{3,2,1,0:T(8,128)(2,1)}, u32[]{:S(2)}) copy-start(bf16[3,4,256,256]{3,2,1,0:T(8,128)(2,1)} %copy-done) | copy-start | bytes 4718596

commit v5 on v4

--- a/solution.py
+++ b/solution.py
@@ -36,7 +36,7 @@
     return pltpu.with_memory_space_constraint(x, pltpu.HBM)
 
 
-def after(value, *earlier):
+def after(value, *earlier, cost=DEAR):
     return pl.pallas_call(
         lambda *refs: None,
         in_specs=[ANY] * (1 + len(earlier)),
@@ -44,7 +44,7 @@
         out_shape=jax.ShapeDtypeStruct(value.shape, value.dtype),
         input_output_aliases={0: 0},
         compiler_params=SMALL,
-        cost_estimate=DEAR,
+        cost_estimate=cost,
         name="after",
     )(value, *earlier)
 
@@ -297,51 +297,41 @@
             terms.multiply(q, 0, add_to(total, 0, terms.block))
 
 
-def store_kernel(place, sum_ref, arrived_ref, *refs):
-    out_ref, held, arrived, sems = refs[-4:]
+def store_kernel(place, sum_ref, arrived, *refs):
+    out_ref, held, sems = refs[-3:]
     listed, orbitals, width = arrived.shape
     block = width // 2
     energy = odd() * place + (1 - odd()) * (1 - place)
-    step = orbitals // sems.shape[1]
-    rows = [pl.ds(piece * step, step) for piece in range(sems.shape[1])]
-
-    def read(i):
-        return pltpu.make_async_copy(arrived_ref.at[:, rows[i], :], arrived.at[:, rows[i], :], sems.at[0, i])
-
-    def write(i):
-        return pltpu.make_async_copy(held.at[:, rows[i], :], out_ref.at[0, energy, :, rows[i], :], sems.at[1, i])
-
-    for i in range(len(rows)):
-        read(i).start()
-    for i, here in enumerate(rows):
-        read(i).wait()
+    copies = []
+    for piece in range(orbitals // block):
+        rows = pl.ds(piece * block, block)
         for column in range(listed):
             columns = pl.ds(column * block, block)
             for part in range(2):
-                held[part, here, columns] = sum_ref[0, part, here, columns] + arrived[
-                    column, here, pl.ds(part * block, block)
+                held[part, rows, columns] = sum_ref[0, part, rows, columns] + arrived[
+                    column, rows, pl.ds(part * block, block)
                 ].astype(jnp.float32)
-        write(i).start()
-    for i in range(len(rows)):
-        write(i).wait()
+        copies.append(pltpu.make_async_copy(held.at[:, rows, :], out_ref.at[0, energy, :, rows, :], sems.at[piece]))
+        copies[-1].start()
+    for copy in copies:
+        copy.wait()
 
 
 def store(place, sums, arrived, result, *earlier):
     return pl.pallas_call(
         functools.partial(store_kernel, place),
-        in_specs=[VMEM, ANY] + [ANY] * len(earlier),
+        in_specs=[VMEM, VMEM] + [ANY] * len(earlier),
         out_specs=ANY,
         out_shape=result,
         scratch_shapes=[
             pltpu.VMEM(result.shape[2:], jnp.float32),
-            pltpu.VMEM(arrived.shape, arrived.dtype),
-            pltpu.SemaphoreType.DMA((2, 2 * PIECES)),
+            pltpu.SemaphoreType.DMA((2 * arrived.shape[1] // arrived.shape[2],)),
         ],
         input_output_aliases={2: 0} if earlier else {},
         compiler_params=SMALL,
         cost_estimate=CHEAP,
         name="store%d" % place,
-    )(in_vmem(sums), arrived, *earlier)
+    )(in_vmem(sums), in_vmem(arrived), *earlier)
 
 
 def on_device(green_lesser, coupling, block_list, offsets, shifts, occupation):
@@ -378,7 +368,7 @@
         kernel = functools.partial(message_kernel, place, 1, row)
         return call(
             kernel,
-            jax.ShapeDtypeStruct(total.shape, jnp.bfloat16),
+            pltpu.VMEM(total.shape, jnp.bfloat16),
             transfers,
             "message%d" % place,
             *operands,
@@ -403,14 +393,14 @@
     own = (own_, own0, own1, own2, own3, relayed2)
     sent0 = message(0, *own[:-2], relayed2)
     arrived0 = lax.ppermute(sent0, "kz", forward)
-    near1 = after(near1, sent0, mate1)
+    near1 = after(near1, sent0, mate1, cost=CHEAP)
     near2 = lax.ppermute(near1, "en", between)
     sent1 = message(1, *own)
     arrived1 = lax.ppermute(sent1, "kz", forward)
-    near0 = after(near0, sent1, sent0, mate1)
+    near0 = after(near0, sent1, sent0, mate1, cost=CHEAP)
     near3 = lax.ppermute(near0, "en", between)
     mate0 = lax.ppermute(near0, "en", on_chip)
-    near2 = after(near2, arrived0)
+    near2 = after(near2, arrived0, cost=CHEAP)
 
     near = (mate1, mate0, near0, near1, near2)
     first = functools.partial(first_kernel, 0, -1, row)

time: 100 us -> 99.1 us (level)
  Pallas kernels: 26.8 us -> 21.3 us
  waiting for transfers between devices: 46.9 us -> 52.3 us
    pallas_call x4, Pallas kernels: 18.4 us -> 14.9 us  [call(): pl.pallas_call(kernel, in_specs=[SMEM] * 4 + [VMEM] * 2 + [ANY] * len(ope...]
    ppermute x1, waiting for transfers between devices: 11.2 us -> 13.3 us  [on_device(): near2 = lax.ppermute(near1, 'en', between)]
    pallas_call x2, Pallas kernels: 4.88 us -> 2.82 us  [store(): pl.pallas_call(functools.partial(store_kernel, place), in_specs=[VMEM, VM...]
    ppermute x1, waiting for transfers between devices: 2.52 us -> 4.47 us  [on_device(): near3 = lax.ppermute(near0, 'en', between)]
    ppermute x1, waiting for transfers between devices: 2.06 us -> 3.33 us  [on_device(): arrived1 = lax.ppermute(sent1, 'kz', forward)]
    ppermute x1, waiting for transfers between devices: 14.8 us -> 16 us  [on_device(): relayed2 = lax.ppermute(own2, 'en', arriving)]
    ppermute x1, waiting for transfers between devices: 5.74 us -> 4.53 us  [on_device(): arrived0 = lax.ppermute(sent0, 'kz', forward)]
  transfers between devices with their start and end apart: 12 -> 12, of which waited for: 6 -> 6; matrix products, arithmetic and copies ran while one was open for 0% -> 0% of each run, Pallas kernels for 23% -> 19%
where the time goes in v5:
time: 99.1 us; the launch traced here: 97.3 us
  waiting for transfers between devices  52.3 us (53%)
  starting transfers between devices  22.1 us (22%)
  Pallas kernels  21.3 us (21%)
  local copies, waits for them, and re-layouts  1.36 us (1%)
    ppermute x1, waiting for transfers between devices, on_device(): relayed2 = lax.ppermute(own2, 'en', arriving)  16 us
    pallas_call x4, Pallas kernels, call(): pl.pallas_call(kernel, in_specs=[SMEM] * 4 + [VMEM] * 2 + [ANY] * len(ope...  14.9 us
    ppermute x1, waiting for transfers between devices, on_device(): near2 = lax.ppermute(near1, 'en', between)  13.3 us
    ppermute x1, waiting for transfers between devices, on_device(): near1 = lax.ppermute(own1, 'kz', backward)  10.6 us
    ppermute x1, waiting for transfers between devices, on_device(): arrived0 = lax.ppermute(sent0, 'kz', forward)  4.53 us
    ppermute x1, waiting for transfers between devices, on_device(): near3 = lax.ppermute(near0, 'en', between)  4.47 us
    ppermute x1, starting transfers between devices, on_device(): own2 = lax.ppermute(own1, 'en', across)  4.2 us
    ppermute x1, starting transfers between devices, on_device(): near2 = lax.ppermute(near1, 'en', between)  4.09 us
  transfers between devices with their start and end apart: 12, of which 6 were waited for; matrix products, arithmetic and copies ran while one was open for 0% of the time, Pallas kernels for 19%

profile of v5, /device:TPU:3, one launch (start us, length us, event | category | flops | bytes accessed | tf_op | source)
XLA Modules:
  0.0 97.3 jit_solution(4280826039838599066)
XLA Ops:
  0.0 0.0 copy-start.2
  0.0 1.5 %take.1._.refs_8_ = bf16[2,512,512]{2,1,0:T(8,128)(2,1)S(1)} custom-call(bf16[1,2,2,512,512]{4,3,2,1,0:T(8,128)(2,1)} %green_ref.3), custom_call_target="tpu_custom_call" | custom-call | flops 1 | bytes 1 | tf_op jit(solution)/shard_map/take/pallas_call | solution.py:98
  1.5 0.0 copy-start.6
  1.5 3.4 %collective-permute-start.2 = (bf16[2,512,512]{2,1,0:T(8,128)(2,1)S(1)}, bf16[2,512,512]{2,1,0:T(8,128)(2,1)}, u32[]{:S(2)}, u32[]{:S(2)}) collective-permute-start(bf16[2,512,512]{2,1,0:T(8,128)(2,1)S(1)} %take.1._.refs_8_), channel_id=1, source_target_pairs={{0,24},{8,0},{16,8},{24,16},{1,25},{9,1},{17,9},{25,17},{2,26},{10... | collective-permute-start | bytes 3145736 | tf_op jit(solution)/shard_map/ppermute | solution.py:382
  4.9 4.2 %collective-permute-start.3 = (bf16[2,512,512]{2,1,0:T(8,128)(2,1)S(1)}, bf16[2,512,512]{2,1,0:T(8,128)(2,1)}, u32[]{:S(2)}, u32[]{:S(2)}) collective-permute-start(bf16[2,512,512]{2,1,0:T(8,128)(2,1)S(1)} %take.1._.refs_8_), channel_id=1, source_target_pairs={{1,2},{5,6},{2,1},{6,5},{3,7},{4,0},{9,10},{13,14},{10,9},{14,13},... | collective-permute-start | bytes 3145736 | tf_op jit(solution)/shard_map/ppermute | solution.py:383
  9.1 0.0 collective-permute-start.1
  9.1 0.0 copy-done.2
  9.1 2.1 %prepare.1 = (bf16[2,512,512]{2,1,0:T(8,128)(2,1)}, bf16[3,4,256,256]{3,2,1,0:T(8,128)(2,1)S(1)}, bf16[3,4,256,256]{3,2,1,0:T(8,128)(2,1)S(1)}) custom-call(bf16[1,2,2,512,512]{4,3,2,1,0:T(8,128)(2,1)} %green_ref.3, f32[3,4,2,128,128]{4,3,2,1,0:T(8,128)S(1)} %copy-done.2, bf16[2,512,512]{2,1,0:T(8,128)(2,1)S(1)} %take.1._.refs_8_), custom_call_target="tpu_custom_call" | custom-call | flops 1 | bytes 1 | tf_op jit(solution)/shard_map/prepare/pallas_call | solution.py:131
  11.2 0.0 copy-start
  11.2 1.1 %copy-done = bf16[3,4,256,256]{3,2,1,0:T(8,128)(2,1)} copy-done((bf16[3,4,256,256]{3,2,1,0:T(8,128)(2,1)}, bf16[3,4,256,256]{3,2,1,0:T(8,128)(2,1)S(1)}, u32[]{:S(2)}) %copy-start) | copy-done | bytes 1572888
  12.3 3.3 %collective-permute-start.4 = (bf16[2,512,512]{2,1,0:T(8,128)(2,1)}, bf16[2,512,512]{2,1,0:T(8,128)(2,1)}, u32[]{:S(2)}, u32[]{:S(2)}) collective-permute-start(bf16[2,512,512]{2,1,0:T(8,128)(2,1)} %get-tuple-element.10.refs_7_), channel_id=1, source_target_pairs={{1,2},{3,4},{5,6},{2,1},{4,3},{6,5},{9,10},{11,12},{13,14},{10,9},... | collective-permute-start | bytes 3145736 | tf_op jit(solution)/shard_map/ppermute | solution.py:386
  15.6 0.2 collective-permute-start
  15.9 0.0 copy-done.6
  15.9 0.1 copy.14
  16.0 0.1 reshape.3.refs_0_
  16.1 10.6 %collective-permute-done.2.refs_1_.refs_0_ = bf16[2,512,512]{2,1,0:T(8,128)(2,1)} collective-permute-done((bf16[2,512,512]{2,1,0:T(8,128)(2,1)S(1)}, bf16[2,512,512]{2,1,0:T(8,128)(2,1)}, u32[]{:S(2)}, u32[]{:S(2)}) %collective-permute-start.2) | collective-permute-done | bytes 1048608 | tf_op jit(solution)/shard_map/ppermute | solution.py:382
  26.7 0.0 collective-permute-done.3.refs_0_
  26.7 1.3 %collective-permute-start.5 = (bf16[2,512,512]{2,1,0:T(8,128)(2,1)}, bf16[2,512,512]{2,1,0:T(8,128)(2,1)}, u32[]{:S(2)}, u32[]{:S(2)}) collective-permute-start(bf16[2,512,512]{2,1,0:T(8,128)(2,1)} %after.6.refs_9_), channel_id=1, source_target_pairs={{7,4},{0,3},{15,12},{8,11},{23,20},{16,19},{31,28},{24,27}} | collective-permute-start | bytes 3145736 | tf_op jit(solution)/shard_map/ppermute | solution.py:392
  28.0 3.1 %collective-permute-start.6 = (bf16[2,512,512]{2,1,0:T(8,128)(2,1)}, bf16[2,512,512]{2,1,0:T(8,128)(2,1)}, u32[]{:S(2)}, u32[]{:S(2)}) collective-permute-start(bf16[2,512,512]{2,1,0:T(8,128)(2,1)} %collective-permute-done.2.refs_1_.refs_0_), channel_id=1, source_target_pairs={{0,1},{2,3},{4,5},{6,7},{1,0},{3,2},{5,4},{7,6},{8,9},{10,11},{12,... | collective-permute-start | bytes 3145736 | tf_op jit(solution)/shard_map/ppermute | solution.py:389
  31.0 0.0 collective-permute-done.1.refs_0_
  31.1 0.0 copy-start.1
  31.1 0.0 copy-start.3
  31.1 0.0 copy-start.4
  31.1 0.0 copy-start.5
  31.1 16.0 %collective-permute-done.5.refs_11_.refs_10_ = bf16[2,512,512]{2,1,0:T(8,128)(2,1)} collective-permute-done((bf16[2,512,512]{2,1,0:T(8,128)(2,1)}, bf16[2,512,512]{2,1,0:T(8,128)(2,1)}, u32[]{:S(2)}, u32[]{:S(2)}) %collective-permute-start.5) | collective-permute-done | bytes 1048608 | tf_op jit(solution)/shard_map/ppermute | solution.py:392
  47.1 0.0 copy-done.1
  47.1 0.0 copy-done.3
  47.1 0.0 copy-done.4
  47.1 0.0 copy-done.5
  47.1 3.1 %message0.1.refs_2_.refs_1_ = bf16[4,512,256]{2,1,0:T(8,128)(2,1)S(1)} custom-call(s32[24]{0:T(128)S(1)} %reshape.3.refs_0_, s32[3]{0:T(128)S(1)} %copy-done.3, s32[3]{0:T(128)S(1)} %copy-done.4, f32[3]{0:T(128)S(1)} %copy-done.5, bf16[3,4,256,256]{3,2,1,0:T(8,128)(2,1)S(1)} %get-tuple-element.8.refs_4_, bf16[3,4,256,256]{3,2,1,0:T(8,128)(2,1)S(1)} %copy-done.1, ...), custom_call_target="tpu_custom_call" | custom-call | flops 1 | bytes 1 | tf_op jit(solution)/shard_map/message0/pallas_call | solution.py:355
  50.3 0.1 collective-permute-start.10
  50.3 0.0 collective-permute-done.6.refs_3_.refs_2_.refs_12_
  50.4 4.1 %collective-permute-start.9 = (bf16[2,512,512]{2,1,0:T(8,128)(2,1)}, bf16[2,512,512]{2,1,0:T(8,128)(2,1)S(1)}, u32[]{:S(2)}, u32[]{:S(2)}) collective-permute-start(bf16[2,512,512]{2,1,0:T(8,128)(2,1)} %after.8.refs_15_), channel_id=1, source_target_pairs={{1,2},{3,4},{5,6},{2,1},{4,3},{6,5},{9,10},{11,12},{13,14},{10,9},... | collective-permute-start | bytes 3145736 | tf_op jit(solution)/shard_map/ppermute | solution.py:397
  54.5 0.0 collective-permute-done.4.refs_10_
  54.5 3.4 %message1.1.refs_1_ = bf16[4,512,256]{2,1,0:T(8,128)(2,1)S(1)} custom-call(s32[24]{0:T(128)S(1)} %reshape.3.refs_0_, s32[3]{0:T(128)S(1)} %copy-done.3, s32[3]{0:T(128)S(1)} %copy-done.4, f32[3]{0:T(128)S(1)} %copy-done.5, bf16[3,4,256,256]{3,2,1,0:T(8,128)(2,1)S(1)} %get-tuple-element.8.refs_4_, bf16[3,4,256,256]{3,2,1,0:T(8,128)(2,1)S(1)} %copy-done.1, ...), custom_call_target="tpu_custom_call" | custom-call | flops 1 | bytes 1 | tf_op jit(solution)/shard_map/message1/pallas_call | solution.py:355
  57.9 0.0 collective-permute-done.refs_0_
  57.9 0.1 collective-permute-start.7
  58.0 2.4 %collective-permute-start.8 = (bf16[2,512,512]{2,1,0:T(8,128)(2,1)}, bf16[2,512,512]{2,1,0:T(8,128)(2,1)S(1)}, u32[]{:S(2)}, u32[]{:S(2)}) collective-permute-start(bf16[2,512,512]{2,1,0:T(8,128)(2,1)} %after.7.refs_14_), channel_id=1, source_target_pairs={{1,2},{3,4},{5,6},{2,1},{4,3},{6,5},{9,10},{11,12},{13,14},{10,9},... | collective-permute-start | bytes 3145736 | tf_op jit(solution)/shard_map/ppermute | solution.py:401
  60.4 0.1 collective-permute-start.11
  60.5 13.3 %collective-permute-done.9.refs_0_ = bf16[2,512,512]{2,1,0:T(8,128)(2,1)S(1)} collective-permute-done((bf16[2,512,512]{2,1,0:T(8,128)(2,1)}, bf16[2,512,512]{2,1,0:T(8,128)(2,1)S(1)}, u32[]{:S(2)}, u32[]{:S(2)}) %collective-permute-start.9) | collective-permute-done | bytes 1048608 | tf_op jit(solution)/shard_map/ppermute | solution.py:397
  73.8 4.5 %collective-permute-done.10.refs_1_.arrived = bf16[4,512,256]{2,1,0:T(8,128)(2,1)S(1)} collective-permute-done((bf16[4,512,256]{2,1,0:T(8,128)(2,1)S(1)}, bf16[4,512,256]{2,1,0:T(8,128)(2,1)S(1)}, u32[]{:S(2)}, u32[]{:S(2)}) %collective-permute-start.10) | collective-permute-done | bytes 1048608 | tf_op jit(solution)/shard_map/ppermute | solution.py:395
  78.3 0.0 collective-permute-done.7.refs_13_.refs_6_
  78.3 6.2 %first.1.refs_8_.sum_ref = f32[2,2,512,512]{3,2,1,0:T(8,128)S(1)} custom-call(s32[24]{0:T(128)S(1)} %reshape.3.refs_0_, s32[3]{0:T(128)S(1)} %copy-done.3, s32[3]{0:T(128)S(1)} %copy-done.4, f32[3]{0:T(128)S(1)} %copy-done.5, bf16[3,4,256,256]{3,2,1,0:T(8,128)(2,1)S(1)} %get-tuple-element.8.refs_4_, bf16[3,4,256,256]{3,2,1,0:T(8,128)(2,1)S(1)} %copy-done.1, ...), custom_call_target="tpu_custom_call" | custom-call | flops 1 | bytes 1 | tf_op jit(solution)/shard_map/first/pallas_call | solution.py:355
  84.5 1.4 %store0.1.refs_0_ = f32[1,2,2,512,512]{4,3,2,1,0:T(8,128)} custom-call(f32[2,2,512,512]{3,2,1,0:T(8,128)S(1)} %first.1.refs_8_.sum_ref, bf16[4,512,256]{2,1,0:T(8,128)(2,1)S(1)} %collective-permute-done.10.refs_1_.arrived), custom_call_target="tpu_custom_call" | custom-call | flops 1 | bytes 1 | tf_op jit(solution)/shard_map/store0/pallas_call | solution.py:321
  85.9 4.5 %collective-permute-done.8.refs_7_ = bf16[2,512,512]{2,1,0:T(8,128)(2,1)S(1)} collective-permute-done((bf16[2,512,512]{2,1,0:T(8,128)(2,1)}, bf16[2,512,512]{2,1,0:T(8,128)(2,1)S(1)}, u32[]{:S(2)}, u32[]{:S(2)}) %collective-permute-start.8) | collective-permute-done | bytes 1048608 | tf_op jit(solution)/shard_map/ppermute | solution.py:401
  90.4 2.2 %second.1.sum_ref = f32[1,2,512,512]{3,2,1,0:T(8,128)S(1)} custom-call(s32[24]{0:T(128)S(1)} %reshape.3.refs_0_, s32[3]{0:T(128)S(1)} %copy-done.3, s32[3]{0:T(128)S(1)} %copy-done.4, f32[3]{0:T(128)S(1)} %copy-done.5, bf16[3,4,256,256]{3,2,1,0:T(8,128)(2,1)S(1)} %get-tuple-element.8.refs_4_, bf16[3,4,256,256]{3,2,1,0:T(8,128)(2,1)S(1)} %copy-done.1, ...), custom_call_target="tpu_custom_call" | custom-call | flops 1 | bytes 1 | tf_op jit(solution)/shard_map/second/pallas_call | solution.py:355
  92.5 3.3 %collective-permute-done.11.arrived = bf16[4,512,256]{2,1,0:T(8,128)(2,1)S(1)} collective-permute-done((bf16[4,512,256]{2,1,0:T(8,128)(2,1)S(1)}, bf16[4,512,256]{2,1,0:T(8,128)(2,1)S(1)}, u32[]{:S(2)}, u32[]{:S(2)}) %collective-permute-start.11) | collective-permute-done | bytes 1048608 | tf_op jit(solution)/shard_map/ppermute | solution.py:399
  95.9 1.4 %store1.1 = f32[1,2,2,512,512]{4,3,2,1,0:T(8,128)} custom-call(f32[1,2,512,512]{3,2,1,0:T(8,128)S(1)} %second.1.sum_ref, bf16[4,512,256]{2,1,0:T(8,128)(2,1)S(1)} %collective-permute-done.11.arrived, f32[1,2,2,512,512]{4,3,2,1,0:T(8,128)} %store0.1.refs_0_), custom_call_target="tpu_custom_call", output_to_operand_aliasing={{}: (2, {})} | custom-call | flops 1 | bytes 1 | tf_op jit(solution)/shard_map/store1/pallas_call | solution.py:321
  (5 shorter events, 0.0 us)
Async XLA Ops:
  0.0 9.1 %copy-start.2 = (f32[3,4,2,128,128]{4,3,2,1,0:T(8,128)S(1)}, f32[3,4,2,128,128]{4,3,2,1,0:T(8,128)}, u32[]{:S(2)}) copy-start(f32[3,4,2,128,128]{4,3,2,1,0:T(8,128)} %coupling_ref.1) | copy-start | bytes 4718596
  1.5 14.4 %copy-start.6 = (s32[3,4,2]{1,2,0:T(2,128)S(1)}, s32[3,4,2]{1,2,0:T(2,128)}, u32[]{:S(2)}) copy-start(s32[3,4,2]{1,2,0:T(2,128)} %param.8) | copy-start | bytes 292
  1.5 25.2 %collective-permute-start.2 = (bf16[2,512,512]{2,1,0:T(8,128)(2,1)S(1)}, bf16[2,512,512]{2,1,0:T(8,128)(2,1)}, u32[]{:S(2)}, u32[]{:S(2)}) collective-permute-start(bf16[2,512,512]{2,1,0:T(8,128)(2,1)S(1)} %take.1._.refs_8_), channel_id=1, source_target_pairs={{0,24},{8,0},{16,8},{24,16},{1,25},{9,1},{17,9},{25,17},{2,26},{10... | collective-permute-start | bytes 3145736 | tf_op jit(solution)/shard_map/ppermute | solution.py:382
  4.9 21.8 %collective-permute-start.3 = (bf16[2,512,512]{2,1,0:T(8,128)(2,1)S(1)}, bf16[2,512,512]{2,1,0:T(8,128)(2,1)}, u32[]{:S(2)}, u32[]{:S(2)}) collective-permute-start(bf16[2,512,512]{2,1,0:T(8,128)(2,1)S(1)} %take.1._.refs_8_), channel_id=1, source_target_pairs={{1,2},{5,6},{2,1},{6,5},{3,7},{4,0},{9,10},{13,14},{10,9},{14,13},... | collective-permute-start | bytes 3145736 | tf_op jit(solution)/shard_map/ppermute | solution.py:383
  9.1 22.0 %collective-permute-start.1 = (bf16[1,2,2,512,512]{4,3,2,1,0:T(8,128)(2,1)}, bf16[1,2,2,512,512]{4,3,2,1,0:T(8,128)(2,1)}, u32[]{:S(2)}, u32[]{:S(2)}) collective-permute-start(bf16[1,2,2,512,512]{4,3,2,1,0:T(8,128)(2,1)} %green_ref.3), channel_id=1, source_target_pairs={{0,1},{2,3},{4,5},{6,7},{1,0},{3,2},{5,4},{7,6},{8,9},{10,11},{12,... | collective-permute-start | bytes 6291464 | tf_op jit(solution)/shard_map/ppermute | solution.py:387
  11.2 1.1 %copy-start = (bf16[3,4,256,256]{3,2,1,0:T(8,128)(2,1)}, bf16[3,4,256,256]{3,2,1,0:T(8,128)(2,1)S(1)}, u32[]{:S(2)}) copy-start(bf16[3,4,256,256]{3,2,1,0:T(8,128)(2,1)S(1)} %get-tuple-element.9.refs_5_) | copy-start | bytes 4718596
  12.3 42.1 %collective-permute-start.4 = (bf16[2,512,512]{2,1,0:T(8,128)(2,1)}, bf16[2,512,512]{2,1,0:T(8,128)(2,1)}, u32[]{:S(2)}, u32[]{:S(2)}) collective-permute-start(bf16[2,512,512]{2,1,0:T(8,128)(2,1)} %get-tuple-element.10.refs_7_), channel_id=1, source_target_pairs={{1,2},{3,4},{5,6},{2,1},{4,3},{6,5},{9,10},{11,12},{13,14},{10,9},... | collective-permute-start | bytes 3145736 | tf_op jit(solution)/shard_map/ppermute | solution.py:386
  15.6 42.3 %collective-permute-start = (bf16[2,512,512]{2,1,0:T(8,128)(2,1)}, bf16[2,512,512]{2,1,0:T(8,128)(2,1)}, u32[]{:S(2)}, u32[]{:S(2)}) collective-permute-start(bf16[2,512,512]{2,1,0:T(8,128)(2,1)} %get-tuple-element.10.refs_7_), channel_id=1, source_target_pairs={{0,24},{8,0},{16,8},{24,16},{1,25},{9,1},{17,9},{25,17},{2,26},{10... | collective-permute-start | bytes 3145736 | tf_op jit(solution)/shard_map/ppermute | solution.py:385
  26.7 20.4 %collective-permute-start.5 = (bf16[2,512,512]{2,1,0:T(8,128)(2,1)}, bf16[2,512,512]{2,1,0:T(8,128)(2,1)}, u32[]{:S(2)}, u32[]{:S(2)}) collective-permute-start(bf16[2,512,512]{2,1,0:T(8,128)(2,1)} %after.6.refs_9_), channel_id=1, source_target_pairs={{7,4},{0,3},{15,12},{8,11},{23,20},{16,19},{31,28},{24,27}} | collective-permute-start | bytes 3145736 | tf_op jit(solution)/shard_map/ppermute | solution.py:392
  28.0 22.4 %collective-permute-start.6 = (bf16[2,512,512]{2,1,0:T(8,128)(2,1)}, bf16[2,512,512]{2,1,0:T(8,128)(2,1)}, u32[]{:S(2)}, u32[]{:S(2)}) collective-permute-start(bf16[2,512,512]{2,1,0:T(8,128)(2,1)} %collective-permute-done.2.refs_1_.refs_0_), channel_id=1, source_target_pairs={{0,1},{2,3},{4,5},{6,7},{1,0},{3,2},{5,4},{7,6},{8,9},{10,11},{12,... | collective-permute-start | bytes 3145736 | tf_op jit(solution)/shard_map/ppermute | solution.py:389
  31.1 16.1 %copy-start.1 = (bf16[3,4,256,256]{3,2,1,0:T(8,128)(2,1)S(1)}, bf16[3,4,256,256]{3,2,1,0:T(8,128)(2,1)}, u32[]{:S(2)}) copy-start(bf16[3,4,256,256]{3,2,1,0:T(8,128)(2,1)} %copy-done) | copy-start | bytes 4718596
  31.1 16.1 %copy-start.3 = (s32[3]{0:T(128)S(1)}, s32[3]{0:T(128)}, u32[]{:S(2)}) copy-start(s32[3]{0:T(128)} %refs_1_.7) | copy-start | bytes 40
  31.1 16.1 %copy-start.4 = (s32[3]{0:T(128)S(1)}, s32[3]{0:T(128)}, u32[]{:S(2)}) copy-start(s32[3]{0:T(128)} %refs_2_.7) | copy-start | bytes 40
  31.1 16.1 %copy-start.5 = (f32[3]{0:T(128)S(1)}, f32[3]{0:T(128)}, u32[]{:S(2)}) copy-start(f32[3]{0:T(128)} %refs_3_.7) | copy-start | bytes 40
  50.3 28.0 %collective-permute-start.10 = (bf16[4,512,256]{2,1,0:T(8,128)(2,1)S(1)}, bf16[4,512,256]{2,1,0:T(8,128)(2,1)S(1)}, u32[]{:S(2)}, u32[]{:S(2)}) collective-permute-start(bf16[4,512,256]{2,1,0:T(8,128)(2,1)S(1)} %message0.1.refs_2_.refs_1_), channel_id=1, source_target_pairs={{0,8},{8,16},{16,24},{24,0},{1,9},{9,17},{17,25},{25,1},{2,10},{10... | collective-permute-start | bytes 3145736 | tf_op jit(solution)/shard_map/ppermute | solution.py:395
  50.4 23.4 %collective-permute-start.9 = (bf16[2,512,512]{2,1,0:T(8,128)(2,1)}, bf16[2,512,512]{2,1,0:T(8,128)(2,1)S(1)}, u32[]{:S(2)}, u32[]{:S(2)}) collective-permute-start(bf16[2,512,512]{2,1,0:T(8,128)(2,1)} %after.8.refs_15_), channel_id=1, source_target_pairs={{1,2},{3,4},{5,6},{2,1},{4,3},{6,5},{9,10},{11,12},{13,14},{10,9},... | collective-permute-start | bytes 3145736 | tf_op jit(solution)/shard_map/ppermute | solution.py:397
  57.9 20.4 %collective-permute-start.7 = (bf16[2,512,512]{2,1,0:T(8,128)(2,1)}, bf16[2,512,512]{2,1,0:T(8,128)(2,1)S(1)}, u32[]{:S(2)}, u32[]{:S(2)}) collective-permute-start(bf16[2,512,512]{2,1,0:T(8,128)(2,1)} %after.7.refs_14_), channel_id=1, source_target_pairs={{0,1},{2,3},{4,5},{6,7},{1,0},{3,2},{5,4},{7,6},{8,9},{10,11},{12,... | collective-permute-start | bytes 3145736 | tf_op jit(solution)/shard_map/ppermute | solution.py:402
  58.0 32.3 %collective-permute-start.8 = (bf16[2,512,512]{2,1,0:T(8,128)(2,1)}, bf16[2,512,512]{2,1,0:T(8,128)(2,1)S(1)}, u32[]{:S(2)}, u32[]{:S(2)}) collective-permute-start(bf16[2,512,512]{2,1,0:T(8,128)(2,1)} %after.7.refs_14_), channel_id=1, source_target_pairs={{1,2},{3,4},{5,6},{2,1},{4,3},{6,5},{9,10},{11,12},{13,14},{10,9},... | collective-permute-start | bytes 3145736 | tf_op jit(solution)/shard_map/ppermute | solution.py:401
  60.4 35.5 %collective-permute-start.11 = (bf16[4,512,256]{2,1,0:T(8,128)(2,1)S(1)}, bf16[4,512,256]{2,1,0:T(8,128)(2,1)S(1)}, u32[]{:S(2)}, u32[]{:S(2)}) collective-permute-start(bf16[4,512,256]{2,1,0:T(8,128)(2,1)S(1)} %message1.1.refs_1_), channel_id=1, source_target_pairs={{0,8},{8,16},{16,24},{24,0},{1,9},{9,17},{17,25},{25,1},{2,10},{10... | collective-permute-start | bytes 3145736 | tf_op jit(solution)/shard_map/ppermute | solution.py:399

commit v6 on v5

--- a/solution.py
+++ b/solution.py
@@ -9,7 +9,7 @@
 from jax.sharding import PartitionSpec as P
 
 SMAX = 2
-PIECES = 4
+PIECES = 1
 MIB = 1024 * 1024
 SMALL = pltpu.CompilerParams(vmem_limit_bytes=6 * MIB)
 LARGE = pltpu.CompilerParams(vmem_limit_bytes=24 * MIB)

time: 99.1 us -> 98.9 us (level)
  no operation moved by 1% of the time
where the time goes in v6:
time: 98.9 us; the launch traced here: 97.1 us
  waiting for transfers between devices  52.4 us (53%)
  starting transfers between devices  22.1 us (22%)
  Pallas kernels  21.1 us (21%)
  local copies, waits for them, and re-layouts  1.36 us (1%)
    ppermute x1, waiting for transfers between devices, on_device(): relayed2 = lax.ppermute(own2, 'en', arriving)  15.7 us
    pallas_call x4, Pallas kernels, call(): pl.pallas_call(kernel, in_specs=[SMEM] * 4 + [VMEM] * 2 + [ANY] * len(ope...  14.9 us
    ppermute x1, waiting for transfers between devices, on_device(): near2 = lax.ppermute(near1, 'en', between)  13.3 us
    ppermute x1, waiting for transfers between devices, on_device(): near1 = lax.ppermute(own1, 'kz', backward)  10.7 us
    ppermute x1, waiting for transfers between devices, on_device(): near3 = lax.ppermute(near0, 'en', between)  4.84 us
    ppermute x1, waiting for transfers between devices, on_device(): arrived0 = lax.ppermute(sent0, 'kz', forward)  4.55 us
    ppermute x1, starting transfers between devices, on_device(): own2 = lax.ppermute(own1, 'en', across)  4.2 us
    ppermute x1, starting transfers between devices, on_device(): near2 = lax.ppermute(near1, 'en', between)  4.07 us
  transfers between devices with their start and end apart: 12, of which 6 were waited for; matrix products, arithmetic and copies ran while one was open for 0% of the time, Pallas kernels for 19%

profile of v6, /device:TPU:3, one launch (start us, length us, event | category | flops | bytes accessed | tf_op | source)
XLA Modules:
  0.0 97.1 jit_solution(4576298635693658842)
XLA Ops:
  0.0 0.0 copy-start.2
  0.0 1.3 %take.1._.refs_8_ = bf16[2,512,512]{2,1,0:T(8,128)(2,1)S(1)} custom-call(bf16[1,2,2,512,512]{4,3,2,1,0:T(8,128)(2,1)} %green_ref.3), custom_call_target="tpu_custom_call" | custom-call | flops 1 | bytes 1 | tf_op jit(solution)/shard_map/take/pallas_call | solution.py:98
  1.3 0.0 copy-start.6
  1.4 3.4 %collective-permute-start.2 = (bf16[2,512,512]{2,1,0:T(8,128)(2,1)S(1)}, bf16[2,512,512]{2,1,0:T(8,128)(2,1)}, u32[]{:S(2)}, u32[]{:S(2)}) collective-permute-start(bf16[2,512,512]{2,1,0:T(8,128)(2,1)S(1)} %take.1._.refs_8_), channel_id=1, source_target_pairs={{0,24},{8,0},{16,8},{24,16},{1,25},{9,1},{17,9},{25,17},{2,26},{10... | collective-permute-start | bytes 3145736 | tf_op jit(solution)/shard_map/ppermute | solution.py:382
  4.7 4.2 %collective-permute-start.3 = (bf16[2,512,512]{2,1,0:T(8,128)(2,1)S(1)}, bf16[2,512,512]{2,1,0:T(8,128)(2,1)}, u32[]{:S(2)}, u32[]{:S(2)}) collective-permute-start(bf16[2,512,512]{2,1,0:T(8,128)(2,1)S(1)} %take.1._.refs_8_), channel_id=1, source_target_pairs={{1,2},{5,6},{2,1},{6,5},{3,7},{4,0},{9,10},{13,14},{10,9},{14,13},... | collective-permute-start | bytes 3145736 | tf_op jit(solution)/shard_map/ppermute | solution.py:383
  8.9 0.0 collective-permute-start.1
  8.9 0.0 copy-done.2
  8.9 2.0 %prepare.1 = (bf16[2,512,512]{2,1,0:T(8,128)(2,1)}, bf16[3,4,256,256]{3,2,1,0:T(8,128)(2,1)S(1)}, bf16[3,4,256,256]{3,2,1,0:T(8,128)(2,1)S(1)}) custom-call(bf16[1,2,2,512,512]{4,3,2,1,0:T(8,128)(2,1)} %green_ref.3, f32[3,4,2,128,128]{4,3,2,1,0:T(8,128)S(1)} %copy-done.2, bf16[2,512,512]{2,1,0:T(8,128)(2,1)S(1)} %take.1._.refs_8_), custom_call_target="tpu_custom_call" | custom-call | flops 1 | bytes 1 | tf_op jit(solution)/shard_map/prepare/pallas_call | solution.py:131
  11.0 0.0 copy-start
  11.0 1.1 %copy-done = bf16[3,4,256,256]{3,2,1,0:T(8,128)(2,1)} copy-done((bf16[3,4,256,256]{3,2,1,0:T(8,128)(2,1)}, bf16[3,4,256,256]{3,2,1,0:T(8,128)(2,1)S(1)}, u32[]{:S(2)}) %copy-start) | copy-done | bytes 1572888
  12.1 3.3 %collective-permute-start.4 = (bf16[2,512,512]{2,1,0:T(8,128)(2,1)}, bf16[2,512,512]{2,1,0:T(8,128)(2,1)}, u32[]{:S(2)}, u32[]{:S(2)}) collective-permute-start(bf16[2,512,512]{2,1,0:T(8,128)(2,1)} %get-tuple-element.10.refs_7_), channel_id=1, source_target_pairs={{1,2},{3,4},{5,6},{2,1},{4,3},{6,5},{9,10},{11,12},{13,14},{10,9},... | collective-permute-start | bytes 3145736 | tf_op jit(solution)/shard_map/ppermute | solution.py:386
  15.5 0.2 collective-permute-start
  15.7 0.0 copy-done.6
  15.7 0.1 copy.14
  15.8 0.1 reshape.3.refs_0_
  15.9 10.7 %collective-permute-done.2.refs_1_.refs_0_ = bf16[2,512,512]{2,1,0:T(8,128)(2,1)} collective-permute-done((bf16[2,512,512]{2,1,0:T(8,128)(2,1)S(1)}, bf16[2,512,512]{2,1,0:T(8,128)(2,1)}, u32[]{:S(2)}, u32[]{:S(2)}) %collective-permute-start.2) | collective-permute-done | bytes 1048608 | tf_op jit(solution)/shard_map/ppermute | solution.py:382
  26.6 0.0 collective-permute-done.3.refs_0_
  26.6 1.3 %collective-permute-start.5 = (bf16[2,512,512]{2,1,0:T(8,128)(2,1)}, bf16[2,512,512]{2,1,0:T(8,128)(2,1)}, u32[]{:S(2)}, u32[]{:S(2)}) collective-permute-start(bf16[2,512,512]{2,1,0:T(8,128)(2,1)} %after.6.refs_9_), channel_id=1, source_target_pairs={{7,4},{0,3},{15,12},{8,11},{23,20},{16,19},{31,28},{24,27}} | collective-permute-start | bytes 3145736 | tf_op jit(solution)/shard_map/ppermute | solution.py:392
  27.9 3.1 %collective-permute-start.6 = (bf16[2,512,512]{2,1,0:T(8,128)(2,1)}, bf16[2,512,512]{2,1,0:T(8,128)(2,1)}, u32[]{:S(2)}, u32[]{:S(2)}) collective-permute-start(bf16[2,512,512]{2,1,0:T(8,128)(2,1)} %collective-permute-done.2.refs_1_.refs_0_), channel_id=1, source_target_pairs={{0,1},{2,3},{4,5},{6,7},{1,0},{3,2},{5,4},{7,6},{8,9},{10,11},{12,... | collective-permute-start | bytes 3145736 | tf_op jit(solution)/shard_map/ppermute | solution.py:389
  30.9 0.0 collective-permute-done.1.refs_0_
  30.9 0.0 copy-start.1
  30.9 0.0 copy-start.3
  30.9 0.0 copy-start.4
  30.9 0.0 copy-start.5
  31.0 15.7 %collective-permute-done.5.refs_11_.refs_10_ = bf16[2,512,512]{2,1,0:T(8,128)(2,1)} collective-permute-done((bf16[2,512,512]{2,1,0:T(8,128)(2,1)}, bf16[2,512,512]{2,1,0:T(8,128)(2,1)}, u32[]{:S(2)}, u32[]{:S(2)}) %collective-permute-start.5) | collective-permute-done | bytes 1048608 | tf_op jit(solution)/shard_map/ppermute | solution.py:392
  46.7 0.0 copy-done.1
  46.7 0.0 copy-done.3
  46.7 0.0 copy-done.4
  46.7 0.0 copy-done.5
  46.7 3.5 %message0.1.refs_2_.refs_1_ = bf16[4,512,256]{2,1,0:T(8,128)(2,1)S(1)} custom-call(s32[24]{0:T(128)S(1)} %reshape.3.refs_0_, s32[3]{0:T(128)S(1)} %copy-done.3, s32[3]{0:T(128)S(1)} %copy-done.4, f32[3]{0:T(128)S(1)} %copy-done.5, bf16[3,4,256,256]{3,2,1,0:T(8,128)(2,1)S(1)} %get-tuple-element.8.refs_4_, bf16[3,4,256,256]{3,2,1,0:T(8,128)(2,1)S(1)} %copy-done.1, ...), custom_call_target="tpu_custom_call" | custom-call | flops 1 | bytes 1 | tf_op jit(solution)/shard_map/message0/pallas_call | solution.py:355
  50.2 0.1 collective-permute-start.10
  50.2 0.0 collective-permute-done.6.refs_3_.refs_2_.refs_12_
  50.2 4.1 %collective-permute-start.9 = (bf16[2,512,512]{2,1,0:T(8,128)(2,1)}, bf16[2,512,512]{2,1,0:T(8,128)(2,1)S(1)}, u32[]{:S(2)}, u32[]{:S(2)}) collective-permute-start(bf16[2,512,512]{2,1,0:T(8,128)(2,1)} %after.8.refs_15_), channel_id=1, source_target_pairs={{1,2},{3,4},{5,6},{2,1},{4,3},{6,5},{9,10},{11,12},{13,14},{10,9},... | collective-permute-start | bytes 3145736 | tf_op jit(solution)/shard_map/ppermute | solution.py:397
  54.3 0.0 collective-permute-done.4.refs_10_
  54.3 3.5 %message1.1.refs_1_ = bf16[4,512,256]{2,1,0:T(8,128)(2,1)S(1)} custom-call(s32[24]{0:T(128)S(1)} %reshape.3.refs_0_, s32[3]{0:T(128)S(1)} %copy-done.3, s32[3]{0:T(128)S(1)} %copy-done.4, f32[3]{0:T(128)S(1)} %copy-done.5, bf16[3,4,256,256]{3,2,1,0:T(8,128)(2,1)S(1)} %get-tuple-element.8.refs_4_, bf16[3,4,256,256]{3,2,1,0:T(8,128)(2,1)S(1)} %copy-done.1, ...), custom_call_target="tpu_custom_call" | custom-call | flops 1 | bytes 1 | tf_op jit(solution)/shard_map/message1/pallas_call | solution.py:355
  57.8 0.0 collective-permute-done.refs_0_
  57.8 0.1 collective-permute-start.7
  57.9 2.4 %collective-permute-start.8 = (bf16[2,512,512]{2,1,0:T(8,128)(2,1)}, bf16[2,512,512]{2,1,0:T(8,128)(2,1)S(1)}, u32[]{:S(2)}, u32[]{:S(2)}) collective-permute-start(bf16[2,512,512]{2,1,0:T(8,128)(2,1)} %after.7.refs_14_), channel_id=1, source_target_pairs={{1,2},{3,4},{5,6},{2,1},{4,3},{6,5},{9,10},{11,12},{13,14},{10,9},... | collective-permute-start | bytes 3145736 | tf_op jit(solution)/shard_map/ppermute | solution.py:401
  60.3 0.1 collective-permute-start.11
  60.4 13.3 %collective-permute-done.9.refs_0_ = bf16[2,512,512]{2,1,0:T(8,128)(2,1)S(1)} collective-permute-done((bf16[2,512,512]{2,1,0:T(8,128)(2,1)}, bf16[2,512,512]{2,1,0:T(8,128)(2,1)S(1)}, u32[]{:S(2)}, u32[]{:S(2)}) %collective-permute-start.9) | collective-permute-done | bytes 1048608 | tf_op jit(solution)/shard_map/ppermute | solution.py:397
  73.6 4.5 %collective-permute-done.10.refs_1_.arrived = bf16[4,512,256]{2,1,0:T(8,128)(2,1)S(1)} collective-permute-done((bf16[4,512,256]{2,1,0:T(8,128)(2,1)S(1)}, bf16[4,512,256]{2,1,0:T(8,128)(2,1)S(1)}, u32[]{:S(2)}, u32[]{:S(2)}) %collective-permute-start.10) | collective-permute-done | bytes 1048608 | tf_op jit(solution)/shard_map/ppermute | solution.py:395
  78.2 0.0 collective-permute-done.7.refs_13_.refs_6_
  78.2 5.8 %first.1.refs_8_.sum_ref = f32[2,2,512,512]{3,2,1,0:T(8,128)S(1)} custom-call(s32[24]{0:T(128)S(1)} %reshape.3.refs_0_, s32[3]{0:T(128)S(1)} %copy-done.3, s32[3]{0:T(128)S(1)} %copy-done.4, f32[3]{0:T(128)S(1)} %copy-done.5, bf16[3,4,256,256]{3,2,1,0:T(8,128)(2,1)S(1)} %get-tuple-element.8.refs_4_, bf16[3,4,256,256]{3,2,1,0:T(8,128)(2,1)S(1)} %copy-done.1, ...), custom_call_target="tpu_custom_call" | custom-call | flops 1 | bytes 1 | tf_op jit(solution)/shard_map/first/pallas_call | solution.py:355
  84.0 1.4 %store0.1.refs_0_ = f32[1,2,2,512,512]{4,3,2,1,0:T(8,128)} custom-call(f32[2,2,512,512]{3,2,1,0:T(8,128)S(1)} %first.1.refs_8_.sum_ref, bf16[4,512,256]{2,1,0:T(8,128)(2,1)S(1)} %collective-permute-done.10.refs_1_.arrived), custom_call_target="tpu_custom_call" | custom-call | flops 1 | bytes 1 | tf_op jit(solution)/shard_map/store0/pallas_call | solution.py:321
  85.4 4.8 %collective-permute-done.8.refs_7_ = bf16[2,512,512]{2,1,0:T(8,128)(2,1)S(1)} collective-permute-done((bf16[2,512,512]{2,1,0:T(8,128)(2,1)}, bf16[2,512,512]{2,1,0:T(8,128)(2,1)S(1)}, u32[]{:S(2)}, u32[]{:S(2)}) %collective-permute-start.8) | collective-permute-done | bytes 1048608 | tf_op jit(solution)/shard_map/ppermute | solution.py:401
  90.2 2.2 %second.1.sum_ref = f32[1,2,512,512]{3,2,1,0:T(8,128)S(1)} custom-call(s32[24]{0:T(128)S(1)} %reshape.3.refs_0_, s32[3]{0:T(128)S(1)} %copy-done.3, s32[3]{0:T(128)S(1)} %copy-done.4, f32[3]{0:T(128)S(1)} %copy-done.5, bf16[3,4,256,256]{3,2,1,0:T(8,128)(2,1)S(1)} %get-tuple-element.8.refs_4_, bf16[3,4,256,256]{3,2,1,0:T(8,128)(2,1)S(1)} %copy-done.1, ...), custom_call_target="tpu_custom_call" | custom-call | flops 1 | bytes 1 | tf_op jit(solution)/shard_map/second/pallas_call | solution.py:355
  92.4 3.3 %collective-permute-done.11.arrived = bf16[4,512,256]{2,1,0:T(8,128)(2,1)S(1)} collective-permute-done((bf16[4,512,256]{2,1,0:T(8,128)(2,1)S(1)}, bf16[4,512,256]{2,1,0:T(8,128)(2,1)S(1)}, u32[]{:S(2)}, u32[]{:S(2)}) %collective-permute-start.11) | collective-permute-done | bytes 1048608 | tf_op jit(solution)/shard_map/ppermute | solution.py:399
  95.7 1.4 %store1.1 = f32[1,2,2,512,512]{4,3,2,1,0:T(8,128)} custom-call(f32[1,2,512,512]{3,2,1,0:T(8,128)S(1)} %second.1.sum_ref, bf16[4,512,256]{2,1,0:T(8,128)(2,1)S(1)} %collective-permute-done.11.arrived, f32[1,2,2,512,512]{4,3,2,1,0:T(8,128)} %store0.1.refs_0_), custom_call_target="tpu_custom_call", output_to_operand_aliasing={{}: (2, {})} | custom-call | flops 1 | bytes 1 | tf_op jit(solution)/shard_map/store1/pallas_call | solution.py:321
  (5 shorter events, 0.0 us)
Async XLA Ops:
  0.0 8.9 %copy-start.2 = (f32[3,4,2,128,128]{4,3,2,1,0:T(8,128)S(1)}, f32[3,4,2,128,128]{4,3,2,1,0:T(8,128)}, u32[]{:S(2)}) copy-start(f32[3,4,2,128,128]{4,3,2,1,0:T(8,128)} %coupling_ref.1) | copy-start | bytes 4718596
  1.3 14.3 %copy-start.6 = (s32[3,4,2]{1,2,0:T(2,128)S(1)}, s32[3,4,2]{1,2,0:T(2,128)}, u32[]{:S(2)}) copy-start(s32[3,4,2]{1,2,0:T(2,128)} %param.8) | copy-start | bytes 292
  1.4 25.2 %collective-permute-start.2 = (bf16[2,512,512]{2,1,0:T(8,128)(2,1)S(1)}, bf16[2,512,512]{2,1,0:T(8,128)(2,1)}, u32[]{:S(2)}, u32[]{:S(2)}) collective-permute-start(bf16[2,512,512]{2,1,0:T(8,128)(2,1)S(1)} %take.1._.refs_8_), channel_id=1, source_target_pairs={{0,24},{8,0},{16,8},{24,16},{1,25},{9,1},{17,9},{25,17},{2,26},{10... | collective-permute-start | bytes 3145736 | tf_op jit(solution)/shard_map/ppermute | solution.py:382
  4.7 21.8 %collective-permute-start.3 = (bf16[2,512,512]{2,1,0:T(8,128)(2,1)S(1)}, bf16[2,512,512]{2,1,0:T(8,128)(2,1)}, u32[]{:S(2)}, u32[]{:S(2)}) collective-permute-start(bf16[2,512,512]{2,1,0:T(8,128)(2,1)S(1)} %take.1._.refs_8_), channel_id=1, source_target_pairs={{1,2},{5,6},{2,1},{6,5},{3,7},{4,0},{9,10},{13,14},{10,9},{14,13},... | collective-permute-start | bytes 3145736 | tf_op jit(solution)/shard_map/ppermute | solution.py:383
  8.9 22.0 %collective-permute-start.1 = (bf16[1,2,2,512,512]{4,3,2,1,0:T(8,128)(2,1)}, bf16[1,2,2,512,512]{4,3,2,1,0:T(8,128)(2,1)}, u32[]{:S(2)}, u32[]{:S(2)}) collective-permute-start(bf16[1,2,2,512,512]{4,3,2,1,0:T(8,128)(2,1)} %green_ref.3), channel_id=1, source_target_pairs={{0,1},{2,3},{4,5},{6,7},{1,0},{3,2},{5,4},{7,6},{8,9},{10,11},{12,... | collective-permute-start | bytes 6291464 | tf_op jit(solution)/shard_map/ppermute | solution.py:387
  11.0 1.1 %copy-start = (bf16[3,4,256,256]{3,2,1,0:T(8,128)(2,1)}, bf16[3,4,256,256]{3,2,1,0:T(8,128)(2,1)S(1)}, u32[]{:S(2)}) copy-start(bf16[3,4,256,256]{3,2,1,0:T(8,128)(2,1)S(1)} %get-tuple-element.9.refs_5_) | copy-start | bytes 4718596
  12.1 42.2 %collective-permute-start.4 = (bf16[2,512,512]{2,1,0:T(8,128)(2,1)}, bf16[2,512,512]{2,1,0:T(8,128)(2,1)}, u32[]{:S(2)}, u32[]{:S(2)}) collective-permute-start(bf16[2,512,512]{2,1,0:T(8,128)(2,1)} %get-tuple-element.10.refs_7_), channel_id=1, source_target_pairs={{1,2},{3,4},{5,6},{2,1},{4,3},{6,5},{9,10},{11,12},{13,14},{10,9},... | collective-permute-start | bytes 3145736 | tf_op jit(solution)/shard_map/ppermute | solution.py:386
  15.5 42.3 %collective-permute-start = (bf16[2,512,512]{2,1,0:T(8,128)(2,1)}, bf16[2,512,512]{2,1,0:T(8,128)(2,1)}, u32[]{:S(2)}, u32[]{:S(2)}) collective-permute-start(bf16[2,512,512]{2,1,0:T(8,128)(2,1)} %get-tuple-element.10.refs_7_), channel_id=1, source_target_pairs={{0,24},{8,0},{16,8},{24,16},{1,25},{9,1},{17,9},{25,17},{2,26},{10... | collective-permute-start | bytes 3145736 | tf_op jit(solution)/shard_map/ppermute | solution.py:385
  26.6 20.1 %collective-permute-start.5 = (bf16[2,512,512]{2,1,0:T(8,128)(2,1)}, bf16[2,512,512]{2,1,0:T(8,128)(2,1)}, u32[]{:S(2)}, u32[]{:S(2)}) collective-permute-start(bf16[2,512,512]{2,1,0:T(8,128)(2,1)} %after.6.refs_9_), channel_id=1, source_target_pairs={{7,4},{0,3},{15,12},{8,11},{23,20},{16,19},{31,28},{24,27}} | collective-permute-start | bytes 3145736 | tf_op jit(solution)/shard_map/ppermute | solution.py:392
  27.9 22.4 %collective-permute-start.6 = (bf16[2,512,512]{2,1,0:T(8,128)(2,1)}, bf16[2,512,512]{2,1,0:T(8,128)(2,1)}, u32[]{:S(2)}, u32[]{:S(2)}) collective-permute-start(bf16[2,512,512]{2,1,0:T(8,128)(2,1)} %collective-permute-done.2.refs_1_.refs_0_), channel_id=1, source_target_pairs={{0,1},{2,3},{4,5},{6,7},{1,0},{3,2},{5,4},{7,6},{8,9},{10,11},{12,... | collective-permute-start | bytes 3145736 | tf_op jit(solution)/shard_map/ppermute | solution.py:389
  30.9 15.7 %copy-start.1 = (bf16[3,4,256,256]{3,2,1,0:T(8,128)(2,1)S(1)}, bf16[3,4,256,256]{3,2,1,0:T(8,128)(2,1)}, u32[]{:S(2)}) copy-start(bf16[3,4,256,256]{3,2,1,0:T(8,128)(2,1)} %copy-done) | copy-start | bytes 4718596
  30.9 15.7 %copy-start.3 = (s32[3]{0:T(128)S(1)}, s32[3]{0:T(128)}, u32[]{:S(2)}) copy-start(s32[3]{0:T(128)} %refs_1_.7) | copy-start | bytes 40
  30.9 15.7 %copy-start.4 = (s32[3]{0:T(128)S(1)}, s32[3]{0:T(128)}, u32[]{:S(2)}) copy-start(s32[3]{0:T(128)} %refs_2_.7) | copy-start | bytes 40
  30.9 15.7 %copy-start.5 = (f32[3]{0:T(128)S(1)}, f32[3]{0:T(128)}, u32[]{:S(2)}) copy-start(f32[3]{0:T(128)} %refs_3_.7) | copy-start | bytes 40
  50.2 28.0 %collective-permute-start.10 = (bf16[4,512,256]{2,1,0:T(8,128)(2,1)S(1)}, bf16[4,512,256]{2,1,0:T(8,128)(2,1)S(1)}, u32[]{:S(2)}, u32[]{:S(2)}) collective-permute-start(bf16[4,512,256]{2,1,0:T(8,128)(2,1)S(1)} %message0.1.refs_2_.refs_1_), channel_id=1, source_target_pairs={{0,8},{8,16},{16,24},{24,0},{1,9},{9,17},{17,25},{25,1},{2,10},{10... | collective-permute-start | bytes 3145736 | tf_op jit(solution)/shard_map/ppermute | solution.py:395
  50.2 23.4 %collective-permute-start.9 = (bf16[2,512,512]{2,1,0:T(8,128)(2,1)}, bf16[2,512,512]{2,1,0:T(8,128)(2,1)S(1)}, u32[]{:S(2)}, u32[]{:S(2)}) collective-permute-start(bf16[2,512,512]{2,1,0:T(8,128)(2,1)} %after.8.refs_15_), channel_id=1, source_target_pairs={{1,2},{3,4},{5,6},{2,1},{4,3},{6,5},{9,10},{11,12},{13,14},{10,9},... | collective-permute-start | bytes 3145736 | tf_op jit(solution)/shard_map/ppermute | solution.py:397
  57.8 20.4 %collective-permute-start.7 = (bf16[2,512,512]{2,1,0:T(8,128)(2,1)}, bf16[2,512,512]{2,1,0:T(8,128)(2,1)S(1)}, u32[]{:S(2)}, u32[]{:S(2)}) collective-permute-start(bf16[2,512,512]{2,1,0:T(8,128)(2,1)} %after.7.refs_14_), channel_id=1, source_target_pairs={{0,1},{2,3},{4,5},{6,7},{1,0},{3,2},{5,4},{7,6},{8,9},{10,11},{12,... | collective-permute-start | bytes 3145736 | tf_op jit(solution)/shard_map/ppermute | solution.py:402
  57.9 32.3 %collective-permute-start.8 = (bf16[2,512,512]{2,1,0:T(8,128)(2,1)}, bf16[2,512,512]{2,1,0:T(8,128)(2,1)S(1)}, u32[]{:S(2)}, u32[]{:S(2)}) collective-permute-start(bf16[2,512,512]{2,1,0:T(8,128)(2,1)} %after.7.refs_14_), channel_id=1, source_target_pairs={{1,2},{3,4},{5,6},{2,1},{4,3},{6,5},{9,10},{11,12},{13,14},{10,9},... | collective-permute-start | bytes 3145736 | tf_op jit(solution)/shard_map/ppermute | solution.py:401
  60.3 35.4 %collective-permute-start.11 = (bf16[4,512,256]{2,1,0:T(8,128)(2,1)S(1)}, bf16[4,512,256]{2,1,0:T(8,128)(2,1)S(1)}, u32[]{:S(2)}, u32[]{:S(2)}) collective-permute-start(bf16[4,512,256]{2,1,0:T(8,128)(2,1)S(1)} %message1.1.refs_1_), channel_id=1, source_target_pairs={{0,8},{8,16},{16,24},{24,0},{1,9},{9,17},{17,25},{25,1},{2,10},{10... | collective-permute-start | bytes 3145736 | tf_op jit(solution)/shard_map/ppermute | solution.py:399

commit v7 on v6

--- a/solution.py
+++ b/solution.py
@@ -218,10 +218,10 @@
     return [(jnp.logical_not(at_row_end(row)), first, second), (at_row_end(row), first, levels[-1])]
 
 
-def message_kernel(place, offset, row, *refs):
+def message_kernel(place, offset, row, count, *refs):
     terms = Terms(refs[:4], refs[4:6], refs[-3:])
-    levels = levels_of(*refs[6:-5])
-    message_ref, total = refs[-5:-3]
+    levels = levels_of(*refs[6 : -4 - count])
+    message_refs, total = refs[-4 - count : -4], refs[-4]
     for q in range(terms.transfers):
         for shift in range(1, SMAX + 1):
             wanted = (terms.offsets[q] == offset) & (terms.shifts[q] == shift)
@@ -238,7 +238,8 @@
             terms.arrive(q)
             terms.multiply(q, q, emit)
 
-    message_ref[...] = total[...].astype(jnp.bfloat16)
+    for i, ref in enumerate(message_refs):
+        ref[...] = total[:, pl.ds(i * ref.shape[1], ref.shape[1]), :].astype(jnp.bfloat16)
 
 
 def add_to(total, place, block):
@@ -297,19 +298,19 @@
             terms.multiply(q, 0, add_to(total, 0, terms.block))
 
 
-def store_kernel(place, sum_ref, arrived, *refs):
+def store_kernel(place, start, sum_ref, arrived, *refs):
     out_ref, held, sems = refs[-3:]
-    listed, orbitals, width = arrived.shape
+    listed, count, width = arrived.shape
     block = width // 2
     energy = odd() * place + (1 - odd()) * (1 - place)
     copies = []
-    for piece in range(orbitals // block):
-        rows = pl.ds(piece * block, block)
+    for piece in range(count // block):
+        here, rows = pl.ds(piece * block, block), pl.ds(start + piece * block, block)
         for column in range(listed):
             columns = pl.ds(column * block, block)
             for part in range(2):
                 held[part, rows, columns] = sum_ref[0, part, rows, columns] + arrived[
-                    column, rows, pl.ds(part * block, block)
+                    column, here, pl.ds(part * block, block)
                 ].astype(jnp.float32)
         copies.append(pltpu.make_async_copy(held.at[:, rows, :], out_ref.at[0, energy, :, rows, :], sems.at[piece]))
         copies[-1].start()
@@ -317,9 +318,9 @@
         copy.wait()
 
 
-def store(place, sums, arrived, result, *earlier):
+def store(place, sums, arrived, result, *earlier, half=0):
     return pl.pallas_call(
-        functools.partial(store_kernel, place),
+        functools.partial(store_kernel, place, half * arrived.shape[1]),
         in_specs=[VMEM, VMEM] + [ANY] * len(earlier),
         out_specs=ANY,
         out_shape=result,
@@ -330,7 +331,7 @@
         input_output_aliases={2: 0} if earlier else {},
         compiler_params=SMALL,
         cost_estimate=CHEAP,
-        name="store%d" % place,
+        name="store%d%d" % (place, half),
     )(in_vmem(sums), in_vmem(arrived), *earlier)
 
 
@@ -355,7 +356,7 @@
         return pl.pallas_call(
             kernel,
             in_specs=[SMEM] * 4 + [VMEM] * 2 + [ANY] * len(operands) + [VMEM] * len(sums),
-            out_specs=VMEM,
+            out_specs=[VMEM] * len(out_shape) if isinstance(out_shape, list) else VMEM,
             out_shape=out_shape,
             scratch_shapes=[*scratch, *term_scratch(slots, coupling.shape, orbitals)],
             compiler_params=LARGE,
@@ -363,12 +364,12 @@
             name=name,
         )(*scalar_args, in_vmem(left), in_vmem(right), *operands, *[in_vmem(x) for x in sums])
 
-    def message(place, *operands):
+    def message(place, count, *operands):
         total = pltpu.VMEM((listed, orbitals, 2 * block), jnp.float32)
-        kernel = functools.partial(message_kernel, place, 1, row)
+        kernel = functools.partial(message_kernel, place, 1, row, count)
         return call(
             kernel,
-            pltpu.VMEM(total.shape, jnp.bfloat16),
+            [pltpu.VMEM((listed, orbitals // count, 2 * block), jnp.bfloat16)] * count,
             transfers,
             "message%d" % place,
             *operands,
@@ -391,12 +392,13 @@
     own2 = after(own2, near1)
     relayed2 = lax.ppermute(own2, "en", arriving)
     own = (own_, own0, own1, own2, own3, relayed2)
-    sent0 = message(0, *own[:-2], relayed2)
+    (sent0,) = message(0, 1, *own[:-2], relayed2)
     arrived0 = lax.ppermute(sent0, "kz", forward)
     near1 = after(near1, sent0, mate1, cost=CHEAP)
     near2 = lax.ppermute(near1, "en", between)
-    sent1 = message(1, *own)
+    sent1, sent2 = message(1, 2, *own)
     arrived1 = lax.ppermute(sent1, "kz", forward)
+    arrived2 = lax.ppermute(sent2, "kz", forward)
     near0 = after(near0, sent1, sent0, mate1, cost=CHEAP)
     near3 = lax.ppermute(near0, "en", between)
     mate0 = lax.ppermute(near0, "en", on_chip)
@@ -408,7 +410,8 @@
     partial = store(0, sums, arrived0, result)
     second = functools.partial(second_kernel, -1, 1)
     sums = call(second, sums_at(1), 1, "second", mate0, near3, sums=[sums])
-    return store(1, sums, arrived1, result, partial)
+    partial = store(1, sums, arrived1, result, partial)
+    return store(1, sums, arrived2, result, partial, half=1)
 
 
 def solution(mesh):

time: 98.9 us -> 98.6 us (level)
  waiting for transfers between devices: 52.4 us -> 50.2 us
  starting transfers between devices: 22.1 us -> 23.5 us
    ppermute x1, waiting for transfers between devices: 3.33 us -> 0.01 us  [on_device(): arrived1 = lax.ppermute(sent1, 'kz', forward)]
    ppermute x1, waiting for transfers between devices: 4.84 us -> 2.7 us  [on_device(): near3 = lax.ppermute(near0, 'en', between)]
    ppermute x0 -> x1, waiting for transfers between devices: none -> 2.02 us  [on_device(): arrived2 = lax.ppermute(sent2, 'kz', forward)]
    ppermute x1, waiting for transfers between devices: 4.55 us -> 6.55 us  [on_device(): arrived0 = lax.ppermute(sent0, 'kz', forward)]
    ppermute x1, waiting for transfers between devices: 13.3 us -> 11.6 us  [on_device(): near2 = lax.ppermute(near1, 'en', between)]
    ppermute x1, starting transfers between devices: 0.06 us -> 1.34 us  [on_device(): arrived1 = lax.ppermute(sent1, 'kz', forward)]
    pallas_call x2 -> x3, Pallas kernels: 2.82 us -> 3.51 us  [store(): pl.pallas_call(functools.partial(store_kernel, place, half * arrived.shap...]
  transfers between devices with their start and end apart: 12 -> 13, of which waited for: 6 -> 6; matrix products, arithmetic and copies ran while one was open for 0% -> 0% of each run, Pallas kernels for 19% -> 20%
where the time goes in v7:
time: 98.6 us; the launch traced here: 96.8 us
  waiting for transfers between devices  50.2 us (51%)
  starting transfers between devices  23.5 us (24%)
  Pallas kernels  21.5 us (22%)
  local copies, waits for them, and re-layouts  1.36 us (1%)
    ppermute x1, waiting for transfers between devices, on_device(): relayed2 = lax.ppermute(own2, 'en', arriving)  16.6 us
    pallas_call x4, Pallas kernels, call(): pl.pallas_call(kernel, in_specs=[SMEM] * 4 + [VMEM] * 2 + [ANY] * len(ope...  14.6 us
    ppermute x1, waiting for transfers between devices, on_device(): near2 = lax.ppermute(near1, 'en', between)  11.6 us
    ppermute x1, waiting for transfers between devices, on_device(): near1 = lax.ppermute(own1, 'kz', backward)  10.7 us
    ppermute x1, waiting for transfers between devices, on_device(): arrived0 = lax.ppermute(sent0, 'kz', forward)  6.55 us
    ppermute x1, starting transfers between devices, on_device(): own2 = lax.ppermute(own1, 'en', across)  4.21 us
    ppermute x1, starting transfers between devices, on_device(): near2 = lax.ppermute(near1, 'en', between)  4.08 us
    pallas_call x3, Pallas kernels, store(): pl.pallas_call(functools.partial(store_kernel, place, half * arrived.shap...  3.51 us
  transfers between devices with their start and end apart: 13, of which 6 were waited for; matrix products, arithmetic and copies ran while one was open for 0% of the time, Pallas kernels for 20%

profile of v7, /device:TPU:3, one launch (start us, length us, event | category | flops | bytes accessed | tf_op | source)
XLA Modules:
  0.0 96.8 jit_solution(3630377074983140253)
XLA Ops:
  0.0 0.0 copy-start.2
  0.0 1.3 %take.1._.refs_8_ = bf16[2,512,512]{2,1,0:T(8,128)(2,1)S(1)} custom-call(bf16[1,2,2,512,512]{4,3,2,1,0:T(8,128)(2,1)} %green_ref.3), custom_call_target="tpu_custom_call" | custom-call | flops 1 | bytes 1 | tf_op jit(solution)/shard_map/take/pallas_call | solution.py:98
  1.3 0.0 copy-start.6
  1.4 3.4 %collective-permute-start.2 = (bf16[2,512,512]{2,1,0:T(8,128)(2,1)S(1)}, bf16[2,512,512]{2,1,0:T(8,128)(2,1)}, u32[]{:S(2)}, u32[]{:S(2)}) collective-permute-start(bf16[2,512,512]{2,1,0:T(8,128)(2,1)S(1)} %take.1._.refs_8_), channel_id=1, source_target_pairs={{0,24},{8,0},{16,8},{24,16},{1,25},{9,1},{17,9},{25,17},{2,26},{10... | collective-permute-start | bytes 3145736 | tf_op jit(solution)/shard_map/ppermute | solution.py:383
  4.7 4.2 %collective-permute-start.3 = (bf16[2,512,512]{2,1,0:T(8,128)(2,1)S(1)}, bf16[2,512,512]{2,1,0:T(8,128)(2,1)}, u32[]{:S(2)}, u32[]{:S(2)}) collective-permute-start(bf16[2,512,512]{2,1,0:T(8,128)(2,1)S(1)} %take.1._.refs_8_), channel_id=1, source_target_pairs={{1,2},{5,6},{2,1},{6,5},{3,7},{4,0},{9,10},{13,14},{10,9},{14,13},... | collective-permute-start | bytes 3145736 | tf_op jit(solution)/shard_map/ppermute | solution.py:384
  8.9 0.0 collective-permute-start.1
  8.9 0.0 copy-done.2
  8.9 2.1 %prepare.1 = (bf16[2,512,512]{2,1,0:T(8,128)(2,1)}, bf16[3,4,256,256]{3,2,1,0:T(8,128)(2,1)S(1)}, bf16[3,4,256,256]{3,2,1,0:T(8,128)(2,1)S(1)}) custom-call(bf16[1,2,2,512,512]{4,3,2,1,0:T(8,128)(2,1)} %green_ref.3, f32[3,4,2,128,128]{4,3,2,1,0:T(8,128)S(1)} %copy-done.2, bf16[2,512,512]{2,1,0:T(8,128)(2,1)S(1)} %take.1._.refs_8_), custom_call_target="tpu_custom_call" | custom-call | flops 1 | bytes 1 | tf_op jit(solution)/shard_map/prepare/pallas_call | solution.py:131
  11.0 0.0 copy-start
  11.0 1.1 %copy-done = bf16[3,4,256,256]{3,2,1,0:T(8,128)(2,1)} copy-done((bf16[3,4,256,256]{3,2,1,0:T(8,128)(2,1)}, bf16[3,4,256,256]{3,2,1,0:T(8,128)(2,1)S(1)}, u32[]{:S(2)}) %copy-start) | copy-done | bytes 1572888
  12.2 3.3 %collective-permute-start.4 = (bf16[2,512,512]{2,1,0:T(8,128)(2,1)}, bf16[2,512,512]{2,1,0:T(8,128)(2,1)}, u32[]{:S(2)}, u32[]{:S(2)}) collective-permute-start(bf16[2,512,512]{2,1,0:T(8,128)(2,1)} %get-tuple-element.12.refs_7_), channel_id=1, source_target_pairs={{1,2},{3,4},{5,6},{2,1},{4,3},{6,5},{9,10},{11,12},{13,14},{10,9},... | collective-permute-start | bytes 3145736 | tf_op jit(solution)/shard_map/ppermute | solution.py:387
  15.5 0.2 collective-permute-start
  15.7 0.0 copy-done.6
  15.7 0.1 copy.15
  15.8 0.1 reshape.3.refs_0_
  15.9 10.7 %collective-permute-done.2.refs_1_.refs_0_ = bf16[2,512,512]{2,1,0:T(8,128)(2,1)} collective-permute-done((bf16[2,512,512]{2,1,0:T(8,128)(2,1)S(1)}, bf16[2,512,512]{2,1,0:T(8,128)(2,1)}, u32[]{:S(2)}, u32[]{:S(2)}) %collective-permute-start.2) | collective-permute-done | bytes 1048608 | tf_op jit(solution)/shard_map/ppermute | solution.py:383
  26.6 0.0 collective-permute-done.3.refs_0_
  26.6 1.3 %collective-permute-start.5 = (bf16[2,512,512]{2,1,0:T(8,128)(2,1)}, bf16[2,512,512]{2,1,0:T(8,128)(2,1)}, u32[]{:S(2)}, u32[]{:S(2)}) collective-permute-start(bf16[2,512,512]{2,1,0:T(8,128)(2,1)} %after.6.refs_9_), channel_id=1, source_target_pairs={{7,4},{0,3},{15,12},{8,11},{23,20},{16,19},{31,28},{24,27}} | collective-permute-start | bytes 3145736 | tf_op jit(solution)/shard_map/ppermute | solution.py:393
  27.9 3.0 %collective-permute-start.6 = (bf16[2,512,512]{2,1,0:T(8,128)(2,1)}, bf16[2,512,512]{2,1,0:T(8,128)(2,1)}, u32[]{:S(2)}, u32[]{:S(2)}) collective-permute-start(bf16[2,512,512]{2,1,0:T(8,128)(2,1)} %collective-permute-done.2.refs_1_.refs_0_), channel_id=1, source_target_pairs={{0,1},{2,3},{4,5},{6,7},{1,0},{3,2},{5,4},{7,6},{8,9},{10,11},{12,... | collective-permute-start | bytes 3145736 | tf_op jit(solution)/shard_map/ppermute | solution.py:390
  30.9 0.0 collective-permute-done.1.refs_0_
  30.9 0.0 copy-start.5
  30.9 16.6 %collective-permute-done.5.refs_11_.refs_10_ = bf16[2,512,512]{2,1,0:T(8,128)(2,1)} collective-permute-done((bf16[2,512,512]{2,1,0:T(8,128)(2,1)}, bf16[2,512,512]{2,1,0:T(8,128)(2,1)}, u32[]{:S(2)}, u32[]{:S(2)}) %collective-permute-start.5) | collective-permute-done | bytes 1048608 | tf_op jit(solution)/shard_map/ppermute | solution.py:393
  47.6 0.0 copy-done.1
  47.6 0.0 copy-done.3
  47.6 0.0 copy-done.4
  47.6 0.0 copy-done.5
  47.6 3.1 %message0.1.refs_2_.refs_1_ = bf16[4,512,256]{2,1,0:T(8,128)(2,1)S(1)} custom-call(s32[24]{0:T(128)S(1)} %reshape.3.refs_0_, s32[3]{0:T(128)S(1)} %copy-done.3, s32[3]{0:T(128)S(1)} %copy-done.4, f32[3]{0:T(128)S(1)} %copy-done.5, bf16[3,4,256,256]{3,2,1,0:T(8,128)(2,1)S(1)} %get-tuple-element.10.refs_4_, bf16[3,4,256,256]{3,2,1,0:T(8,128)(2,1)S(1)} %copy-done.1, ...), custom_call_target="tpu_custom_call" | custom-call | flops 1 | bytes 1 | tf_op jit(solution)/shard_map/message0/pallas_call | solution.py:356
  50.8 0.0 collective-permute-done.6.refs_3_.refs_2_.refs_12_
  50.8 4.1 %collective-permute-start.9 = (bf16[2,512,512]{2,1,0:T(8,128)(2,1)}, bf16[2,512,512]{2,1,0:T(8,128)(2,1)S(1)}, u32[]{:S(2)}, u32[]{:S(2)}) collective-permute-start(bf16[2,512,512]{2,1,0:T(8,128)(2,1)} %after.8.refs_15_), channel_id=1, source_target_pairs={{1,2},{3,4},{5,6},{2,1},{4,3},{6,5},{9,10},{11,12},{13,14},{10,9},... | collective-permute-start | bytes 3145736 | tf_op jit(solution)/shard_map/ppermute | solution.py:398
  54.9 0.3 collective-permute-start.10
  55.2 0.0 collective-permute-done.4.refs_10_
  55.2 3.5 %message1.1 = (bf16[4,256,256]{2,1,0:T(8,128)(2,1)S(1)}, bf16[4,256,256]{2,1,0:T(8,128)(2,1)S(1)}) custom-call(s32[24]{0:T(128)S(1)} %reshape.3.refs_0_, s32[3]{0:T(128)S(1)} %copy-done.3, s32[3]{0:T(128)S(1)} %copy-done.4, f32[3]{0:T(128)S(1)} %copy-done.5, bf16[3,4,256,256]{3,2,1,0:T(8,128)(2,1)S(1)} %get-tuple-element.10.refs_4_, ...), custom_call_target="tpu_custom_call" | custom-call | flops 1 | bytes 1 | tf_op jit(solution)/shard_map/message1/pallas_call | solution.py:356
  58.7 0.0 collective-permute-done.refs_0_
  58.7 0.1 collective-permute-start.7
  58.8 2.2 %collective-permute-start.8 = (bf16[2,512,512]{2,1,0:T(8,128)(2,1)}, bf16[2,512,512]{2,1,0:T(8,128)(2,1)S(1)}, u32[]{:S(2)}, u32[]{:S(2)}) collective-permute-start(bf16[2,512,512]{2,1,0:T(8,128)(2,1)} %after.7.refs_14_), channel_id=1, source_target_pairs={{1,2},{3,4},{5,6},{2,1},{4,3},{6,5},{9,10},{11,12},{13,14},{10,9},... | collective-permute-start | bytes 3145736 | tf_op jit(solution)/shard_map/ppermute | solution.py:403
  61.0 1.3 %collective-permute-start.12 = (bf16[4,256,256]{2,1,0:T(8,128)(2,1)S(1)}, bf16[4,256,256]{2,1,0:T(8,128)(2,1)S(1)}, u32[]{:S(2)}, u32[]{:S(2)}) collective-permute-start(bf16[4,256,256]{2,1,0:T(8,128)(2,1)S(1)} %get-tuple-element.13.refs_1_), channel_id=1, source_target_pairs={{0,8},{8,16},{16,24},{24,0},{1,9},{9,17},{17,25},{25,1},{2,10},{10... | collective-permute-start | bytes 1572872 | tf_op jit(solution)/shard_map/ppermute | solution.py:400
  62.3 11.6 %collective-permute-done.9.refs_0_ = bf16[2,512,512]{2,1,0:T(8,128)(2,1)S(1)} collective-permute-done((bf16[2,512,512]{2,1,0:T(8,128)(2,1)}, bf16[2,512,512]{2,1,0:T(8,128)(2,1)S(1)}, u32[]{:S(2)}, u32[]{:S(2)}) %collective-permute-start.9) | collective-permute-done | bytes 1048608 | tf_op jit(solution)/shard_map/ppermute | solution.py:398
  74.0 0.0 collective-permute-start.11
  74.0 6.5 %collective-permute-done.10.refs_1_.arrived = bf16[4,512,256]{2,1,0:T(8,128)(2,1)S(1)} collective-permute-done((bf16[4,512,256]{2,1,0:T(8,128)(2,1)S(1)}, bf16[4,512,256]{2,1,0:T(8,128)(2,1)S(1)}, u32[]{:S(2)}, u32[]{:S(2)}) %collective-permute-start.10) | collective-permute-done | bytes 1048608 | tf_op jit(solution)/shard_map/ppermute | solution.py:396
  80.5 0.0 collective-permute-done.7.refs_13_.refs_6_
  80.5 5.8 %first.1.refs_8_.sum_ref = f32[2,2,512,512]{3,2,1,0:T(8,128)S(1)} custom-call(s32[24]{0:T(128)S(1)} %reshape.3.refs_0_, s32[3]{0:T(128)S(1)} %copy-done.3, s32[3]{0:T(128)S(1)} %copy-done.4, f32[3]{0:T(128)S(1)} %copy-done.5, bf16[3,4,256,256]{3,2,1,0:T(8,128)(2,1)S(1)} %get-tuple-element.10.refs_4_, bf16[3,4,256,256]{3,2,1,0:T(8,128)(2,1)S(1)} %copy-done.1, ...), custom_call_target="tpu_custom_call" | custom-call | flops 1 | bytes 1 | tf_op jit(solution)/shard_map/first/pallas_call | solution.py:356
  86.4 1.4 %store00.1.refs_0_ = f32[1,2,2,512,512]{4,3,2,1,0:T(8,128)} custom-call(f32[2,2,512,512]{3,2,1,0:T(8,128)S(1)} %first.1.refs_8_.sum_ref, bf16[4,512,256]{2,1,0:T(8,128)(2,1)S(1)} %collective-permute-done.10.refs_1_.arrived), custom_call_target="tpu_custom_call" | custom-call | flops 1 | bytes 1 | tf_op jit(solution)/shard_map/store00/pallas_call | solution.py:322
  87.8 2.7 %collective-permute-done.8.refs_7_ = bf16[2,512,512]{2,1,0:T(8,128)(2,1)S(1)} collective-permute-done((bf16[2,512,512]{2,1,0:T(8,128)(2,1)}, bf16[2,512,512]{2,1,0:T(8,128)(2,1)S(1)}, u32[]{:S(2)}, u32[]{:S(2)}) %collective-permute-start.8) | collective-permute-done | bytes 1048608 | tf_op jit(solution)/shard_map/ppermute | solution.py:403
  90.5 2.2 %second.1.sum_ref = f32[1,2,512,512]{3,2,1,0:T(8,128)S(1)} custom-call(s32[24]{0:T(128)S(1)} %reshape.3.refs_0_, s32[3]{0:T(128)S(1)} %copy-done.3, s32[3]{0:T(128)S(1)} %copy-done.4, f32[3]{0:T(128)S(1)} %copy-done.5, bf16[3,4,256,256]{3,2,1,0:T(8,128)(2,1)S(1)} %get-tuple-element.10.refs_4_, bf16[3,4,256,256]{3,2,1,0:T(8,128)(2,1)S(1)} %copy-done.1, ...), custom_call_target="tpu_custom_call" | custom-call | flops 1 | bytes 1 | tf_op jit(solution)/shard_map/second/pallas_call | solution.py:356
  92.6 0.0 collective-permute-done.12.arrived
  92.7 1.1 %store10.1.refs_0_ = f32[1,2,2,512,512]{4,3,2,1,0:T(8,128)} custom-call(f32[1,2,512,512]{3,2,1,0:T(8,128)S(1)} %second.1.sum_ref, bf16[4,256,256]{2,1,0:T(8,128)(2,1)S(1)} %collective-permute-done.12.arrived, f32[1,2,2,512,512]{4,3,2,1,0:T(8,128)} %store00.1.refs_0_), custom_call_target="tpu_custom_call", output_to_operand_aliasing={{}: (2, {})} | custom-call | flops 1 | bytes 1 | tf_op jit(solution)/shard_map/store10/pallas_call | solution.py:322
  93.7 2.0 %collective-permute-done.11.arrived = bf16[4,256,256]{2,1,0:T(8,128)(2,1)S(1)} collective-permute-done((bf16[4,256,256]{2,1,0:T(8,128)(2,1)S(1)}, bf16[4,256,256]{2,1,0:T(8,128)(2,1)S(1)}, u32[]{:S(2)}, u32[]{:S(2)}) %collective-permute-start.11) | collective-permute-done | bytes 524320 | tf_op jit(solution)/shard_map/ppermute | solution.py:401
  95.7 1.0 %store11.1 = f32[1,2,2,512,512]{4,3,2,1,0:T(8,128)} custom-call(f32[1,2,512,512]{3,2,1,0:T(8,128)S(1)} %second.1.sum_ref, bf16[4,256,256]{2,1,0:T(8,128)(2,1)S(1)} %collective-permute-done.11.arrived, f32[1,2,2,512,512]{4,3,2,1,0:T(8,128)} %store10.1.refs_0_), custom_call_target="tpu_custom_call", output_to_operand_aliasing={{}: (2, {})} | custom-call | flops 1 | bytes 1 | tf_op jit(solution)/shard_map/store11/pallas_call | solution.py:322
  (8 shorter events, 0.0 us)
Async XLA Ops:
  0.0 8.9 %copy-start.2 = (f32[3,4,2,128,128]{4,3,2,1,0:T(8,128)S(1)}, f32[3,4,2,128,128]{4,3,2,1,0:T(8,128)}, u32[]{:S(2)}) copy-start(f32[3,4,2,128,128]{4,3,2,1,0:T(8,128)} %coupling_ref.1) | copy-start | bytes 4718596
  1.3 14.4 %copy-start.6 = (s32[3,4,2]{1,2,0:T(2,128)S(1)}, s32[3,4,2]{1,2,0:T(2,128)}, u32[]{:S(2)}) copy-start(s32[3,4,2]{1,2,0:T(2,128)} %param.8) | copy-start | bytes 292
  1.4 25.2 %collective-permute-start.2 = (bf16[2,512,512]{2,1,0:T(8,128)(2,1)S(1)}, bf16[2,512,512]{2,1,0:T(8,128)(2,1)}, u32[]{:S(2)}, u32[]{:S(2)}) collective-permute-start(bf16[2,512,512]{2,1,0:T(8,128)(2,1)S(1)} %take.1._.refs_8_), channel_id=1, source_target_pairs={{0,24},{8,0},{16,8},{24,16},{1,25},{9,1},{17,9},{25,17},{2,26},{10... | collective-permute-start | bytes 3145736 | tf_op jit(solution)/shard_map/ppermute | solution.py:383
  4.7 21.8 %collective-permute-start.3 = (bf16[2,512,512]{2,1,0:T(8,128)(2,1)S(1)}, bf16[2,512,512]{2,1,0:T(8,128)(2,1)}, u32[]{:S(2)}, u32[]{:S(2)}) collective-permute-start(bf16[2,512,512]{2,1,0:T(8,128)(2,1)S(1)} %take.1._.refs_8_), channel_id=1, source_target_pairs={{1,2},{5,6},{2,1},{6,5},{3,7},{4,0},{9,10},{13,14},{10,9},{14,13},... | collective-permute-start | bytes 3145736 | tf_op jit(solution)/shard_map/ppermute | solution.py:384
  8.9 22.0 %collective-permute-start.1 = (bf16[1,2,2,512,512]{4,3,2,1,0:T(8,128)(2,1)}, bf16[1,2,2,512,512]{4,3,2,1,0:T(8,128)(2,1)}, u32[]{:S(2)}, u32[]{:S(2)}) collective-permute-start(bf16[1,2,2,512,512]{4,3,2,1,0:T(8,128)(2,1)} %green_ref.3), channel_id=1, source_target_pairs={{0,1},{2,3},{4,5},{6,7},{1,0},{3,2},{5,4},{7,6},{8,9},{10,11},{12,... | collective-permute-start | bytes 6291464 | tf_op jit(solution)/shard_map/ppermute | solution.py:388
  11.0 1.1 %copy-start = (bf16[3,4,256,256]{3,2,1,0:T(8,128)(2,1)}, bf16[3,4,256,256]{3,2,1,0:T(8,128)(2,1)S(1)}, u32[]{:S(2)}) copy-start(bf16[3,4,256,256]{3,2,1,0:T(8,128)(2,1)S(1)} %get-tuple-element.11.refs_5_) | copy-start | bytes 4718596
  12.2 43.0 %collective-permute-start.4 = (bf16[2,512,512]{2,1,0:T(8,128)(2,1)}, bf16[2,512,512]{2,1,0:T(8,128)(2,1)}, u32[]{:S(2)}, u32[]{:S(2)}) collective-permute-start(bf16[2,512,512]{2,1,0:T(8,128)(2,1)} %get-tuple-element.12.refs_7_), channel_id=1, source_target_pairs={{1,2},{3,4},{5,6},{2,1},{4,3},{6,5},{9,10},{11,12},{13,14},{10,9},... | collective-permute-start | bytes 3145736 | tf_op jit(solution)/shard_map/ppermute | solution.py:387
  15.5 43.2 %collective-permute-start = (bf16[2,512,512]{2,1,0:T(8,128)(2,1)}, bf16[2,512,512]{2,1,0:T(8,128)(2,1)}, u32[]{:S(2)}, u32[]{:S(2)}) collective-permute-start(bf16[2,512,512]{2,1,0:T(8,128)(2,1)} %get-tuple-element.12.refs_7_), channel_id=1, source_target_pairs={{0,24},{8,0},{16,8},{24,16},{1,25},{9,1},{17,9},{25,17},{2,26},{10... | collective-permute-start | bytes 3145736 | tf_op jit(solution)/shard_map/ppermute | solution.py:386
  26.6 21.0 %collective-permute-start.5 = (bf16[2,512,512]{2,1,0:T(8,128)(2,1)}, bf16[2,512,512]{2,1,0:T(8,128)(2,1)}, u32[]{:S(2)}, u32[]{:S(2)}) collective-permute-start(bf16[2,512,512]{2,1,0:T(8,128)(2,1)} %after.6.refs_9_), channel_id=1, source_target_pairs={{7,4},{0,3},{15,12},{8,11},{23,20},{16,19},{31,28},{24,27}} | collective-permute-start | bytes 3145736 | tf_op jit(solution)/shard_map/ppermute | solution.py:393
  27.9 22.9 %collective-permute-start.6 = (bf16[2,512,512]{2,1,0:T(8,128)(2,1)}, bf16[2,512,512]{2,1,0:T(8,128)(2,1)}, u32[]{:S(2)}, u32[]{:S(2)}) collective-permute-start(bf16[2,512,512]{2,1,0:T(8,128)(2,1)} %collective-permute-done.2.refs_1_.refs_0_), channel_id=1, source_target_pairs={{0,1},{2,3},{4,5},{6,7},{1,0},{3,2},{5,4},{7,6},{8,9},{10,11},{12,... | collective-permute-start | bytes 3145736 | tf_op jit(solution)/shard_map/ppermute | solution.py:390
  30.9 16.7 %copy-start.1 = (bf16[3,4,256,256]{3,2,1,0:T(8,128)(2,1)S(1)}, bf16[3,4,256,256]{3,2,1,0:T(8,128)(2,1)}, u32[]{:S(2)}) copy-start(bf16[3,4,256,256]{3,2,1,0:T(8,128)(2,1)} %copy-done) | copy-start | bytes 4718596
  30.9 16.7 %copy-start.3 = (s32[3]{0:T(128)S(1)}, s32[3]{0:T(128)}, u32[]{:S(2)}) copy-start(s32[3]{0:T(128)} %refs_1_.7) | copy-start | bytes 40
  30.9 16.7 %copy-start.4 = (s32[3]{0:T(128)S(1)}, s32[3]{0:T(128)}, u32[]{:S(2)}) copy-start(s32[3]{0:T(128)} %refs_2_.7) | copy-start | bytes 40
  30.9 16.7 %copy-start.5 = (f32[3]{0:T(128)S(1)}, f32[3]{0:T(128)}, u32[]{:S(2)}) copy-start(f32[3]{0:T(128)} %refs_3_.7) | copy-start | bytes 40
  50.8 23.2 %collective-permute-start.9 = (bf16[2,512,512]{2,1,0:T(8,128)(2,1)}, bf16[2,512,512]{2,1,0:T(8,128)(2,1)S(1)}, u32[]{:S(2)}, u32[]{:S(2)}) collective-permute-start(bf16[2,512,512]{2,1,0:T(8,128)(2,1)} %after.8.refs_15_), channel_id=1, source_target_pairs={{1,2},{3,4},{5,6},{2,1},{4,3},{6,5},{9,10},{11,12},{13,14},{10,9},... | collective-permute-start | bytes 3145736 | tf_op jit(solution)/shard_map/ppermute | solution.py:398
  54.9 25.7 %collective-permute-start.10 = (bf16[4,512,256]{2,1,0:T(8,128)(2,1)S(1)}, bf16[4,512,256]{2,1,0:T(8,128)(2,1)S(1)}, u32[]{:S(2)}, u32[]{:S(2)}) collective-permute-start(bf16[4,512,256]{2,1,0:T(8,128)(2,1)S(1)} %message0.1.refs_2_.refs_1_), channel_id=1, source_target_pairs={{0,8},{8,16},{16,24},{24,0},{1,9},{9,17},{17,25},{25,1},{2,10},{10... | collective-permute-start | bytes 3145736 | tf_op jit(solution)/shard_map/ppermute | solution.py:396
  58.7 21.9 %collective-permute-start.7 = (bf16[2,512,512]{2,1,0:T(8,128)(2,1)}, bf16[2,512,512]{2,1,0:T(8,128)(2,1)S(1)}, u32[]{:S(2)}, u32[]{:S(2)}) collective-permute-start(bf16[2,512,512]{2,1,0:T(8,128)(2,1)} %after.7.refs_14_), channel_id=1, source_target_pairs={{0,1},{2,3},{4,5},{6,7},{1,0},{3,2},{5,4},{7,6},{8,9},{10,11},{12,... | collective-permute-start | bytes 3145736 | tf_op jit(solution)/shard_map/ppermute | solution.py:404
  58.8 31.7 %collective-permute-start.8 = (bf16[2,512,512]{2,1,0:T(8,128)(2,1)}, bf16[2,512,512]{2,1,0:T(8,128)(2,1)S(1)}, u32[]{:S(2)}, u32[]{:S(2)}) collective-permute-start(bf16[2,512,512]{2,1,0:T(8,128)(2,1)} %after.7.refs_14_), channel_id=1, source_target_pairs={{1,2},{3,4},{5,6},{2,1},{4,3},{6,5},{9,10},{11,12},{13,14},{10,9},... | collective-permute-start | bytes 3145736 | tf_op jit(solution)/shard_map/ppermute | solution.py:403
  61.0 31.6 %collective-permute-start.12 = (bf16[4,256,256]{2,1,0:T(8,128)(2,1)S(1)}, bf16[4,256,256]{2,1,0:T(8,128)(2,1)S(1)}, u32[]{:S(2)}, u32[]{:S(2)}) collective-permute-start(bf16[4,256,256]{2,1,0:T(8,128)(2,1)S(1)} %get-tuple-element.13.refs_1_), channel_id=1, source_target_pairs={{0,8},{8,16},{16,24},{24,0},{1,9},{9,17},{17,25},{25,1},{2,10},{10... | collective-permute-start | bytes 1572872 | tf_op jit(solution)/shard_map/ppermute | solution.py:400
  74.0 21.7 %collective-permute-start.11 = (bf16[4,256,256]{2,1,0:T(8,128)(2,1)S(1)}, bf16[4,256,256]{2,1,0:T(8,128)(2,1)S(1)}, u32[]{:S(2)}, u32[]{:S(2)}) collective-permute-start(bf16[4,256,256]{2,1,0:T(8,128)(2,1)S(1)} %get-tuple-element.14), channel_id=1, source_target_pairs={{0,8},{8,16},{16,24},{24,0},{1,9},{9,17},{17,25},{25,1},{2,10},{10... | collective-permute-start | bytes 1572872 | tf_op jit(solution)/shard_map/ppermute | solution.py:401

commit v8 on v7

--- a/solution.py
+++ b/solution.py
@@ -83,15 +83,10 @@
     return [pltpu.VMEM(green.shape[2:], green.dtype), pltpu.SemaphoreType.DMA((2, 2 * PIECES))]
 
 
-def take_kernel(green_ref, out_ref, sems):
-    copies = []
-    for i, (part, here) in enumerate(pieces_of(out_ref, PIECES)):
-        copies.append(
-            pltpu.make_async_copy(green_ref.at[0, odd(), part, here, :], out_ref.at[part, here, :], sems.at[i])
-        )
-        copies[-1].start()
-    for copy in copies:
-        copy.wait()
+def take_kernel(green_ref, out_ref, sem):
+    copy = pltpu.make_async_copy(green_ref.at[0, odd()], out_ref, sem)
+    copy.start()
+    copy.wait()
 
 
 def take(green):
@@ -100,7 +95,7 @@
         in_specs=[ANY],
         out_specs=VMEM,
         out_shape=pltpu.VMEM(green.shape[2:], green.dtype),
-        scratch_shapes=[pltpu.SemaphoreType.DMA((2 * PIECES,))],
+        scratch_shapes=[pltpu.SemaphoreType.DMA],
         compiler_params=SMALL,
         cost_estimate=CHEAP,
         name="take",

time: 98.6 us -> 98.6 us (level)
    ppermute x1, waiting for transfers between devices: 2.7 us -> 5.04 us  [on_device(): near3 = lax.ppermute(near0, 'en', between)]
    ppermute x1, waiting for transfers between devices: 11.6 us -> 9.35 us  [on_device(): near2 = lax.ppermute(near1, 'en', between)]
    ppermute x1, waiting for transfers between devices: 2.02 us -> 3.4 us  [on_device(): arrived2 = lax.ppermute(sent2, 'kz', forward)]
    ppermute x1, waiting for transfers between devices: 16.6 us -> 15.5 us  [on_device(): relayed2 = lax.ppermute(own2, 'en', arriving)]
  transfers between devices with their start and end apart: 13 -> 13, of which waited for: 6 -> 6; matrix products, arithmetic and copies ran while one was open for 0% -> 0% of each run, Pallas kernels for 20% -> 19%
where the time goes in v8:
time: 98.6 us; the launch traced here: 96.8 us
  waiting for transfers between devices  50.5 us (51%)
  starting transfers between devices  23.5 us (24%)
  Pallas kernels  21.2 us (22%)
  local copies, waits for them, and re-layouts  1.36 us (1%)
    ppermute x1, waiting for transfers between devices, on_device(): relayed2 = lax.ppermute(own2, 'en', arriving)  15.5 us
    pallas_call x4, Pallas kernels, call(): pl.pallas_call(kernel, in_specs=[SMEM] * 4 + [VMEM] * 2 + [ANY] * len(ope...  14.3 us
    ppermute x1, waiting for transfers between devices, on_device(): near1 = lax.ppermute(own1, 'kz', backward)  10.7 us
    ppermute x1, waiting for transfers between devices, on_device(): near2 = lax.ppermute(near1, 'en', between)  9.35 us
    ppermute x1, waiting for transfers between devices, on_device(): arrived0 = lax.ppermute(sent0, 'kz', forward)  6.53 us
    ppermute x1, waiting for transfers between devices, on_device(): near3 = lax.ppermute(near0, 'en', between)  5.04 us
    ppermute x1, starting transfers between devices, on_device(): own2 = lax.ppermute(own1, 'en', across)  4.21 us
    ppermute x1, starting transfers between devices, on_device(): near2 = lax.ppermute(near1, 'en', between)  4.07 us
  transfers between devices with their start and end apart: 13, of which 6 were waited for; matrix products, arithmetic and copies ran while one was open for 0% of the time, Pallas kernels for 19%

profile of v8, /device:TPU:3, one launch (start us, length us, event | category | flops | bytes accessed | tf_op | source)
XLA Modules:
  0.0 96.8 jit_solution(17604984894090920731)
XLA Ops:
  0.0 0.0 copy-start.2
  0.0 1.4 %take.1._.refs_8_ = bf16[2,512,512]{2,1,0:T(8,128)(2,1)S(1)} custom-call(bf16[1,2,2,512,512]{4,3,2,1,0:T(8,128)(2,1)} %green_ref.3), custom_call_target="tpu_custom_call" | custom-call | flops 1 | bytes 1 | tf_op jit(solution)/shard_map/take/pallas_call | solution.py:93
  1.4 0.0 copy-start.6
  1.4 3.4 %collective-permute-start.2 = (bf16[2,512,512]{2,1,0:T(8,128)(2,1)S(1)}, bf16[2,512,512]{2,1,0:T(8,128)(2,1)}, u32[]{:S(2)}, u32[]{:S(2)}) collective-permute-start(bf16[2,512,512]{2,1,0:T(8,128)(2,1)S(1)} %take.1._.refs_8_), channel_id=1, source_target_pairs={{0,24},{8,0},{16,8},{24,16},{1,25},{9,1},{17,9},{25,17},{2,26},{10... | collective-permute-start | bytes 3145736 | tf_op jit(solution)/shard_map/ppermute | solution.py:378
  4.7 4.2 %collective-permute-start.3 = (bf16[2,512,512]{2,1,0:T(8,128)(2,1)S(1)}, bf16[2,512,512]{2,1,0:T(8,128)(2,1)}, u32[]{:S(2)}, u32[]{:S(2)}) collective-permute-start(bf16[2,512,512]{2,1,0:T(8,128)(2,1)S(1)} %take.1._.refs_8_), channel_id=1, source_target_pairs={{1,2},{5,6},{2,1},{6,5},{3,7},{4,0},{9,10},{13,14},{10,9},{14,13},... | collective-permute-start | bytes 3145736 | tf_op jit(solution)/shard_map/ppermute | solution.py:379
  9.0 0.0 collective-permute-start.1
  9.0 0.0 copy-done.2
  9.0 2.1 %prepare.1 = (bf16[2,512,512]{2,1,0:T(8,128)(2,1)}, bf16[3,4,256,256]{3,2,1,0:T(8,128)(2,1)S(1)}, bf16[3,4,256,256]{3,2,1,0:T(8,128)(2,1)S(1)}) custom-call(bf16[1,2,2,512,512]{4,3,2,1,0:T(8,128)(2,1)} %green_ref.3, f32[3,4,2,128,128]{4,3,2,1,0:T(8,128)S(1)} %copy-done.2, bf16[2,512,512]{2,1,0:T(8,128)(2,1)S(1)} %take.1._.refs_8_), custom_call_target="tpu_custom_call" | custom-call | flops 1 | bytes 1 | tf_op jit(solution)/shard_map/prepare/pallas_call | solution.py:126
  11.0 0.0 copy-start
  11.0 1.1 %copy-done = bf16[3,4,256,256]{3,2,1,0:T(8,128)(2,1)} copy-done((bf16[3,4,256,256]{3,2,1,0:T(8,128)(2,1)}, bf16[3,4,256,256]{3,2,1,0:T(8,128)(2,1)S(1)}, u32[]{:S(2)}) %copy-start) | copy-done | bytes 1572888
  12.2 3.3 %collective-permute-start.4 = (bf16[2,512,512]{2,1,0:T(8,128)(2,1)}, bf16[2,512,512]{2,1,0:T(8,128)(2,1)}, u32[]{:S(2)}, u32[]{:S(2)}) collective-permute-start(bf16[2,512,512]{2,1,0:T(8,128)(2,1)} %get-tuple-element.12.refs_7_), channel_id=1, source_target_pairs={{1,2},{3,4},{5,6},{2,1},{4,3},{6,5},{9,10},{11,12},{13,14},{10,9},... | collective-permute-start | bytes 3145736 | tf_op jit(solution)/shard_map/ppermute | solution.py:382
  15.5 0.2 collective-permute-start
  15.7 0.0 copy-done.6
  15.7 0.1 copy.15
  15.8 0.1 reshape.3.refs_0_
  15.9 10.7 %collective-permute-done.2.refs_1_.refs_0_ = bf16[2,512,512]{2,1,0:T(8,128)(2,1)} collective-permute-done((bf16[2,512,512]{2,1,0:T(8,128)(2,1)S(1)}, bf16[2,512,512]{2,1,0:T(8,128)(2,1)}, u32[]{:S(2)}, u32[]{:S(2)}) %collective-permute-start.2) | collective-permute-done | bytes 1048608 | tf_op jit(solution)/shard_map/ppermute | solution.py:378
  26.6 0.0 collective-permute-done.3.refs_0_
  26.6 1.3 %collective-permute-start.5 = (bf16[2,512,512]{2,1,0:T(8,128)(2,1)}, bf16[2,512,512]{2,1,0:T(8,128)(2,1)}, u32[]{:S(2)}, u32[]{:S(2)}) collective-permute-start(bf16[2,512,512]{2,1,0:T(8,128)(2,1)} %after.6.refs_9_), channel_id=1, source_target_pairs={{7,4},{0,3},{15,12},{8,11},{23,20},{16,19},{31,28},{24,27}} | collective-permute-start | bytes 3145736 | tf_op jit(solution)/shard_map/ppermute | solution.py:388
  27.9 3.0 %collective-permute-start.6 = (bf16[2,512,512]{2,1,0:T(8,128)(2,1)}, bf16[2,512,512]{2,1,0:T(8,128)(2,1)}, u32[]{:S(2)}, u32[]{:S(2)}) collective-permute-start(bf16[2,512,512]{2,1,0:T(8,128)(2,1)} %collective-permute-done.2.refs_1_.refs_0_), channel_id=1, source_target_pairs={{0,1},{2,3},{4,5},{6,7},{1,0},{3,2},{5,4},{7,6},{8,9},{10,11},{12,... | collective-permute-start | bytes 3145736 | tf_op jit(solution)/shard_map/ppermute | solution.py:385
  30.9 0.0 collective-permute-done.1.refs_0_
  30.9 0.0 copy-start.5
  31.0 15.5 %collective-permute-done.5.refs_11_.refs_10_ = bf16[2,512,512]{2,1,0:T(8,128)(2,1)} collective-permute-done((bf16[2,512,512]{2,1,0:T(8,128)(2,1)}, bf16[2,512,512]{2,1,0:T(8,128)(2,1)}, u32[]{:S(2)}, u32[]{:S(2)}) %collective-permute-start.5) | collective-permute-done | bytes 1048608 | tf_op jit(solution)/shard_map/ppermute | solution.py:388
  46.5 0.0 copy-done.1
  46.5 0.0 copy-done.3
  46.5 0.0 copy-done.4
  46.5 0.0 copy-done.5
  46.5 4.3 %message0.1.refs_2_.refs_1_ = bf16[4,512,256]{2,1,0:T(8,128)(2,1)S(1)} custom-call(s32[24]{0:T(128)S(1)} %reshape.3.refs_0_, s32[3]{0:T(128)S(1)} %copy-done.3, s32[3]{0:T(128)S(1)} %copy-done.4, f32[3]{0:T(128)S(1)} %copy-done.5, bf16[3,4,256,256]{3,2,1,0:T(8,128)(2,1)S(1)} %get-tuple-element.10.refs_4_, bf16[3,4,256,256]{3,2,1,0:T(8,128)(2,1)S(1)} %copy-done.1, ...), custom_call_target="tpu_custom_call" | custom-call | flops 1 | bytes 1 | tf_op jit(solution)/shard_map/message0/pallas_call | solution.py:351
  50.8 0.0 collective-permute-done.6.refs_3_.refs_2_.refs_12_
  50.8 4.1 %collective-permute-start.9 = (bf16[2,512,512]{2,1,0:T(8,128)(2,1)}, bf16[2,512,512]{2,1,0:T(8,128)(2,1)S(1)}, u32[]{:S(2)}, u32[]{:S(2)}) collective-permute-start(bf16[2,512,512]{2,1,0:T(8,128)(2,1)} %after.8.refs_15_), channel_id=1, source_target_pairs={{1,2},{3,4},{5,6},{2,1},{4,3},{6,5},{9,10},{11,12},{13,14},{10,9},... | collective-permute-start | bytes 3145736 | tf_op jit(solution)/shard_map/ppermute | solution.py:393
  54.9 0.3 collective-permute-start.10
  55.2 0.0 collective-permute-done.4.refs_10_
  55.2 4.6 %message1.1 = (bf16[4,256,256]{2,1,0:T(8,128)(2,1)S(1)}, bf16[4,256,256]{2,1,0:T(8,128)(2,1)S(1)}) custom-call(s32[24]{0:T(128)S(1)} %reshape.3.refs_0_, s32[3]{0:T(128)S(1)} %copy-done.3, s32[3]{0:T(128)S(1)} %copy-done.4, f32[3]{0:T(128)S(1)} %copy-done.5, bf16[3,4,256,256]{3,2,1,0:T(8,128)(2,1)S(1)} %get-tuple-element.10.refs_4_, ...), custom_call_target="tpu_custom_call" | custom-call | flops 1 | bytes 1 | tf_op jit(solution)/shard_map/message1/pallas_call | solution.py:351
  59.8 0.0 collective-permute-done.refs_0_
  59.9 0.1 collective-permute-start.7
  59.9 2.2 %collective-permute-start.8 = (bf16[2,512,512]{2,1,0:T(8,128)(2,1)}, bf16[2,512,512]{2,1,0:T(8,128)(2,1)S(1)}, u32[]{:S(2)}, u32[]{:S(2)}) collective-permute-start(bf16[2,512,512]{2,1,0:T(8,128)(2,1)} %after.7.refs_14_), channel_id=1, source_target_pairs={{1,2},{3,4},{5,6},{2,1},{4,3},{6,5},{9,10},{11,12},{13,14},{10,9},... | collective-permute-start | bytes 3145736 | tf_op jit(solution)/shard_map/ppermute | solution.py:398
  62.2 1.3 %collective-permute-start.12 = (bf16[4,256,256]{2,1,0:T(8,128)(2,1)S(1)}, bf16[4,256,256]{2,1,0:T(8,128)(2,1)S(1)}, u32[]{:S(2)}, u32[]{:S(2)}) collective-permute-start(bf16[4,256,256]{2,1,0:T(8,128)(2,1)S(1)} %get-tuple-element.13.refs_1_), channel_id=1, source_target_pairs={{0,8},{8,16},{16,24},{24,0},{1,9},{9,17},{17,25},{25,1},{2,10},{10... | collective-permute-start | bytes 1572872 | tf_op jit(solution)/shard_map/ppermute | solution.py:395
  63.5 9.4 %collective-permute-done.9.refs_0_ = bf16[2,512,512]{2,1,0:T(8,128)(2,1)S(1)} collective-permute-done((bf16[2,512,512]{2,1,0:T(8,128)(2,1)}, bf16[2,512,512]{2,1,0:T(8,128)(2,1)S(1)}, u32[]{:S(2)}, u32[]{:S(2)}) %collective-permute-start.9) | collective-permute-done | bytes 1048608 | tf_op jit(solution)/shard_map/ppermute | solution.py:393
  72.9 0.0 collective-permute-start.11
  72.9 6.5 %collective-permute-done.10.refs_1_.arrived = bf16[4,512,256]{2,1,0:T(8,128)(2,1)S(1)} collective-permute-done((bf16[4,512,256]{2,1,0:T(8,128)(2,1)S(1)}, bf16[4,512,256]{2,1,0:T(8,128)(2,1)S(1)}, u32[]{:S(2)}, u32[]{:S(2)}) %collective-permute-start.10) | collective-permute-done | bytes 1048608 | tf_op jit(solution)/shard_map/ppermute | solution.py:391
  79.4 0.0 collective-permute-done.7.refs_13_.refs_6_
  79.4 4.6 %first.1.refs_8_.sum_ref = f32[2,2,512,512]{3,2,1,0:T(8,128)S(1)} custom-call(s32[24]{0:T(128)S(1)} %reshape.3.refs_0_, s32[3]{0:T(128)S(1)} %copy-done.3, s32[3]{0:T(128)S(1)} %copy-done.4, f32[3]{0:T(128)S(1)} %copy-done.5, bf16[3,4,256,256]{3,2,1,0:T(8,128)(2,1)S(1)} %get-tuple-element.10.refs_4_, bf16[3,4,256,256]{3,2,1,0:T(8,128)(2,1)S(1)} %copy-done.1, ...), custom_call_target="tpu_custom_call" | custom-call | flops 1 | bytes 1 | tf_op jit(solution)/shard_map/first/pallas_call | solution.py:351
  84.0 1.4 %store00.1.refs_0_ = f32[1,2,2,512,512]{4,3,2,1,0:T(8,128)} custom-call(f32[2,2,512,512]{3,2,1,0:T(8,128)S(1)} %first.1.refs_8_.sum_ref, bf16[4,512,256]{2,1,0:T(8,128)(2,1)S(1)} %collective-permute-done.10.refs_1_.arrived), custom_call_target="tpu_custom_call" | custom-call | flops 1 | bytes 1 | tf_op jit(solution)/shard_map/store00/pallas_call | solution.py:317
  85.5 5.0 %collective-permute-done.8.refs_7_ = bf16[2,512,512]{2,1,0:T(8,128)(2,1)S(1)} collective-permute-done((bf16[2,512,512]{2,1,0:T(8,128)(2,1)}, bf16[2,512,512]{2,1,0:T(8,128)(2,1)S(1)}, u32[]{:S(2)}, u32[]{:S(2)}) %collective-permute-start.8) | collective-permute-done | bytes 1048608 | tf_op jit(solution)/shard_map/ppermute | solution.py:398
  90.5 0.8 second.1.sum_ref
  91.3 0.0 collective-permute-done.12.arrived
  91.3 1.1 %store10.1.refs_0_ = f32[1,2,2,512,512]{4,3,2,1,0:T(8,128)} custom-call(f32[1,2,512,512]{3,2,1,0:T(8,128)S(1)} %second.1.sum_ref, bf16[4,256,256]{2,1,0:T(8,128)(2,1)S(1)} %collective-permute-done.12.arrived, f32[1,2,2,512,512]{4,3,2,1,0:T(8,128)} %store00.1.refs_0_), custom_call_target="tpu_custom_call", output_to_operand_aliasing={{}: (2, {})} | custom-call | flops 1 | bytes 1 | tf_op jit(solution)/shard_map/store10/pallas_call | solution.py:317
  92.4 3.4 %collective-permute-done.11.arrived = bf16[4,256,256]{2,1,0:T(8,128)(2,1)S(1)} collective-permute-done((bf16[4,256,256]{2,1,0:T(8,128)(2,1)S(1)}, bf16[4,256,256]{2,1,0:T(8,128)(2,1)S(1)}, u32[]{:S(2)}, u32[]{:S(2)}) %collective-permute-start.11) | collective-permute-done | bytes 524320 | tf_op jit(solution)/shard_map/ppermute | solution.py:396
  95.7 1.0 %store11.1 = f32[1,2,2,512,512]{4,3,2,1,0:T(8,128)} custom-call(f32[1,2,512,512]{3,2,1,0:T(8,128)S(1)} %second.1.sum_ref, bf16[4,256,256]{2,1,0:T(8,128)(2,1)S(1)} %collective-permute-done.11.arrived, f32[1,2,2,512,512]{4,3,2,1,0:T(8,128)} %store10.1.refs_0_), custom_call_target="tpu_custom_call", output_to_operand_aliasing={{}: (2, {})} | custom-call | flops 1 | bytes 1 | tf_op jit(solution)/shard_map/store11/pallas_call | solution.py:317
  (8 shorter events, 0.0 us)
Async XLA Ops:
  0.0 9.0 %copy-start.2 = (f32[3,4,2,128,128]{4,3,2,1,0:T(8,128)S(1)}, f32[3,4,2,128,128]{4,3,2,1,0:T(8,128)}, u32[]{:S(2)}) copy-start(f32[3,4,2,128,128]{4,3,2,1,0:T(8,128)} %coupling_ref.1) | copy-start | bytes 4718596
  1.4 14.4 %copy-start.6 = (s32[3,4,2]{1,2,0:T(2,128)S(1)}, s32[3,4,2]{1,2,0:T(2,128)}, u32[]{:S(2)}) copy-start(s32[3,4,2]{1,2,0:T(2,128)} %param.8) | copy-start | bytes 292
  1.4 25.2 %collective-permute-start.2 = (bf16[2,512,512]{2,1,0:T(8,128)(2,1)S(1)}, bf16[2,512,512]{2,1,0:T(8,128)(2,1)}, u32[]{:S(2)}, u32[]{:S(2)}) collective-permute-start(bf16[2,512,512]{2,1,0:T(8,128)(2,1)S(1)} %take.1._.refs_8_), channel_id=1, source_target_pairs={{0,24},{8,0},{16,8},{24,16},{1,25},{9,1},{17,9},{25,17},{2,26},{10... | collective-permute-start | bytes 3145736 | tf_op jit(solution)/shard_map/ppermute | solution.py:378
  4.7 21.8 %collective-permute-start.3 = (bf16[2,512,512]{2,1,0:T(8,128)(2,1)S(1)}, bf16[2,512,512]{2,1,0:T(8,128)(2,1)}, u32[]{:S(2)}, u32[]{:S(2)}) collective-permute-start(bf16[2,512,512]{2,1,0:T(8,128)(2,1)S(1)} %take.1._.refs_8_), channel_id=1, source_target_pairs={{1,2},{5,6},{2,1},{6,5},{3,7},{4,0},{9,10},{13,14},{10,9},{14,13},... | collective-permute-start | bytes 3145736 | tf_op jit(solution)/shard_map/ppermute | solution.py:379
  9.0 22.0 %collective-permute-start.1 = (bf16[1,2,2,512,512]{4,3,2,1,0:T(8,128)(2,1)}, bf16[1,2,2,512,512]{4,3,2,1,0:T(8,128)(2,1)}, u32[]{:S(2)}, u32[]{:S(2)}) collective-permute-start(bf16[1,2,2,512,512]{4,3,2,1,0:T(8,128)(2,1)} %green_ref.3), channel_id=1, source_target_pairs={{0,1},{2,3},{4,5},{6,7},{1,0},{3,2},{5,4},{7,6},{8,9},{10,11},{12,... | collective-permute-start | bytes 6291464 | tf_op jit(solution)/shard_map/ppermute | solution.py:383
  11.0 1.1 %copy-start = (bf16[3,4,256,256]{3,2,1,0:T(8,128)(2,1)}, bf16[3,4,256,256]{3,2,1,0:T(8,128)(2,1)S(1)}, u32[]{:S(2)}) copy-start(bf16[3,4,256,256]{3,2,1,0:T(8,128)(2,1)S(1)} %get-tuple-element.11.refs_5_) | copy-start | bytes 4718596
  12.2 43.0 %collective-permute-start.4 = (bf16[2,512,512]{2,1,0:T(8,128)(2,1)}, bf16[2,512,512]{2,1,0:T(8,128)(2,1)}, u32[]{:S(2)}, u32[]{:S(2)}) collective-permute-start(bf16[2,512,512]{2,1,0:T(8,128)(2,1)} %get-tuple-element.12.refs_7_), channel_id=1, source_target_pairs={{1,2},{3,4},{5,6},{2,1},{4,3},{6,5},{9,10},{11,12},{13,14},{10,9},... | collective-permute-start | bytes 3145736 | tf_op jit(solution)/shard_map/ppermute | solution.py:382
  15.5 44.4 %collective-permute-start = (bf16[2,512,512]{2,1,0:T(8,128)(2,1)}, bf16[2,512,512]{2,1,0:T(8,128)(2,1)}, u32[]{:S(2)}, u32[]{:S(2)}) collective-permute-start(bf16[2,512,512]{2,1,0:T(8,128)(2,1)} %get-tuple-element.12.refs_7_), channel_id=1, source_target_pairs={{0,24},{8,0},{16,8},{24,16},{1,25},{9,1},{17,9},{25,17},{2,26},{10... | collective-permute-start | bytes 3145736 | tf_op jit(solution)/shard_map/ppermute | solution.py:381
  26.6 19.9 %collective-permute-start.5 = (bf16[2,512,512]{2,1,0:T(8,128)(2,1)}, bf16[2,512,512]{2,1,0:T(8,128)(2,1)}, u32[]{:S(2)}, u32[]{:S(2)}) collective-permute-start(bf16[2,512,512]{2,1,0:T(8,128)(2,1)} %after.6.refs_9_), channel_id=1, source_target_pairs={{7,4},{0,3},{15,12},{8,11},{23,20},{16,19},{31,28},{24,27}} | collective-permute-start | bytes 3145736 | tf_op jit(solution)/shard_map/ppermute | solution.py:388
  27.9 22.9 %collective-permute-start.6 = (bf16[2,512,512]{2,1,0:T(8,128)(2,1)}, bf16[2,512,512]{2,1,0:T(8,128)(2,1)}, u32[]{:S(2)}, u32[]{:S(2)}) collective-permute-start(bf16[2,512,512]{2,1,0:T(8,128)(2,1)} %collective-permute-done.2.refs_1_.refs_0_), channel_id=1, source_target_pairs={{0,1},{2,3},{4,5},{6,7},{1,0},{3,2},{5,4},{7,6},{8,9},{10,11},{12,... | collective-permute-start | bytes 3145736 | tf_op jit(solution)/shard_map/ppermute | solution.py:385
  30.9 15.5 %copy-start.1 = (bf16[3,4,256,256]{3,2,1,0:T(8,128)(2,1)S(1)}, bf16[3,4,256,256]{3,2,1,0:T(8,128)(2,1)}, u32[]{:S(2)}) copy-start(bf16[3,4,256,256]{3,2,1,0:T(8,128)(2,1)} %copy-done) | copy-start | bytes 4718596
  30.9 15.5 %copy-start.3 = (s32[3]{0:T(128)S(1)}, s32[3]{0:T(128)}, u32[]{:S(2)}) copy-start(s32[3]{0:T(128)} %refs_1_.7) | copy-start | bytes 40
  30.9 15.5 %copy-start.4 = (s32[3]{0:T(128)S(1)}, s32[3]{0:T(128)}, u32[]{:S(2)}) copy-start(s32[3]{0:T(128)} %refs_2_.7) | copy-start | bytes 40
  30.9 15.5 %copy-start.5 = (f32[3]{0:T(128)S(1)}, f32[3]{0:T(128)}, u32[]{:S(2)}) copy-start(f32[3]{0:T(128)} %refs_3_.7) | copy-start | bytes 40
  50.8 22.1 %collective-permute-start.9 = (bf16[2,512,512]{2,1,0:T(8,128)(2,1)}, bf16[2,512,512]{2,1,0:T(8,128)(2,1)S(1)}, u32[]{:S(2)}, u32[]{:S(2)}) collective-permute-start(bf16[2,512,512]{2,1,0:T(8,128)(2,1)} %after.8.refs_15_), channel_id=1, source_target_pairs={{1,2},{3,4},{5,6},{2,1},{4,3},{6,5},{9,10},{11,12},{13,14},{10,9},... | collective-permute-start | bytes 3145736 | tf_op jit(solution)/shard_map/ppermute | solution.py:393
  54.9 24.5 %collective-permute-start.10 = (bf16[4,512,256]{2,1,0:T(8,128)(2,1)S(1)}, bf16[4,512,256]{2,1,0:T(8,128)(2,1)S(1)}, u32[]{:S(2)}, u32[]{:S(2)}) collective-permute-start(bf16[4,512,256]{2,1,0:T(8,128)(2,1)S(1)} %message0.1.refs_2_.refs_1_), channel_id=1, source_target_pairs={{0,8},{8,16},{16,24},{24,0},{1,9},{9,17},{17,25},{25,1},{2,10},{10... | collective-permute-start | bytes 3145736 | tf_op jit(solution)/shard_map/ppermute | solution.py:391
  59.9 19.5 %collective-permute-start.7 = (bf16[2,512,512]{2,1,0:T(8,128)(2,1)}, bf16[2,512,512]{2,1,0:T(8,128)(2,1)S(1)}, u32[]{:S(2)}, u32[]{:S(2)}) collective-permute-start(bf16[2,512,512]{2,1,0:T(8,128)(2,1)} %after.7.refs_14_), channel_id=1, source_target_pairs={{0,1},{2,3},{4,5},{6,7},{1,0},{3,2},{5,4},{7,6},{8,9},{10,11},{12,... | collective-permute-start | bytes 3145736 | tf_op jit(solution)/shard_map/ppermute | solution.py:399
  59.9 30.6 %collective-permute-start.8 = (bf16[2,512,512]{2,1,0:T(8,128)(2,1)}, bf16[2,512,512]{2,1,0:T(8,128)(2,1)S(1)}, u32[]{:S(2)}, u32[]{:S(2)}) collective-permute-start(bf16[2,512,512]{2,1,0:T(8,128)(2,1)} %after.7.refs_14_), channel_id=1, source_target_pairs={{1,2},{3,4},{5,6},{2,1},{4,3},{6,5},{9,10},{11,12},{13,14},{10,9},... | collective-permute-start | bytes 3145736 | tf_op jit(solution)/shard_map/ppermute | solution.py:398
  62.2 29.1 %collective-permute-start.12 = (bf16[4,256,256]{2,1,0:T(8,128)(2,1)S(1)}, bf16[4,256,256]{2,1,0:T(8,128)(2,1)S(1)}, u32[]{:S(2)}, u32[]{:S(2)}) collective-permute-start(bf16[4,256,256]{2,1,0:T(8,128)(2,1)S(1)} %get-tuple-element.13.refs_1_), channel_id=1, source_target_pairs={{0,8},{8,16},{16,24},{24,0},{1,9},{9,17},{17,25},{25,1},{2,10},{10... | collective-permute-start | bytes 1572872 | tf_op jit(solution)/shard_map/ppermute | solution.py:395
  72.9 22.9 %collective-permute-start.11 = (bf16[4,256,256]{2,1,0:T(8,128)(2,1)S(1)}, bf16[4,256,256]{2,1,0:T(8,128)(2,1)S(1)}, u32[]{:S(2)}, u32[]{:S(2)}) collective-permute-start(bf16[4,256,256]{2,1,0:T(8,128)(2,1)S(1)} %get-tuple-element.14), channel_id=1, source_target_pairs={{0,8},{8,16},{16,24},{24,0},{1,9},{9,17},{17,25},{25,1},{2,10},{10... | collective-permute-start | bytes 1572872 | tf_op jit(solution)/shard_map/ppermute | solution.py:396

commit v9 on v8

--- a/solution.py
+++ b/solution.py
@@ -299,8 +299,9 @@
     block = width // 2
     energy = odd() * place + (1 - odd()) * (1 - place)
     copies = []
-    for piece in range(count // block):
-        here, rows = pl.ds(piece * block, block), pl.ds(start + piece * block, block)
+    step = count // sems.shape[0]
+    for piece in range(sems.shape[0]):
+        here, rows = pl.ds(piece * step, step), pl.ds(start + piece * step, step)
         for column in range(listed):
             columns = pl.ds(column * block, block)
             for part in range(2):
@@ -321,7 +322,7 @@
         out_shape=result,
         scratch_shapes=[
             pltpu.VMEM(result.shape[2:], jnp.float32),
-            pltpu.SemaphoreType.DMA((2 * arrived.shape[1] // arrived.shape[2],)),
+            pltpu.SemaphoreType.DMA((4,)),
         ],
         input_output_aliases={2: 0} if earlier else {},
         compiler_params=SMALL,

time: 98.6 us -> 98.6 us (level)
    ppermute x1, waiting for transfers between devices: 5.04 us -> 1.06 us  [on_device(): near3 = lax.ppermute(near0, 'en', between)]
    ppermute x1, waiting for transfers between devices: 9.35 us -> 11.7 us  [on_device(): near2 = lax.ppermute(near1, 'en', between)]
    ppermute x1, waiting for transfers between devices: 15.5 us -> 16.6 us  [on_device(): relayed2 = lax.ppermute(own2, 'en', arriving)]
  transfers between devices with their start and end apart: 13 -> 13, of which waited for: 6 -> 6; matrix products, arithmetic and copies ran while one was open for 0% -> 0% of each run, Pallas kernels for 19% -> 20%
where the time goes in v9:
time: 98.6 us; the launch traced here: 96.8 us
  waiting for transfers between devices  50.1 us (51%)
  starting transfers between devices  23.5 us (24%)
  Pallas kernels  21.6 us (22%)
  local copies, waits for them, and re-layouts  1.36 us (1%)
    ppermute x1, waiting for transfers between devices, on_device(): relayed2 = lax.ppermute(own2, 'en', arriving)  16.6 us
    pallas_call x4, Pallas kernels, call(): pl.pallas_call(kernel, in_specs=[SMEM] * 4 + [VMEM] * 2 + [ANY] * len(ope...  14.8 us
    ppermute x1, waiting for transfers between devices, on_device(): near2 = lax.ppermute(near1, 'en', between)  11.7 us
    ppermute x1, waiting for transfers between devices, on_device(): near1 = lax.ppermute(own1, 'kz', backward)  10.7 us
    ppermute x1, waiting for transfers between devices, on_device(): arrived0 = lax.ppermute(sent0, 'kz', forward)  6.56 us
    ppermute x1, starting transfers between devices, on_device(): own2 = lax.ppermute(own1, 'en', across)  4.21 us
    ppermute x1, starting transfers between devices, on_device(): near2 = lax.ppermute(near1, 'en', between)  4.08 us
    pallas_call x3, Pallas kernels, store(): pl.pallas_call(functools.partial(store_kernel, place, half * arrived.shap...  3.47 us
  transfers between devices with their start and end apart: 13, of which 6 were waited for; matrix products, arithmetic and copies ran while one was open for 0% of the time, Pallas kernels for 20%

profile of v9, /device:TPU:3, one launch (start us, length us, event | category | flops | bytes accessed | tf_op | source)
XLA Modules:
  0.0 96.8 jit_solution(2999558297147696954)
XLA Ops:
  0.0 0.0 copy-start.2
  0.0 1.4 %take.1._.refs_8_ = bf16[2,512,512]{2,1,0:T(8,128)(2,1)S(1)} custom-call(bf16[1,2,2,512,512]{4,3,2,1,0:T(8,128)(2,1)} %green_ref.3), custom_call_target="tpu_custom_call" | custom-call | flops 1 | bytes 1 | tf_op jit(solution)/shard_map/take/pallas_call | solution.py:93
  1.4 0.0 copy-start.6
  1.4 3.4 %collective-permute-start.2 = (bf16[2,512,512]{2,1,0:T(8,128)(2,1)S(1)}, bf16[2,512,512]{2,1,0:T(8,128)(2,1)}, u32[]{:S(2)}, u32[]{:S(2)}) collective-permute-start(bf16[2,512,512]{2,1,0:T(8,128)(2,1)S(1)} %take.1._.refs_8_), channel_id=1, source_target_pairs={{0,24},{8,0},{16,8},{24,16},{1,25},{9,1},{17,9},{25,17},{2,26},{10... | collective-permute-start | bytes 3145736 | tf_op jit(solution)/shard_map/ppermute | solution.py:379
  4.7 4.2 %collective-permute-start.3 = (bf16[2,512,512]{2,1,0:T(8,128)(2,1)S(1)}, bf16[2,512,512]{2,1,0:T(8,128)(2,1)}, u32[]{:S(2)}, u32[]{:S(2)}) collective-permute-start(bf16[2,512,512]{2,1,0:T(8,128)(2,1)S(1)} %take.1._.refs_8_), channel_id=1, source_target_pairs={{1,2},{5,6},{2,1},{6,5},{3,7},{4,0},{9,10},{13,14},{10,9},{14,13},... | collective-permute-start | bytes 3145736 | tf_op jit(solution)/shard_map/ppermute | solution.py:380
  9.0 0.0 collective-permute-start.1
  9.0 0.0 copy-done.2
  9.0 2.1 %prepare.1 = (bf16[2,512,512]{2,1,0:T(8,128)(2,1)}, bf16[3,4,256,256]{3,2,1,0:T(8,128)(2,1)S(1)}, bf16[3,4,256,256]{3,2,1,0:T(8,128)(2,1)S(1)}) custom-call(bf16[1,2,2,512,512]{4,3,2,1,0:T(8,128)(2,1)} %green_ref.3, f32[3,4,2,128,128]{4,3,2,1,0:T(8,128)S(1)} %copy-done.2, bf16[2,512,512]{2,1,0:T(8,128)(2,1)S(1)} %take.1._.refs_8_), custom_call_target="tpu_custom_call" | custom-call | flops 1 | bytes 1 | tf_op jit(solution)/shard_map/prepare/pallas_call | solution.py:126
  11.0 0.0 copy-start
  11.0 1.1 %copy-done = bf16[3,4,256,256]{3,2,1,0:T(8,128)(2,1)} copy-done((bf16[3,4,256,256]{3,2,1,0:T(8,128)(2,1)}, bf16[3,4,256,256]{3,2,1,0:T(8,128)(2,1)S(1)}, u32[]{:S(2)}) %copy-start) | copy-done | bytes 1572888
  12.2 3.3 %collective-permute-start.4 = (bf16[2,512,512]{2,1,0:T(8,128)(2,1)}, bf16[2,512,512]{2,1,0:T(8,128)(2,1)}, u32[]{:S(2)}, u32[]{:S(2)}) collective-permute-start(bf16[2,512,512]{2,1,0:T(8,128)(2,1)} %get-tuple-element.12.refs_7_), channel_id=1, source_target_pairs={{1,2},{3,4},{5,6},{2,1},{4,3},{6,5},{9,10},{11,12},{13,14},{10,9},... | collective-permute-start | bytes 3145736 | tf_op jit(solution)/shard_map/ppermute | solution.py:383
  15.5 0.2 collective-permute-start
  15.7 0.0 copy-done.6
  15.7 0.1 copy.15
  15.8 0.1 reshape.3.refs_0_
  15.9 10.7 %collective-permute-done.2.refs_1_.refs_0_ = bf16[2,512,512]{2,1,0:T(8,128)(2,1)} collective-permute-done((bf16[2,512,512]{2,1,0:T(8,128)(2,1)S(1)}, bf16[2,512,512]{2,1,0:T(8,128)(2,1)}, u32[]{:S(2)}, u32[]{:S(2)}) %collective-permute-start.2) | collective-permute-done | bytes 1048608 | tf_op jit(solution)/shard_map/ppermute | solution.py:379
  26.6 0.0 collective-permute-done.3.refs_0_
  26.6 1.3 %collective-permute-start.5 = (bf16[2,512,512]{2,1,0:T(8,128)(2,1)}, bf16[2,512,512]{2,1,0:T(8,128)(2,1)}, u32[]{:S(2)}, u32[]{:S(2)}) collective-permute-start(bf16[2,512,512]{2,1,0:T(8,128)(2,1)} %after.6.refs_9_), channel_id=1, source_target_pairs={{7,4},{0,3},{15,12},{8,11},{23,20},{16,19},{31,28},{24,27}} | collective-permute-start | bytes 3145736 | tf_op jit(solution)/shard_map/ppermute | solution.py:389
  27.9 3.0 %collective-permute-start.6 = (bf16[2,512,512]{2,1,0:T(8,128)(2,1)}, bf16[2,512,512]{2,1,0:T(8,128)(2,1)}, u32[]{:S(2)}, u32[]{:S(2)}) collective-permute-start(bf16[2,512,512]{2,1,0:T(8,128)(2,1)} %collective-permute-done.2.refs_1_.refs_0_), channel_id=1, source_target_pairs={{0,1},{2,3},{4,5},{6,7},{1,0},{3,2},{5,4},{7,6},{8,9},{10,11},{12,... | collective-permute-start | bytes 3145736 | tf_op jit(solution)/shard_map/ppermute | solution.py:386
  30.9 0.0 collective-permute-done.1.refs_0_
  30.9 0.0 copy-start.5
  31.0 16.6 %collective-permute-done.5.refs_11_.refs_10_ = bf16[2,512,512]{2,1,0:T(8,128)(2,1)} collective-permute-done((bf16[2,512,512]{2,1,0:T(8,128)(2,1)}, bf16[2,512,512]{2,1,0:T(8,128)(2,1)}, u32[]{:S(2)}, u32[]{:S(2)}) %collective-permute-start.5) | collective-permute-done | bytes 1048608 | tf_op jit(solution)/shard_map/ppermute | solution.py:389
  47.6 0.0 copy-done.1
  47.6 0.0 copy-done.3
  47.6 0.0 copy-done.4
  47.6 0.0 copy-done.5
  47.6 3.1 %message0.1.refs_2_.refs_1_ = bf16[4,512,256]{2,1,0:T(8,128)(2,1)S(1)} custom-call(s32[24]{0:T(128)S(1)} %reshape.3.refs_0_, s32[3]{0:T(128)S(1)} %copy-done.3, s32[3]{0:T(128)S(1)} %copy-done.4, f32[3]{0:T(128)S(1)} %copy-done.5, bf16[3,4,256,256]{3,2,1,0:T(8,128)(2,1)S(1)} %get-tuple-element.10.refs_4_, bf16[3,4,256,256]{3,2,1,0:T(8,128)(2,1)S(1)} %copy-done.1, ...), custom_call_target="tpu_custom_call" | custom-call | flops 1 | bytes 1 | tf_op jit(solution)/shard_map/message0/pallas_call | solution.py:352
  50.8 0.0 collective-permute-done.6.refs_3_.refs_2_.refs_12_
  50.8 4.1 %collective-permute-start.9 = (bf16[2,512,512]{2,1,0:T(8,128)(2,1)}, bf16[2,512,512]{2,1,0:T(8,128)(2,1)S(1)}, u32[]{:S(2)}, u32[]{:S(2)}) collective-permute-start(bf16[2,512,512]{2,1,0:T(8,128)(2,1)} %after.8.refs_15_), channel_id=1, source_target_pairs={{1,2},{3,4},{5,6},{2,1},{4,3},{6,5},{9,10},{11,12},{13,14},{10,9},... | collective-permute-start | bytes 3145736 | tf_op jit(solution)/shard_map/ppermute | solution.py:394
  54.9 0.3 collective-permute-start.10
  55.2 0.0 collective-permute-done.4.refs_10_
  55.2 3.4 %message1.1 = (bf16[4,256,256]{2,1,0:T(8,128)(2,1)S(1)}, bf16[4,256,256]{2,1,0:T(8,128)(2,1)S(1)}) custom-call(s32[24]{0:T(128)S(1)} %reshape.3.refs_0_, s32[3]{0:T(128)S(1)} %copy-done.3, s32[3]{0:T(128)S(1)} %copy-done.4, f32[3]{0:T(128)S(1)} %copy-done.5, bf16[3,4,256,256]{3,2,1,0:T(8,128)(2,1)S(1)} %get-tuple-element.10.refs_4_, ...), custom_call_target="tpu_custom_call" | custom-call | flops 1 | bytes 1 | tf_op jit(solution)/shard_map/message1/pallas_call | solution.py:352
  58.7 0.0 collective-permute-done.refs_0_
  58.7 0.1 collective-permute-start.7
  58.8 2.2 %collective-permute-start.8 = (bf16[2,512,512]{2,1,0:T(8,128)(2,1)}, bf16[2,512,512]{2,1,0:T(8,128)(2,1)S(1)}, u32[]{:S(2)}, u32[]{:S(2)}) collective-permute-start(bf16[2,512,512]{2,1,0:T(8,128)(2,1)} %after.7.refs_14_), channel_id=1, source_target_pairs={{1,2},{3,4},{5,6},{2,1},{4,3},{6,5},{9,10},{11,12},{13,14},{10,9},... | collective-permute-start | bytes 3145736 | tf_op jit(solution)/shard_map/ppermute | solution.py:399
  61.0 1.3 %collective-permute-start.12 = (bf16[4,256,256]{2,1,0:T(8,128)(2,1)S(1)}, bf16[4,256,256]{2,1,0:T(8,128)(2,1)S(1)}, u32[]{:S(2)}, u32[]{:S(2)}) collective-permute-start(bf16[4,256,256]{2,1,0:T(8,128)(2,1)S(1)} %get-tuple-element.13.refs_1_), channel_id=1, source_target_pairs={{0,8},{8,16},{16,24},{24,0},{1,9},{9,17},{17,25},{25,1},{2,10},{10... | collective-permute-start | bytes 1572872 | tf_op jit(solution)/shard_map/ppermute | solution.py:396
  62.3 11.7 %collective-permute-done.9.refs_0_ = bf16[2,512,512]{2,1,0:T(8,128)(2,1)S(1)} collective-permute-done((bf16[2,512,512]{2,1,0:T(8,128)(2,1)}, bf16[2,512,512]{2,1,0:T(8,128)(2,1)S(1)}, u32[]{:S(2)}, u32[]{:S(2)}) %collective-permute-start.9) | collective-permute-done | bytes 1048608 | tf_op jit(solution)/shard_map/ppermute | solution.py:394
  74.0 0.0 collective-permute-start.11
  74.0 6.6 %collective-permute-done.10.refs_1_.arrived = bf16[4,512,256]{2,1,0:T(8,128)(2,1)S(1)} collective-permute-done((bf16[4,512,256]{2,1,0:T(8,128)(2,1)S(1)}, bf16[4,512,256]{2,1,0:T(8,128)(2,1)S(1)}, u32[]{:S(2)}, u32[]{:S(2)}) %collective-permute-start.10) | collective-permute-done | bytes 1048608 | tf_op jit(solution)/shard_map/ppermute | solution.py:392
  80.6 0.0 collective-permute-done.7.refs_13_.refs_6_
  80.6 7.4 %first.1.refs_8_.sum_ref = f32[2,2,512,512]{3,2,1,0:T(8,128)S(1)} custom-call(s32[24]{0:T(128)S(1)} %reshape.3.refs_0_, s32[3]{0:T(128)S(1)} %copy-done.3, s32[3]{0:T(128)S(1)} %copy-done.4, f32[3]{0:T(128)S(1)} %copy-done.5, bf16[3,4,256,256]{3,2,1,0:T(8,128)(2,1)S(1)} %get-tuple-element.10.refs_4_, bf16[3,4,256,256]{3,2,1,0:T(8,128)(2,1)S(1)} %copy-done.1, ...), custom_call_target="tpu_custom_call" | custom-call | flops 1 | bytes 1 | tf_op jit(solution)/shard_map/first/pallas_call | solution.py:352
  88.0 1.4 %store00.1.refs_0_ = f32[1,2,2,512,512]{4,3,2,1,0:T(8,128)} custom-call(f32[2,2,512,512]{3,2,1,0:T(8,128)S(1)} %first.1.refs_8_.sum_ref, bf16[4,512,256]{2,1,0:T(8,128)(2,1)S(1)} %collective-permute-done.10.refs_1_.arrived), custom_call_target="tpu_custom_call" | custom-call | flops 1 | bytes 1 | tf_op jit(solution)/shard_map/store00/pallas_call | solution.py:318
  89.4 1.1 %collective-permute-done.8.refs_7_ = bf16[2,512,512]{2,1,0:T(8,128)(2,1)S(1)} collective-permute-done((bf16[2,512,512]{2,1,0:T(8,128)(2,1)}, bf16[2,512,512]{2,1,0:T(8,128)(2,1)S(1)}, u32[]{:S(2)}, u32[]{:S(2)}) %collective-permute-start.8) | collective-permute-done | bytes 1048608 | tf_op jit(solution)/shard_map/ppermute | solution.py:399
  90.5 0.8 second.1.sum_ref
  91.3 0.0 collective-permute-done.12.arrived
  91.3 1.0 %store10.1.refs_0_ = f32[1,2,2,512,512]{4,3,2,1,0:T(8,128)} custom-call(f32[1,2,512,512]{3,2,1,0:T(8,128)S(1)} %second.1.sum_ref, bf16[4,256,256]{2,1,0:T(8,128)(2,1)S(1)} %collective-permute-done.12.arrived, f32[1,2,2,512,512]{4,3,2,1,0:T(8,128)} %store00.1.refs_0_), custom_call_target="tpu_custom_call", output_to_operand_aliasing={{}: (2, {})} | custom-call | flops 1 | bytes 1 | tf_op jit(solution)/shard_map/store10/pallas_call | solution.py:318
  92.3 3.4 %collective-permute-done.11.arrived = bf16[4,256,256]{2,1,0:T(8,128)(2,1)S(1)} collective-permute-done((bf16[4,256,256]{2,1,0:T(8,128)(2,1)S(1)}, bf16[4,256,256]{2,1,0:T(8,128)(2,1)S(1)}, u32[]{:S(2)}, u32[]{:S(2)}) %collective-permute-start.11) | collective-permute-done | bytes 524320 | tf_op jit(solution)/shard_map/ppermute | solution.py:397
  95.7 1.0 %store11.1 = f32[1,2,2,512,512]{4,3,2,1,0:T(8,128)} custom-call(f32[1,2,512,512]{3,2,1,0:T(8,128)S(1)} %second.1.sum_ref, bf16[4,256,256]{2,1,0:T(8,128)(2,1)S(1)} %collective-permute-done.11.arrived, f32[1,2,2,512,512]{4,3,2,1,0:T(8,128)} %store10.1.refs_0_), custom_call_target="tpu_custom_call", output_to_operand_aliasing={{}: (2, {})} | custom-call | flops 1 | bytes 1 | tf_op jit(solution)/shard_map/store11/pallas_call | solution.py:318
  (8 shorter events, 0.0 us)
Async XLA Ops:
  0.0 9.0 %copy-start.2 = (f32[3,4,2,128,128]{4,3,2,1,0:T(8,128)S(1)}, f32[3,4,2,128,128]{4,3,2,1,0:T(8,128)}, u32[]{:S(2)}) copy-start(f32[3,4,2,128,128]{4,3,2,1,0:T(8,128)} %coupling_ref.1) | copy-start | bytes 4718596
  1.4 14.4 %copy-start.6 = (s32[3,4,2]{1,2,0:T(2,128)S(1)}, s32[3,4,2]{1,2,0:T(2,128)}, u32[]{:S(2)}) copy-start(s32[3,4,2]{1,2,0:T(2,128)} %param.8) | copy-start | bytes 292
  1.4 25.2 %collective-permute-start.2 = (bf16[2,512,512]{2,1,0:T(8,128)(2,1)S(1)}, bf16[2,512,512]{2,1,0:T(8,128)(2,1)}, u32[]{:S(2)}, u32[]{:S(2)}) collective-permute-start(bf16[2,512,512]{2,1,0:T(8,128)(2,1)S(1)} %take.1._.refs_8_), channel_id=1, source_target_pairs={{0,24},{8,0},{16,8},{24,16},{1,25},{9,1},{17,9},{25,17},{2,26},{10... | collective-permute-start | bytes 3145736 | tf_op jit(solution)/shard_map/ppermute | solution.py:379
  4.7 21.8 %collective-permute-start.3 = (bf16[2,512,512]{2,1,0:T(8,128)(2,1)S(1)}, bf16[2,512,512]{2,1,0:T(8,128)(2,1)}, u32[]{:S(2)}, u32[]{:S(2)}) collective-permute-start(bf16[2,512,512]{2,1,0:T(8,128)(2,1)S(1)} %take.1._.refs_8_), channel_id=1, source_target_pairs={{1,2},{5,6},{2,1},{6,5},{3,7},{4,0},{9,10},{13,14},{10,9},{14,13},... | collective-permute-start | bytes 3145736 | tf_op jit(solution)/shard_map/ppermute | solution.py:380
  9.0 22.0 %collective-permute-start.1 = (bf16[1,2,2,512,512]{4,3,2,1,0:T(8,128)(2,1)}, bf16[1,2,2,512,512]{4,3,2,1,0:T(8,128)(2,1)}, u32[]{:S(2)}, u32[]{:S(2)}) collective-permute-start(bf16[1,2,2,512,512]{4,3,2,1,0:T(8,128)(2,1)} %green_ref.3), channel_id=1, source_target_pairs={{0,1},{2,3},{4,5},{6,7},{1,0},{3,2},{5,4},{7,6},{8,9},{10,11},{12,... | collective-permute-start | bytes 6291464 | tf_op jit(solution)/shard_map/ppermute | solution.py:384
  11.0 1.1 %copy-start = (bf16[3,4,256,256]{3,2,1,0:T(8,128)(2,1)}, bf16[3,4,256,256]{3,2,1,0:T(8,128)(2,1)S(1)}, u32[]{:S(2)}) copy-start(bf16[3,4,256,256]{3,2,1,0:T(8,128)(2,1)S(1)} %get-tuple-element.11.refs_5_) | copy-start | bytes 4718596
  12.2 43.0 %collective-permute-start.4 = (bf16[2,512,512]{2,1,0:T(8,128)(2,1)}, bf16[2,512,512]{2,1,0:T(8,128)(2,1)}, u32[]{:S(2)}, u32[]{:S(2)}) collective-permute-start(bf16[2,512,512]{2,1,0:T(8,128)(2,1)} %get-tuple-element.12.refs_7_), channel_id=1, source_target_pairs={{1,2},{3,4},{5,6},{2,1},{4,3},{6,5},{9,10},{11,12},{13,14},{10,9},... | collective-permute-start | bytes 3145736 | tf_op jit(solution)/shard_map/ppermute | solution.py:383
  15.5 43.2 %collective-permute-start = (bf16[2,512,512]{2,1,0:T(8,128)(2,1)}, bf16[2,512,512]{2,1,0:T(8,128)(2,1)}, u32[]{:S(2)}, u32[]{:S(2)}) collective-permute-start(bf16[2,512,512]{2,1,0:T(8,128)(2,1)} %get-tuple-element.12.refs_7_), channel_id=1, source_target_pairs={{0,24},{8,0},{16,8},{24,16},{1,25},{9,1},{17,9},{25,17},{2,26},{10... | collective-permute-start | bytes 3145736 | tf_op jit(solution)/shard_map/ppermute | solution.py:382
  26.6 21.0 %collective-permute-start.5 = (bf16[2,512,512]{2,1,0:T(8,128)(2,1)}, bf16[2,512,512]{2,1,0:T(8,128)(2,1)}, u32[]{:S(2)}, u32[]{:S(2)}) collective-permute-start(bf16[2,512,512]{2,1,0:T(8,128)(2,1)} %after.6.refs_9_), channel_id=1, source_target_pairs={{7,4},{0,3},{15,12},{8,11},{23,20},{16,19},{31,28},{24,27}} | collective-permute-start | bytes 3145736 | tf_op jit(solution)/shard_map/ppermute | solution.py:389
  27.9 22.9 %collective-permute-start.6 = (bf16[2,512,512]{2,1,0:T(8,128)(2,1)}, bf16[2,512,512]{2,1,0:T(8,128)(2,1)}, u32[]{:S(2)}, u32[]{:S(2)}) collective-permute-start(bf16[2,512,512]{2,1,0:T(8,128)(2,1)} %collective-permute-done.2.refs_1_.refs_0_), channel_id=1, source_target_pairs={{0,1},{2,3},{4,5},{6,7},{1,0},{3,2},{5,4},{7,6},{8,9},{10,11},{12,... | collective-permute-start | bytes 3145736 | tf_op jit(solution)/shard_map/ppermute | solution.py:386
  30.9 16.7 %copy-start.1 = (bf16[3,4,256,256]{3,2,1,0:T(8,128)(2,1)S(1)}, bf16[3,4,256,256]{3,2,1,0:T(8,128)(2,1)}, u32[]{:S(2)}) copy-start(bf16[3,4,256,256]{3,2,1,0:T(8,128)(2,1)} %copy-done) | copy-start | bytes 4718596
  30.9 16.7 %copy-start.3 = (s32[3]{0:T(128)S(1)}, s32[3]{0:T(128)}, u32[]{:S(2)}) copy-start(s32[3]{0:T(128)} %refs_1_.7) | copy-start | bytes 40
  30.9 16.7 %copy-start.4 = (s32[3]{0:T(128)S(1)}, s32[3]{0:T(128)}, u32[]{:S(2)}) copy-start(s32[3]{0:T(128)} %refs_2_.7) | copy-start | bytes 40
  30.9 16.7 %copy-start.5 = (f32[3]{0:T(128)S(1)}, f32[3]{0:T(128)}, u32[]{:S(2)}) copy-start(f32[3]{0:T(128)} %refs_3_.7) | copy-start | bytes 40
  50.8 23.2 %collective-permute-start.9 = (bf16[2,512,512]{2,1,0:T(8,128)(2,1)}, bf16[2,512,512]{2,1,0:T(8,128)(2,1)S(1)}, u32[]{:S(2)}, u32[]{:S(2)}) collective-permute-start(bf16[2,512,512]{2,1,0:T(8,128)(2,1)} %after.8.refs_15_), channel_id=1, source_target_pairs={{1,2},{3,4},{5,6},{2,1},{4,3},{6,5},{9,10},{11,12},{13,14},{10,9},... | collective-permute-start | bytes 3145736 | tf_op jit(solution)/shard_map/ppermute | solution.py:394
  54.9 25.7 %collective-permute-start.10 = (bf16[4,512,256]{2,1,0:T(8,128)(2,1)S(1)}, bf16[4,512,256]{2,1,0:T(8,128)(2,1)S(1)}, u32[]{:S(2)}, u32[]{:S(2)}) collective-permute-start(bf16[4,512,256]{2,1,0:T(8,128)(2,1)S(1)} %message0.1.refs_2_.refs_1_), channel_id=1, source_target_pairs={{0,8},{8,16},{16,24},{24,0},{1,9},{9,17},{17,25},{25,1},{2,10},{10... | collective-permute-start | bytes 3145736 | tf_op jit(solution)/shard_map/ppermute | solution.py:392
  58.7 21.9 %collective-permute-start.7 = (bf16[2,512,512]{2,1,0:T(8,128)(2,1)}, bf16[2,512,512]{2,1,0:T(8,128)(2,1)S(1)}, u32[]{:S(2)}, u32[]{:S(2)}) collective-permute-start(bf16[2,512,512]{2,1,0:T(8,128)(2,1)} %after.7.refs_14_), channel_id=1, source_target_pairs={{0,1},{2,3},{4,5},{6,7},{1,0},{3,2},{5,4},{7,6},{8,9},{10,11},{12,... | collective-permute-start | bytes 3145736 | tf_op jit(solution)/shard_map/ppermute | solution.py:400
  58.8 31.7 %collective-permute-start.8 = (bf16[2,512,512]{2,1,0:T(8,128)(2,1)}, bf16[2,512,512]{2,1,0:T(8,128)(2,1)S(1)}, u32[]{:S(2)}, u32[]{:S(2)}) collective-permute-start(bf16[2,512,512]{2,1,0:T(8,128)(2,1)} %after.7.refs_14_), channel_id=1, source_target_pairs={{1,2},{3,4},{5,6},{2,1},{4,3},{6,5},{9,10},{11,12},{13,14},{10,9},... | collective-permute-start | bytes 3145736 | tf_op jit(solution)/shard_map/ppermute | solution.py:399
  61.0 30.3 %collective-permute-start.12 = (bf16[4,256,256]{2,1,0:T(8,128)(2,1)S(1)}, bf16[4,256,256]{2,1,0:T(8,128)(2,1)S(1)}, u32[]{:S(2)}, u32[]{:S(2)}) collective-permute-start(bf16[4,256,256]{2,1,0:T(8,128)(2,1)S(1)} %get-tuple-element.13.refs_1_), channel_id=1, source_target_pairs={{0,8},{8,16},{16,24},{24,0},{1,9},{9,17},{17,25},{25,1},{2,10},{10... | collective-permute-start | bytes 1572872 | tf_op jit(solution)/shard_map/ppermute | solution.py:396
  74.0 21.7 %collective-permute-start.11 = (bf16[4,256,256]{2,1,0:T(8,128)(2,1)S(1)}, bf16[4,256,256]{2,1,0:T(8,128)(2,1)S(1)}, u32[]{:S(2)}, u32[]{:S(2)}) collective-permute-start(bf16[4,256,256]{2,1,0:T(8,128)(2,1)S(1)} %get-tuple-element.14), channel_id=1, source_target_pairs={{0,8},{8,16},{16,24},{24,0},{1,9},{9,17},{17,25},{25,1},{2,10},{10... | collective-permute-start | bytes 1572872 | tf_op jit(solution)/shard_map/ppermute | solution.py:397
